TPU v7x, 32 devices: a whole 2x2x4 slice. The times are simulated.
32 devices in a mesh: dp: 4 (over y, x), vocab: 8 (over z, core).
Axes of the slice: x: 2, y: 2, z: 4, core: 2. Of those that a mesh axis runs over, the one named last changes fastest.
Arguments:
- x_clean: int32 [32, 256], P(('dp', 'vocab')), may hold values from 0 to 50256
- mask_index: int32 [32, 96], P(('dp', 'vocab')), may hold values from 0 to 256, as said below
- segment_ids: int32 [32, 256], P(('dp', 'vocab')), may hold values from 0 to 15, never falling along the last dimension, each value on 1 to 128 neighbouring positions
- noise_level: float32 [32], P('dp'), may hold values from 0.01 to 1
- embedding: float32 [50304, 768], P('vocab', 'dp'), may hold values from -6 to 6
- head_table: float32 [768, 50304], P('dp', 'vocab'), may hold values from -1 to 1
- w_time: float32 [256, 128], P(('dp', 'vocab')), may hold values from -0.375 to 0.375
- w_ada: float32 [128, 6144], P(None, ('dp', 'vocab')), may hold values from -0.5 to 0.5
- norm_gains: float32 [3, 768], P(None, ('dp', 'vocab')), may hold values from 0.3 to 2.5
- w_qkv: float32 [768, 2304], P(('dp', 'vocab')), may hold values from -0.21875 to 0.21875
- w_out: float32 [768, 768], P(('dp', 'vocab')), may hold values from -0.875 to 0.875
- w_up: float32 [768, 3072], P(('dp', 'vocab')), may hold values from -0.21875 to 0.21875
- w_down: float32 [3072, 768], P(('dp', 'vocab')), may hold values from -0.109375 to 0.109375
- moment_embedding: float32 [50304, 768], P('vocab', 'dp'), may hold values from -0.00061035156 to 0.00061035156
- moment_head_table: float32 [768, 50304], P('dp', 'vocab'), may hold values from -0.00061035156 to 0.00061035156
- moment_w_time: float32 [256, 128], P(('dp', 'vocab')), may hold values from -0.00061035156 to 0.00061035156
- moment_w_ada: float32 [128, 6144], P(None, ('dp', 'vocab')), may hold values from -0.00061035156 to 0.00061035156
- moment_norm_gains: float32 [3, 768], P(None, ('dp', 'vocab')), may hold values from -0.00061035156 to 0.00061035156
- moment_w_qkv: float32 [768, 2304], P(('dp', 'vocab')), may hold values from -0.00061035156 to 0.00061035156
- moment_w_out: float32 [768, 768], P(('dp', 'vocab')), may hold values from -0.00061035156 to 0.00061035156
- moment_w_up: float32 [768, 3072], P(('dp', 'vocab')), may hold values from -0.00061035156 to 0.00061035156
- moment_w_down: float32 [3072, 768], P(('dp', 'vocab')), may hold values from -0.00061035156 to 0.00061035156
- average_embedding: float32 [50304, 768], P('vocab', 'dp'), may hold values from -6 to 6
- average_head_table: float32 [768, 50304], P('dp', 'vocab'), may hold values from -0.21875 to 0.21875
- average_w_time: float32 [256, 128], P(('dp', 'vocab')), may hold values from -0.375 to 0.375
- average_w_ada: float32 [128, 6144], P(None, ('dp', 'vocab')), may hold values from -0.5 to 0.5
- average_norm_gains: float32 [3, 768], P(None, ('dp', 'vocab')), may hold values from 0.5 to 1.5
- average_w_qkv: float32 [768, 2304], P(('dp', 'vocab')), may hold values from -0.21875 to 0.21875
- average_w_out: float32 [768, 768], P(('dp', 'vocab')), may hold values from -0.875 to 0.875
- average_w_up: float32 [768, 3072], P(('dp', 'vocab')), may hold values from -0.21875 to 0.21875
- average_w_down: float32 [3072, 768], P(('dp', 'vocab')), may hold values from -0.109375 to 0.109375
Outputs:
- new_embedding: float32 [50304, 768], P('vocab', 'dp')
- new_head_table: float32 [768, 50304], P('dp', 'vocab')
- new_w_time: float32 [256, 128], P(('dp', 'vocab'))
- new_w_ada: float32 [128, 6144], P(None, ('dp', 'vocab'))
- new_norm_gains: float32 [3, 768], P(None, ('dp', 'vocab'))
- new_w_qkv: float32 [768, 2304], P(('dp', 'vocab'))
- new_w_out: float32 [768, 768], P(('dp', 'vocab'))
- new_w_up: float32 [768, 3072], P(('dp', 'vocab'))
- new_w_down: float32 [3072, 768], P(('dp', 'vocab'))
- new_moment_embedding: float32 [50304, 768], P('vocab', 'dp')
- new_moment_head_table: float32 [768, 50304], P('dp', 'vocab')
- new_moment_w_time: float32 [256, 128], P(('dp', 'vocab'))
- new_moment_w_ada: float32 [128, 6144], P(None, ('dp', 'vocab'))
- new_moment_norm_gains: float32 [3, 768], P(None, ('dp', 'vocab'))
- new_moment_w_qkv: float32 [768, 2304], P(('dp', 'vocab'))
- new_moment_w_out: float32 [768, 768], P(('dp', 'vocab'))
- new_moment_w_up: float32 [768, 3072], P(('dp', 'vocab'))
- new_moment_w_down: float32 [3072, 768], P(('dp', 'vocab'))
- new_average_embedding: float32 [50304, 768], P('vocab', 'dp')
- new_average_head_table: float32 [768, 50304], P('dp', 'vocab')
- new_average_w_time: float32 [256, 128], P(('dp', 'vocab'))
- new_average_w_ada: float32 [128, 6144], P(None, ('dp', 'vocab'))
- new_average_norm_gains: float32 [3, 768], P(None, ('dp', 'vocab'))
- new_average_w_qkv: float32 [768, 2304], P(('dp', 'vocab'))
- new_average_w_out: float32 [768, 768], P(('dp', 'vocab'))
- new_average_w_up: float32 [768, 3072], P(('dp', 'vocab'))
- new_average_w_down: float32 [3072, 768], P(('dp', 'vocab'))
- loss_sum: float32 [], replicated
- masked_count: float32 [], replicated
- grad_norm: float32 [], replicated
Inputs may be any that keep to these rules, and one draw needn't show every extreme that they name: `mask_index`: each sequence's list names, in rising order, 32 to 96 distinct positions of that sequence, followed by 256 in the other slots; some sequence lists exactly 96 positions and another exactly 32.
All inputs are finite; a program needn't handle non-finite values.
Results may differ from a plain program's by a relative error of at most 0.011.
The roundings to bfloat16 on the way count: a program that leaves them out, or rounds other values in their place, can miss the bound.
Values may be sent and summed in bfloat16 or wider, within the bound.
No kernel may reach another device: no remote copies, remote signals or barrier semaphores. Data moves between devices by JAX's collectives and lax.ppermute only.
A program may use at most 320 MiB of HBM per device.

v0:
```python
import jax
import jax.numpy as jnp
from jax import lax
from jax.sharding import PartitionSpec as P

HEAD_DIM = 64
VOCAB = 50258
FREQ = 256


norm_epsilon = 1e-06
weight_cap = 20.0
clip_level = 1.0
learn_rate = 30.0
embed_rate = 2000.0
momentum_rate = 0.9
average_rate = 0.5
highest = lax.Precision.HIGHEST


def combined_all(value, axis, join):
    pieces = jax.tree.map(lambda part: lax.all_gather(part, axis), value)
    head = jax.tree.map(lambda part: part[0], pieces)
    tail = jax.tree.map(lambda part: part[1:], pieces)
    subtotal, _ = lax.scan(lambda subtotal, share: (join(subtotal, share), None), head, tail)
    return subtotal


def features(level, freq_count):
    sigma_level = -jnp.log1p(-(1.0 - 0.001) * level)
    half_count = freq_count // 2
    frequency = jnp.exp(-jnp.log(10000.0) * jnp.arange(half_count, dtype=jnp.float32) / half_count)
    angles = sigma_level * frequency
    return jnp.concatenate([jnp.cos(angles), jnp.sin(angles)])


def nelbo_weight(level):
    sigma_level = -jnp.log1p(-(1.0 - 0.001) * level)
    rate_value = (1.0 - 0.001) / (1.0 - (1.0 - 0.001) * level)
    return jnp.minimum(rate_value / jnp.expm1(sigma_level), weight_cap)


def norm_mod(values, gain_row, shift_row, scale_row):
    center = values - jnp.mean(values, -1, keepdims=True)
    spread = jnp.mean(center * center, -1, keepdims=True)
    return center * lax.rsqrt(spread + norm_epsilon) * gain_row * (1.0 + scale_row) + shift_row


def condition(w_time, w_ada, spectrum):
    hidden_time = jax.nn.silu(jnp.dot(spectrum, w_time, precision=highest))
    return jnp.dot(hidden_time, w_ada, precision=highest).reshape(8, -1)


def times_rows(left_matrix, right_matrix):
    return lax.dot_general(
        left_matrix, right_matrix, (((0,), (0,)), ((), ())), preferred_element_type=jnp.float32
    )


def times_transposed(left_matrix, right_matrix):
    return lax.dot_general(
        left_matrix, right_matrix, (((1,), (1,)), ((), ())), preferred_element_type=jnp.float32
    )


def combine_stats(first, second):
    peak_value = jnp.maximum(first[0], second[0])
    summed = first[1] * jnp.exp(first[0] - peak_value) + second[1] * jnp.exp(second[0] - peak_value)
    return (peak_value, summed, first[2] + second[2])


def masked_ids(clean_rows, slot_rows, length):
    positions = jnp.arange(length)
    masked = jnp.any(slot_rows[:, :, None] == positions[None, None, :], axis=1)
    return jnp.where(masked, VOCAB - 1, clean_rows)


def attend(queries, keys_all, values_all, segment, block_rows):
    total_rows, head_count, head_width = queries.shape
    blocks = total_rows // block_rows
    factor = head_width ** (-0.5)

    def one_block(item):
        query_part, segment_part = item
        scores = (
            jnp.einsum("qhd,khd->hqk", query_part, keys_all, preferred_element_type=jnp.float32)
            * factor
        )
        scores = jnp.where((segment_part[:, None] == segment[None, :])[None], scores, -1e30)
        peak_value = jnp.max(scores, -1, keepdims=True)
        expo = jnp.exp(scores - peak_value)
        summed = jnp.sum(expo, -1, keepdims=True)
        probs = (expo / summed).astype(jnp.bfloat16)
        result = jnp.einsum("hqk,khd->qhd", probs, values_all, preferred_element_type=jnp.float32)
        return (result, (peak_value + jnp.log(summed))[..., 0])

    results, log_total = lax.map(
        one_block,
        (
            queries.reshape(blocks, block_rows, head_count, head_width),
            segment.reshape(blocks, block_rows),
        ),
    )
    return (results.reshape(total_rows, head_count * head_width), log_total)


def attend_back(queries, keys_all, values_all, segment, log_total, grad_attended, block_rows):
    total_rows, head_count, head_width = queries.shape
    blocks = total_rows // block_rows
    factor = head_width ** (-0.5)

    def one_block(item):
        query_part, segment_part, total_part, grad_part = item
        scores = (
            jnp.einsum("qhd,khd->hqk", query_part, keys_all, preferred_element_type=jnp.float32)
            * factor
        )
        scores = jnp.where((segment_part[:, None] == segment[None, :])[None], scores, -1e30)
        probs = jnp.exp(scores - total_part[..., None])
        grad_values = jnp.einsum(
            "hqk,qhd->khd",
            probs.astype(jnp.bfloat16),
            grad_part,
            preferred_element_type=jnp.float32,
        )
        grad_probs = jnp.einsum(
            "qhd,khd->hqk", grad_part, values_all, preferred_element_type=jnp.float32
        )
        grad_scores = (
            probs * (grad_probs - jnp.sum(probs * grad_probs, -1, keepdims=True))
        ).astype(jnp.bfloat16)
        grad_query = (
            jnp.einsum("hqk,khd->qhd", grad_scores, keys_all, preferred_element_type=jnp.float32)
            * factor
        )
        grad_keys = (
            jnp.einsum("hqk,qhd->khd", grad_scores, query_part, preferred_element_type=jnp.float32)
            * factor
        )
        return (grad_query, grad_keys, grad_values)

    grad_query, grad_keys, grad_values = lax.map(
        one_block,
        (
            queries.reshape(blocks, block_rows, head_count, head_width),
            segment.reshape(blocks, block_rows),
            log_total,
            grad_attended.reshape(blocks, block_rows, head_count, head_width),
        ),
    )
    return (
        grad_query.reshape(total_rows, head_count, head_width),
        jnp.sum(grad_keys, 0),
        jnp.sum(grad_values, 0),
    )


def layer_forward(weights, hidden_start, modulation, segment, block_rows):
    gains_full = weights[2].astype(jnp.float32)
    total_rows, model_width = hidden_start.shape
    head_count = model_width // HEAD_DIM
    normed_a = norm_mod(hidden_start, gains_full[0], modulation[0], modulation[1]).astype(
        jnp.bfloat16
    )
    triple = jnp.dot(normed_a, weights[3], preferred_element_type=jnp.float32).astype(jnp.bfloat16)
    triple = triple.reshape(total_rows, 3, head_count, HEAD_DIM)
    attended, log_total = attend(triple[:, 0], triple[:, 1], triple[:, 2], segment, block_rows)
    attended = attended.astype(jnp.bfloat16)
    branch_a = jnp.dot(attended, weights[4], preferred_element_type=jnp.float32)
    hidden_mid = hidden_start + modulation[2] * branch_a
    normed_b = norm_mod(hidden_mid, gains_full[1], modulation[3], modulation[4]).astype(
        jnp.bfloat16
    )
    up_values = jnp.dot(normed_b, weights[5], preferred_element_type=jnp.float32)
    active = jax.nn.gelu(up_values, approximate=True).astype(jnp.bfloat16)
    branch_m = jnp.dot(active, weights[6], preferred_element_type=jnp.float32)
    hidden_end = hidden_mid + modulation[5] * branch_m
    final_rows = norm_mod(hidden_end, gains_full[2], modulation[6], modulation[7])
    kept = (
        normed_a,
        triple,
        attended,
        log_total,
        branch_a,
        hidden_mid,
        normed_b,
        up_values,
        active,
        branch_m,
        hidden_end,
    )
    return (final_rows, kept)


def layer_backward(weights, hidden_start, modulation, segment, block_rows, kept, grad_final):
    (
        normed_a,
        triple,
        attended,
        log_total,
        branch_a,
        hidden_mid,
        normed_b,
        up_values,
        active,
        branch_m,
        hidden_end,
    ) = kept
    gains_full = weights[2].astype(jnp.float32)
    total_rows = hidden_start.shape[0]
    _, back_third = jax.vjp(norm_mod, hidden_end, gains_full[2], modulation[6], modulation[7])
    grad_end, grad_gain3, grad_shift3, grad_scale3 = back_third(grad_final)
    grad_gate2 = jnp.sum(grad_end * branch_m, 0)
    grad_branch_m = (modulation[5] * grad_end).astype(jnp.bfloat16)
    grad_down = times_rows(active, grad_branch_m)
    grad_active = times_transposed(grad_branch_m, weights[6])
    _, back_gelu = jax.vjp(lambda inputs: jax.nn.gelu(inputs, approximate=True), up_values)
    grad_upper = back_gelu(grad_active)[0].astype(jnp.bfloat16)
    grad_up = times_rows(normed_b, grad_upper)
    grad_normed_b = times_transposed(grad_upper, weights[5])
    _, back_second = jax.vjp(norm_mod, hidden_mid, gains_full[1], modulation[3], modulation[4])
    grad_mid_norm, grad_gain2, grad_shift2, grad_scale2 = back_second(grad_normed_b)
    grad_mid = grad_end + grad_mid_norm
    grad_gate1 = jnp.sum(grad_mid * branch_a, 0)
    grad_branch_a = (modulation[2] * grad_mid).astype(jnp.bfloat16)
    grad_out = times_rows(attended, grad_branch_a)
    grad_attended = times_transposed(grad_branch_a, weights[4]).astype(jnp.bfloat16)
    grad_attended = grad_attended.reshape(total_rows, triple.shape[2], HEAD_DIM)
    grad_query, grad_keys, grad_values = attend_back(
        triple[:, 0], triple[:, 1], triple[:, 2], segment, log_total, grad_attended, block_rows
    )
    grad_triple = (
        jnp.stack([grad_query, grad_keys, grad_values], 1)
        .reshape(total_rows, -1)
        .astype(jnp.bfloat16)
    )
    grad_qkv = times_rows(normed_a, grad_triple)
    grad_normed_a = times_transposed(grad_triple, weights[3])
    _, back_first = jax.vjp(norm_mod, hidden_start, gains_full[0], modulation[0], modulation[1])
    grad_start_norm, grad_gain1, grad_shift1, grad_scale1 = back_first(grad_normed_a)
    grad_start = grad_mid + grad_start_norm
    grad_mod = jnp.stack(
        [
            grad_shift1,
            grad_scale1,
            grad_gate1,
            grad_shift2,
            grad_scale2,
            grad_gate2,
            grad_shift3,
            grad_scale3,
        ]
    )
    grad_gains = jnp.stack([grad_gain1, grad_gain2, grad_gain3])
    return (grad_start, grad_mod, grad_gains, grad_qkv, grad_out, grad_up, grad_down)


def advance(weight_now, moment_now, average_now, gradient, clip_factor, rate_now):
    clipped = gradient * clip_factor
    moment_next = momentum_rate * moment_now + clipped
    weight_next = weight_now - rate_now * (clipped + momentum_rate * moment_next)
    return (
        weight_next,
        moment_next,
        average_rate * average_now + (1.0 - average_rate) * weight_next,
    )


def shards(
    x_clean,
    mask_index,
    segment_ids,
    noise_level,
    embedding,
    head_table,
    w_time,
    w_ada,
    norm_gains,
    w_qkv,
    w_out,
    w_up,
    w_down,
    moment_embedding,
    moment_head_table,
    moment_w_time,
    moment_w_ada,
    moment_norm_gains,
    moment_w_qkv,
    moment_w_out,
    moment_w_up,
    moment_w_down,
    average_embedding,
    average_head_table,
    average_w_time,
    average_w_ada,
    average_norm_gains,
    average_w_qkv,
    average_w_out,
    average_w_up,
    average_w_down,
):
    vocab_index = lax.axis_index("vocab")
    dp_index = lax.axis_index("dp")
    vocab_count = lax.axis_size("vocab")
    length = x_clean.shape[1]
    slot_count = mask_index.shape[1]
    block_rows = min(length, 512)
    clean_all, slots_all = (
        lax.all_gather(x_clean, ("dp", "vocab"), axis=0, tiled=True),
        lax.all_gather(mask_index, ("dp", "vocab"), axis=0, tiled=True),
    )
    masked_count = jnp.sum((slots_all < length).astype(jnp.float32))
    clean_group = lax.dynamic_slice_in_dim(clean_all, dp_index * vocab_count, vocab_count, 0)
    slots_group = lax.dynamic_slice_in_dim(slots_all, dp_index * vocab_count, vocab_count, 0)
    live_group = (slots_group < length).astype(jnp.float32)
    gathered = (
        lax.all_gather(w_time.astype(jnp.bfloat16), ("dp", "vocab"), axis=0, tiled=True),
        lax.all_gather(w_ada.astype(jnp.bfloat16), ("dp", "vocab"), axis=1, tiled=True),
        lax.all_gather(norm_gains.astype(jnp.bfloat16), ("dp", "vocab"), axis=1, tiled=True),
        lax.all_gather(w_qkv.astype(jnp.bfloat16), ("dp", "vocab"), axis=0, tiled=True),
        lax.all_gather(w_out.astype(jnp.bfloat16), ("dp", "vocab"), axis=0, tiled=True),
        lax.all_gather(w_up.astype(jnp.bfloat16), ("dp", "vocab"), axis=0, tiled=True),
        lax.all_gather(w_down.astype(jnp.bfloat16), ("dp", "vocab"), axis=0, tiled=True),
    )
    table_rows, head_columns = (
        lax.all_gather(embedding.astype(jnp.bfloat16), "dp", axis=1, tiled=True),
        lax.all_gather(head_table.astype(jnp.bfloat16), "dp", axis=0, tiled=True),
    )
    span = table_rows.shape[0]
    noisy_group = masked_ids(clean_group, slots_group, length)
    local_ids = noisy_group.reshape(-1) - vocab_index * span
    inside = (local_ids >= 0) & (local_ids < span)
    looked = jnp.take(table_rows, jnp.clip(local_ids, 0, span - 1), axis=0)
    looked = jnp.where(inside[:, None], looked, jnp.zeros((), jnp.bfloat16)).astype(jnp.float32)
    hidden_start = lax.psum_scatter(
        looked.astype(jnp.bfloat16), "vocab", scatter_dimension=0, tiled=True
    ).astype(jnp.float32)
    level = lax.dynamic_index_in_dim(noise_level, vocab_index, keepdims=False)
    spectrum = features(level, FREQ)
    time_weight = gathered[0].astype(jnp.float32)
    ada_weight = gathered[1].astype(jnp.float32)
    modulation = condition(time_weight, ada_weight, spectrum)
    segment = segment_ids[0]
    final_rows, kept = layer_forward(gathered, hidden_start, modulation, segment, block_rows)
    own_slots = mask_index[0]
    spots = jnp.minimum(own_slots, length - 1)
    own_live = (own_slots < length).astype(jnp.float32)
    group_rows = lax.all_gather(final_rows[spots].astype(jnp.bfloat16), "vocab", axis=0, tiled=True)
    columns = head_columns.shape[1]
    logits = jnp.dot(group_rows, head_columns, preferred_element_type=jnp.float32)
    column_ids = vocab_index * columns + jnp.arange(columns)
    logits = jnp.where((column_ids < VOCAB)[None, :], logits, -1e30)
    peak_value = jnp.max(logits, 1)
    expo_total = jnp.sum(jnp.exp(logits - peak_value[:, None]), 1)
    targets = jnp.take_along_axis(clean_group, jnp.minimum(slots_group, length - 1), 1).reshape(-1)
    target_local = targets - vocab_index * columns
    onehot = jnp.arange(columns)[None, :] == target_local[:, None]
    target_logit = jnp.sum(jnp.where(onehot, logits, 0.0), 1)
    peak_all, expo_all, target_all = combined_all(
        (peak_value, expo_total, target_logit), "vocab", combine_stats
    )
    log_total = peak_all + jnp.log(expo_all)
    row_weight = jnp.repeat(nelbo_weight(noise_level), slot_count) * live_group.reshape(-1)
    loss_group = jnp.sum(row_weight * (log_total - target_all))
    grad_logits = (row_weight / masked_count)[:, None] * (
        jnp.exp(logits - log_total[:, None]) - onehot.astype(jnp.float32)
    )
    grad_logits = grad_logits.astype(jnp.bfloat16)
    grad_head = times_rows(group_rows, grad_logits)
    grad_rows = times_transposed(grad_logits, head_columns)
    grad_mine = lax.psum_scatter(
        grad_rows.astype(jnp.bfloat16), "vocab", scatter_dimension=0, tiled=True
    ).astype(jnp.float32)
    grad_final = (
        jnp.zeros(final_rows.shape, jnp.float32).at[spots].add(grad_mine * own_live[:, None])
    )
    grad_start, grad_mod, grad_gains, grad_qkv, grad_out, grad_up, grad_down = layer_backward(
        gathered, hidden_start, modulation, segment, block_rows, kept, grad_final
    )
    _, cond_back = jax.vjp(condition, time_weight, ada_weight, spectrum)
    grad_time, grad_ada, _ = cond_back(grad_mod)
    start_low = grad_start.astype(jnp.bfloat16)
    returned = lax.all_gather(start_low, "vocab", axis=0, tiled=True)
    grad_table = jax.ops.segment_sum(
        returned.astype(jnp.float32), jnp.where(inside, local_ids, span), num_segments=span + 1
    )[:span]
    grad_embedding, grad_head_shard = (
        lax.psum_scatter(
            grad_table.astype(jnp.bfloat16), "dp", scatter_dimension=1, tiled=True
        ).astype(jnp.float32),
        lax.psum_scatter(
            grad_head.astype(jnp.bfloat16), "dp", scatter_dimension=0, tiled=True
        ).astype(jnp.float32),
    )
    shard_grads = (
        lax.psum_scatter(grad_time, ("dp", "vocab"), scatter_dimension=0, tiled=True),
        lax.psum_scatter(grad_ada, ("dp", "vocab"), scatter_dimension=1, tiled=True),
        lax.psum_scatter(grad_gains, ("dp", "vocab"), scatter_dimension=1, tiled=True),
        lax.psum_scatter(grad_qkv, ("dp", "vocab"), scatter_dimension=0, tiled=True),
        lax.psum_scatter(grad_out, ("dp", "vocab"), scatter_dimension=0, tiled=True),
        lax.psum_scatter(grad_up, ("dp", "vocab"), scatter_dimension=0, tiled=True),
        lax.psum_scatter(grad_down, ("dp", "vocab"), scatter_dimension=0, tiled=True),
    )
    grads_all = (grad_embedding, grad_head_shard) + tuple(shard_grads)
    squares = jnp.sum(jnp.stack([jnp.sum(gradient * gradient) for gradient in grads_all]))
    loss_term = jnp.where(vocab_index == 0, loss_group, 0.0)
    square_total, loss_sum = lax.psum((squares, loss_term), ("dp", "vocab"))
    grad_norm = jnp.sqrt(square_total)
    clip_factor = jnp.minimum(1.0, clip_level / (grad_norm + 1e-06))
    weights = (embedding, head_table, w_time, w_ada, norm_gains, w_qkv, w_out, w_up, w_down)
    moments = (
        moment_embedding,
        moment_head_table,
        moment_w_time,
        moment_w_ada,
        moment_norm_gains,
        moment_w_qkv,
        moment_w_out,
        moment_w_up,
        moment_w_down,
    )
    averages = (
        average_embedding,
        average_head_table,
        average_w_time,
        average_w_ada,
        average_norm_gains,
        average_w_qkv,
        average_w_out,
        average_w_up,
        average_w_down,
    )
    updated = [
        advance(
            weight_now,
            moment_now,
            average_now,
            gradient,
            clip_factor,
            embed_rate if weight_place == 0 else learn_rate,
        )
        for weight_place, (weight_now, moment_now, average_now, gradient) in enumerate(
            zip(weights, moments, averages, grads_all)
        )
    ]
    new_weights = tuple((result[0] for result in updated))
    new_moments = tuple((result[1] for result in updated))
    new_averages = tuple((result[2] for result in updated))
    return (*new_weights, *new_moments, *new_averages, loss_sum, masked_count, grad_norm)


def solution(mesh):
    placed = (
        P(("dp", "vocab"), None),
        P(("dp", "vocab"), None),
        P(("dp", "vocab"), None),
        P("dp"),
        P("vocab", "dp"),
        P("dp", "vocab"),
        P(("dp", "vocab"), None),
        P(None, ("dp", "vocab")),
        P(None, ("dp", "vocab")),
        P(("dp", "vocab"), None),
        P(("dp", "vocab"), None),
        P(("dp", "vocab"), None),
        P(("dp", "vocab"), None),
        P("vocab", "dp"),
        P("dp", "vocab"),
        P(("dp", "vocab"), None),
        P(None, ("dp", "vocab")),
        P(None, ("dp", "vocab")),
        P(("dp", "vocab"), None),
        P(("dp", "vocab"), None),
        P(("dp", "vocab"), None),
        P(("dp", "vocab"), None),
        P("vocab", "dp"),
        P("dp", "vocab"),
        P(("dp", "vocab"), None),
        P(None, ("dp", "vocab")),
        P(None, ("dp", "vocab")),
        P(("dp", "vocab"), None),
        P(("dp", "vocab"), None),
        P(("dp", "vocab"), None),
        P(("dp", "vocab"), None),
    )
    return jax.shard_map(
        shards,
        mesh=mesh,
        in_specs=placed,
        out_specs=(
            P("vocab", "dp"),
            P("dp", "vocab"),
            P(("dp", "vocab"), None),
            P(None, ("dp", "vocab")),
            P(None, ("dp", "vocab")),
            P(("dp", "vocab"), None),
            P(("dp", "vocab"), None),
            P(("dp", "vocab"), None),
            P(("dp", "vocab"), None),
            P("vocab", "dp"),
            P("dp", "vocab"),
            P(("dp", "vocab"), None),
            P(None, ("dp", "vocab")),
            P(None, ("dp", "vocab")),
            P(("dp", "vocab"), None),
            P(("dp", "vocab"), None),
            P(("dp", "vocab"), None),
            P(("dp", "vocab"), None),
            P("vocab", "dp"),
            P("dp", "vocab"),
            P(("dp", "vocab"), None),
            P(None, ("dp", "vocab")),
            P(None, ("dp", "vocab")),
            P(("dp", "vocab"), None),
            P(("dp", "vocab"), None),
            P(("dp", "vocab"), None),
            P(("dp", "vocab"), None),
            P(),
            P(),
            P(),
        ),
        check_vma=False,
    )
```

profile of v0, /device:TPU:0, one launch (start us, length us, event | category | flops | bytes accessed | tf_op | source)
XLA Modules:
  0.0 1875.8 jit_solution(1137196376444612607)
XLA Ops:
  12.2 43.1 %all-gather.3 = s32[32,1,96]{2,1,0:T(1,128)S(1)} all-gather(s32[1,1,96]{2,1,0:T(1,128)S(1)} %bitcast.164), channel_id=1, replica_groups=mesh['dp'=4,'vocab'=8] {'dp','vocab'}, dimensions={0}, use_global_device_ids=true | all-gather | bytes 12672 | tf_op jit(solution)/shard_map/all_gather | solution.py:310
  55.3 36.7 %all-gather.4 = s32[32,1,256]{2,1,0:T(1,128)S(1)} all-gather(s32[1,1,256]{2,1,0:T(1,128)S(1)} %bitcast.163), channel_id=1, replica_groups=mesh['dp'=4,'vocab'=8] {'dp','vocab'}, dimensions={0}, use_global_device_ids=true | all-gather | bytes 33792 | tf_op jit(solution)/shard_map/all_gather | solution.py:309
  93.5 20.6 %all-gather.19.cloned.1.call-done = bf16[6288,768]{0,1:T(8,128)(2,1)} async-done(((bf16[6288,192]{0,1:T(8,128)(2,1)}), bf16[6288,768]{0,1:T(8,128)(2,1)}) %all-gather.19.cloned.1.call-update) | async-done | bytes 9658384 | tf_op jit(solution)/shard_map/all_gather | solution.py:326
  114.1 13.7 copy.113
  127.8 13.4 gather_fusion
  152.7 41.0 %all-gather.5 = bf16[32,24,3]{1,2,0:T(4,128)(2,1)S(1)} all-gather(bf16[1,24,3]{1,2,0:T(4,128)(2,1)S(1)} %convert_bitcast_fusion), channel_id=1, replica_groups=mesh['dp'=4,'vocab'=8] {'dp','vocab'}, dimensions={0}, use_global_device_ids=true | all-gather | bytes 4752 | tf_op jit(solution)/shard_map/all_gather | solution.py:319
  194.0 37.7 %all_gather.60 = bf16[256,128]{1,0:T(8,128)(2,1)S(1)} all-gather(bf16[8,128]{1,0:T(8,128)(2,1)S(1)} %convert_element_type.135), channel_id=1, replica_groups=mesh['dp'=4,'vocab'=8] {'dp','vocab'}, dimensions={0}, use_global_device_ids=true | all-gather | bytes 67584 | tf_op jit(solution)/shard_map/all_gather | solution.py:317
  239.7 38.8 %all-gather.23.cloned.1.call-done = bf16[768,2304]{1,0:T(8,128)(2,1)} async-done(((bf16[24,2304]{1,0:T(8,128)(2,1)}), bf16[768,2304]{1,0:T(8,128)(2,1)}) %all-gather.23.cloned.1.call-update) | async-done | bytes 3538960 | tf_op jit(solution)/shard_map/all_gather | solution.py:320
  288.7 46.2 %all-gather.25.cloned.1.call-done = bf16[768,768]{1,0:T(8,128)(2,1)} async-done(((bf16[24,768]{1,0:T(8,128)(2,1)}), bf16[768,768]{1,0:T(8,128)(2,1)}) %all-gather.25.cloned.1.call-update) | async-done | bytes 1179664 | tf_op jit(solution)/shard_map/all_gather | solution.py:321
  339.8 61.1 %all-gather.27.cloned.1.call-done = bf16[768,3072]{1,0:T(8,128)(2,1)} async-done(((bf16[24,3072]{1,0:T(8,128)(2,1)}), bf16[768,3072]{1,0:T(8,128)(2,1)}) %all-gather.27.cloned.1.call-update) | async-done | bytes 4718608 | tf_op jit(solution)/shard_map/all_gather | solution.py:322
  406.7 60.3 %all-gather.29.cloned.1.call-done = bf16[3072,768]{1,0:T(8,128)(2,1)} async-done(((bf16[96,768]{1,0:T(8,128)(2,1)}), bf16[3072,768]{1,0:T(8,128)(2,1)}) %all-gather.29.cloned.1.call-update) | async-done | bytes 4718608 | tf_op jit(solution)/shard_map/all_gather | solution.py:323
  493.2 74.8 %all-gather.33.cloned.1.call-done = bf16[768,6288]{1,0:T(8,128)(2,1)} async-done(((bf16[192,6288]{1,0:T(8,128)(2,1)}), bf16[768,6288]{1,0:T(8,128)(2,1)}) %all-gather.33.cloned.1.call-update) | async-done | bytes 9658384 | tf_op jit(solution)/shard_map/all_gather | solution.py:327
  568.0 24.9 %all-gather.31.cloned.1.call-done = bf16[768,768]{1,0:T(8,128)(2,1)} async-done(((bf16[96,768]{1,0:T(8,128)(2,1)}), bf16[768,768]{1,0:T(8,128)(2,1)}) %all-gather.31.cloned.1.call-update) | async-done | bytes 1179664 | tf_op jit(solution)/shard_map/all_gather | solution.py:348
  592.9 15.8 select_reduce_fusion.1
  618.9 13.9 all-gather.8
  633.4 13.9 all-gather.7
  647.9 13.9 all-gather.6
  664.2 29.0 %while.2 = (s32[]{:T(128)}, f32[768]{0:T(1024)}, f32[768]{0:T(1024)}, f32[768]{0:T(1024)}, f32[7,768]{1,0:T(8,128)}, /*index=5*/f32[7,768]{1,0:T(8,128)}, f32[7,768]{1,0:T(8,128)}, s32[]{:T(128)}) while((s32[]{:T(128)}, f32[768]{0:T(1024)}, f32[768]{0:T(1024)}, f32[768]{0:T(1024)}, f32[7,768]{1,0:T(8,128)}, /*index=5*/f32[7,768]{1,0:T(8,128)}, ...), condition=%wide.region_15.16_spmd, body=%wide.region_14.15_spmd.sunk | while | flops 5378 | bytes 46173 | solution.py:25
  695.8 18.3 convolution_convert_fusion.2
  717.1 29.6 %reduce-scatter.15.cloned.1.call-done = bf16[96,768]{1,0:T(8,128)(2,1)} async-done(((bf16[768,768]{1,0:T(8,128)(2,1)}), bf16[96,768]{1,0:T(8,128)(2,1)}) %reduce-scatter.15.cloned.1.call-update) | async-done | bytes 147472 | tf_op jit(solution)/shard_map/reduce_scatter | solution.py:371
  813.2 18.9 %convolution_convert_fusion = bf16[768,6288]{1,0:T(8,128)(2,1)} fusion(bf16[768,768]{1,0:T(8,128)(2,1)S(1)} %copy-done.118, f32[768,6288]{0,1:T(8,128)} %get-tuple-element.338, f32[768]{0:T(1024)S(1)} %copy-done.104, s32[768]{0:T(1024)S(1)} %copy-done.91, f32[768]{0:T(1024)S(1)} %copy-done.106, pred[6288]{0:T(1024)(128)(4,1)S(1)} %copy-done.72), kind=kOutput, calls=%fused_computation.15 | convolution fusion | flops 7456260096 | bytes 30170256 | tf_op jit(solution)/shard_map/dot_general | solution.py:55
  832.2 22.9 %scatter_custom_fusion.1 = f32[6289,768]{1,0:T(8,128)} fusion(s32[2048]{0:T(1024)} %bitcast.161, f32[]{:T(128)} %constant.64.clone.1, bf16[2048,768]{1,0:T(8,128)(2,1)} %all-gather.35.cloned.1.call-done), kind=kCustom, calls=%fused_computation.16 | custom fusion | flops 3145728 | bytes 22466048 | tf_op jit(solution)/shard_map/scatter-add | solution.py:384
  866.5 13.5 copy.132
  893.3 38.1 %all-reduce.1 = f32[3,768]{1,0:T(4,128)S(1)} all-reduce(f32[3,768]{1,0:T(4,128)S(1)} %pad_maximum_fusion.1), channel_id=11, replica_groups=mesh['dp'=4,'vocab'=8] {'dp','vocab'}, use_global_device_ids=true, to_apply=%region_45.46.clone | all-reduce | flops 2304 | bytes 18432
  942.9 102.7 %reduce-scatter.23.cloned.1.call-done = f32[24,768]{1,0:T(8,128)} async-done(((f32[768,768]{1,0:T(8,128)}), f32[24,768]{1,0:T(8,128)}) %reduce-scatter.23.cloned.1.call-update) | async-done | bytes 73744 | tf_op jit(solution)/shard_map/reduce_scatter | solution.py:400
  1047.1 105.8 %reduce-scatter.19.cloned.1.call-done = f32[128,192]{0,1:T(8,128)} async-done(((f32[128,6144]{0,1:T(8,128)}), f32[128,192]{0,1:T(8,128)}) %reduce-scatter.19.cloned.1.call-update) | async-done | bytes 98320 | tf_op jit(solution)/shard_map/reduce_scatter | solution.py:397
  1154.4 123.1 %reduce-scatter.21.cloned.1.call-done = f32[24,2304]{1,0:T(8,128)} async-done(((f32[768,2304]{1,0:T(8,128)}), f32[24,2304]{1,0:T(8,128)}) %reduce-scatter.21.cloned.1.call-update) | async-done | bytes 221200 | tf_op jit(solution)/shard_map/reduce_scatter | solution.py:399
  1279.1 139.1 %reduce-scatter.27.cloned.1.call-done = f32[96,768]{1,0:T(8,128)} async-done(((f32[3072,768]{1,0:T(8,128)}), f32[96,768]{1,0:T(8,128)}) %reduce-scatter.27.cloned.1.call-update) | async-done | bytes 294928 | tf_op jit(solution)/shard_map/reduce_scatter | solution.py:402
  1419.8 139.6 %reduce-scatter.25.cloned.1.call-done = f32[24,3072]{1,0:T(8,128)} async-done(((f32[768,3072]{1,0:T(8,128)}), f32[24,3072]{1,0:T(8,128)}) %reduce-scatter.25.cloned.1.call-update) | async-done | bytes 294928 | tf_op jit(solution)/shard_map/reduce_scatter | solution.py:401
  1561.1 98.8 %reduce-scatter.17.cloned.1.call-done = bf16[192,6288]{1,0:T(8,128)(2,1)} async-done(((bf16[768,6288]{1,0:T(8,128)(2,1)}), bf16[192,6288]{1,0:T(8,128)(2,1)}) %reduce-scatter.17.cloned.1.call-update) | async-done | bytes 2414608 | tf_op jit(solution)/shard_map/reduce_scatter | solution.py:391
  1663.4 97.8 %reduce-scatter.29.cloned.1.call-done = bf16[192,6288]{1,0:T(8,128)(2,1)} async-done(((bf16[768,6288]{1,0:T(8,128)(2,1)}), bf16[192,6288]{1,0:T(8,128)(2,1)}) %reduce-scatter.29.cloned.1.call-update) | async-done | bytes 2414608
  1779.3 39.3 %all-reduce.2 = (f32[]{:T(128)}, f32[]{:T(128)}) all-reduce(f32[]{:T(128)S(6)} %reduce_sum.508, f32[]{:T(128)S(6)} %select_n.105), channel_id=1, replica_groups=mesh['dp'=4,'vocab'=8] {'dp','vocab'}, use_global_device_ids=true, to_apply=%region_55.56 | all-reduce | flops 2 | bytes 16 | tf_op jit(solution)/shard_map/psum | solution.py:407
  (469 shorter events, 294.1 us)
Async XLA Ops:
  7.2 48.1 %copy-start.114 = (s32[1,256]{1,0:T(1,128)S(1)}, s32[1,256]{1,0:T(1,128)}, u32[]{:S(2)}) copy-start(s32[1,256]{1,0:T(1,128)} %param.33) | copy-start | bytes 3076
  7.2 106.8 %all-gather.19.cloned.1.call-start = ((), (), s32[]{:S(2)}) async-start(), calls=%async_computation.9 | async-start | bytes 12288000 | tf_op jit(solution)/shard_map/all_gather | solution.py:326
  11.4 222.5 %all-gather.21.cloned.1.call-start = ((), (), s32[]{:S(2)}) async-start(), calls=%async_computation.11 | async-start | bytes 1622016 | tf_op jit(solution)/shard_map/all_gather | solution.py:318
  12.1 225.1 %reduce-scatter.13.cloned.1.call-start = ((), (), s32[]{:S(2)}) async-start(), calls=%async_computation.10 | async-start | bytes 3538944 | tf_op jit(solution)/shard_map/reduce_scatter | solution.py:335
  143.3 135.1 %all-gather.23.cloned.1.call-start = ((), (), s32[]{:S(2)}) async-start(), calls=%async_computation.12 | async-start | bytes 3649536 | tf_op jit(solution)/shard_map/all_gather | solution.py:320
  144.9 190.0 %all-gather.25.cloned.1.call-start = ((), (), s32[]{:S(2)}) async-start(), calls=%async_computation.13 | async-start | bytes 1216512 | tf_op jit(solution)/shard_map/all_gather | solution.py:321
  145.6 255.4 %all-gather.27.cloned.1.call-start = ((), (), s32[]{:S(2)}) async-start(), calls=%async_computation.14 | async-start | bytes 4866048 | tf_op jit(solution)/shard_map/all_gather | solution.py:322
  146.4 320.7 %all-gather.29.cloned.1.call-start = ((), (), s32[]{:S(2)}) async-start(), calls=%async_computation.15 | async-start | bytes 4866048 | tf_op jit(solution)/shard_map/all_gather | solution.py:323
  147.2 86.5 %copy-start.107 = (s32[1,256]{1,0:T(1,128)S(1)}, s32[1,256]{1,0:T(1,128)}, u32[]{:S(2)}) copy-start(s32[1,256]{1,0:T(1,128)} %param.35) | copy-start | bytes 3076
  147.2 420.8 %all-gather.33.cloned.1.call-start = ((), (), s32[]{:S(2)}) async-start(), calls=%async_computation.17 | async-start | bytes 12288000 | tf_op jit(solution)/shard_map/all_gather | solution.py:327
  151.3 441.5 %all-gather.31.cloned.1.call-start = ((), (), s32[]{:S(2)}) async-start(), calls=%async_computation.16 | async-start | bytes 1327104 | tf_op jit(solution)/shard_map/all_gather | solution.py:348
  231.8 46.6 %copy-start.92 = (f32[256]{0:T(256)}, f32[256]{0:T(256)S(1)}, u32[]{:S(2)}) copy-start(f32[256]{0:T(256)S(1)} %pad_maximum_fusion.2) | copy-start | bytes 3076
  233.0 48.7 %copy-start.43 = (f32[768]{0:T(1024)}, f32[768]{0:T(1024)S(1)}, u32[]{:S(2)}) copy-start(f32[768]{0:T(1024)S(1)} %get-tuple-element.259) | copy-start | bytes 9220
  233.0 167.9 %copy-start.47 = (f32[768]{0:T(1024)}, f32[768]{0:T(1024)S(1)}, u32[]{:S(2)}) copy-start(f32[768]{0:T(1024)S(1)} %get-tuple-element.258) | copy-start | bytes 9220
  237.2 44.6 %copy-start.52 = (f32[768]{0:T(1024)}, f32[768]{0:T(1024)S(1)}, u32[]{:S(2)}) copy-start(f32[768]{0:T(1024)S(1)} %get-tuple-element.325) | copy-start | bytes 9220
  237.2 163.7 %copy-start.45 = (f32[768]{0:T(1024)}, f32[768]{0:T(1024)S(1)}, u32[]{:S(2)}) copy-start(f32[768]{0:T(1024)S(1)} %get-tuple-element.323) | copy-start | bytes 9220
  286.3 48.6 %copy-start = (bf16[256,768]{1,0:T(8,128)(2,1)S(1)}, bf16[256,768]{1,0:T(8,128)(2,1)}, u32[]{:S(2)}) copy-start(bf16[256,768]{1,0:T(8,128)(2,1)} %reduce-scatter.13.cloned.1.call-done) | copy-start | bytes 1179652
  288.7 112.2 %copy-start.50 = (f32[768]{0:T(1024)S(1)}, f32[768]{0:T(1024)}, u32[]{:S(2)}) copy-start(f32[768]{0:T(1024)} %get-tuple-element.322) | copy-start | bytes 9220
  478.6 268.0 %reduce-scatter.15.cloned.1.call-start = ((), (), s32[]{:S(2)}) async-start(), calls=%async_computation.18 | async-start | bytes 1327104 | tf_op jit(solution)/shard_map/reduce_scatter | solution.py:371
  491.8 116.9 %copy-start.71 = (pred[6288]{0:T(1024)(128)(4,1)}, pred[6288]{0:T(1024)(128)(4,1)S(1)}, u32[]{:S(2)}) copy-start(pred[6288]{0:T(1024)(128)(4,1)S(1)} %add_compare_fusion) | copy-start | bytes 18868
  695.8 53.4 %copy-start.62 = (f32[768]{0:T(1024)S(1)}, f32[768]{0:T(1024)}, u32[]{:S(2)}) copy-start(f32[768]{0:T(1024)} %get-tuple-element.320) | copy-start | bytes 9220
  695.8 53.4 %copy-start.64 = (f32[768]{0:T(1024)S(1)}, f32[768]{0:T(1024)}, u32[]{:S(2)}) copy-start(f32[768]{0:T(1024)} %get-tuple-element.257) | copy-start | bytes 9220
  695.8 53.4 %copy-start.77 = (f32[256]{0:T(256)S(1)}, f32[256]{0:T(256)}, u32[]{:S(2)}) copy-start(f32[256]{0:T(256)} %copy-done.76) | copy-start | bytes 3076
  714.1 118.1 %all-gather.35.cloned.1.call-start = ((), (), s32[]{:S(2)}) async-start(), calls=%async_computation.19 | async-start | bytes 3538944 | tf_op jit(solution)/shard_map/all_gather | solution.py:383
  777.9 163.8 %all-reduce.5.cloned.1.call-start = ((), (), s32[]{:S(2)}) async-start(), calls=%async_computation.27 | async-start | bytes 262144
  786.5 259.1 %reduce-scatter.23.cloned.1.call-start = ((), (), s32[]{:S(2)}) async-start(), calls=%async_computation.23 | async-start | bytes 2433024 | tf_op jit(solution)/shard_map/reduce_scatter | solution.py:400
  789.5 363.4 %reduce-scatter.19.cloned.1.call-start = ((), (), s32[]{:S(2)}) async-start(), calls=%async_computation.21 | async-start | bytes 3244032 | tf_op jit(solution)/shard_map/reduce_scatter | solution.py:397
  791.8 485.7 %reduce-scatter.21.cloned.1.call-start = ((), (), s32[]{:S(2)}) async-start(), calls=%async_computation.22 | async-start | bytes 7299072 | tf_op jit(solution)/shard_map/reduce_scatter | solution.py:399
  796.2 622.0 %reduce-scatter.27.cloned.1.call-start = ((), (), s32[]{:S(2)}) async-start(), calls=%async_computation.25 | async-start | bytes 9732096 | tf_op jit(solution)/shard_map/reduce_scatter | solution.py:402
  805.2 754.3 %reduce-scatter.25.cloned.1.call-start = ((), (), s32[]{:S(2)}) async-start(), calls=%async_computation.24 | async-start | bytes 9732096 | tf_op jit(solution)/shard_map/reduce_scatter | solution.py:401
  812.0 847.9 %reduce-scatter.17.cloned.1.call-start = ((), (), s32[]{:S(2)}) async-start(), calls=%async_computation.20 | async-start | bytes 12288000 | tf_op jit(solution)/shard_map/reduce_scatter | solution.py:391
  832.1 929.1 %reduce-scatter.29.cloned.1.call-start = ((), (), s32[]{:S(2)}) async-start(), calls=%async_computation.26 | async-start | bytes 12288000
  (109 other events, 546.0 us)
Sparse Core Ops, SparseCore 0:
  11.5 102.5 all-gather.18
  117.7 55.0 all-gather.20
  175.6 39.6 reduce-scatter.12
  218.8 59.5 all-gather.22
  281.9 52.9 all-gather.24
  338.3 62.5 all-gather.26
  404.6 62.4 all-gather.28
  469.5 98.4 all-gather.32
  570.2 22.6 all-gather.30
  714.3 32.3 reduce-scatter.14
  778.0 36.3 all-gather.34
  820.3 121.2 all-reduce.4
  947.5 98.0 reduce-scatter.22
  1052.3 100.5 reduce-scatter.18
  1159.4 118.0 reduce-scatter.20
  1283.2 134.9 reduce-scatter.26
  1424.9 134.4 reduce-scatter.24
  1562.4 97.3 reduce-scatter.16
  1663.0 98.2 reduce-scatter.28
where the time goes:
time: 1880 us
  waiting for transfers between devices  1170 us (62%)
  blocking collectives  277 us (15%)
  local copies, waits for them, and re-layouts  144 us (8%)
  other arithmetic  141 us (8%)
  matrix products  114 us (6%)
  between operations  24.7 us (1%)
    reduce_scatter x1, waiting for transfers between devices, shards(): lax.psum_scatter(grad_up, ('dp', 'vocab'), scatter_dimension=0, tiled=True)  140 us
    reduce_scatter x1, waiting for transfers between devices, shards(): lax.psum_scatter(grad_down, ('dp', 'vocab'), scatter_dimension=0, tiled=T...  139 us
    reduce_scatter x1, waiting for transfers between devices, shards(): lax.psum_scatter(grad_qkv, ('dp', 'vocab'), scatter_dimension=0, tiled=True)  123 us
    unnamed x21, waiting for transfers between devices  108 us
    reduce_scatter x1, waiting for transfers between devices, shards(): lax.psum_scatter(grad_ada, ('dp', 'vocab'), scatter_dimension=1, tiled=True)  106 us
    reduce_scatter x1, waiting for transfers between devices, shards(): lax.psum_scatter(grad_out, ('dp', 'vocab'), scatter_dimension=0, tiled=True)  103 us
    reduce_scatter x1, waiting for transfers between devices, shards(): lax.psum_scatter(grad_head.astype(jnp.bfloat16), 'dp', scatter_dimension=...  98.8 us
    all_gather x1, waiting for transfers between devices, shards(): lax.all_gather(head_table.astype(jnp.bfloat16), 'dp', axis=0, tiled=True)  74.8 us
  transfers between devices with their start and end apart: 19, of which 16 were waited for; matrix products, arithmetic and copies ran while one was open for 11% of the time, Pallas kernels for 0%

commit v1 on v0

v1 whole, which is shorter than its diff:
```python
import functools

import jax
import jax.numpy as jnp
from jax import lax
from jax.experimental import pallas as pl
from jax.experimental.pallas import tpu as pltpu
from jax.sharding import PartitionSpec as P

HEAD_DIM = 64
VOCAB = 50258
FREQ = 256
FEWEST_MASKED = 32
LANES = 128


norm_epsilon = 1e-06
weight_cap = 20.0
clip_level = 1.0
learn_rate = 30.0
embed_rate = 2000.0
momentum_rate = 0.9
average_rate = 0.5
highest = lax.Precision.HIGHEST
low = jnp.bfloat16
wide = jnp.float32


class Links:
    def __init__(self, dp_count, vocab_count):
        core = 2 if vocab_count % 2 == 0 else 1
        side = 1
        while side * side < dp_count:
            side *= 2
        self.dp_count, self.vocab_count = dp_count, vocab_count
        self.axes = {
            "u": ("dp", side, dp_count // side),
            "v": ("dp", 1, side),
            "z": ("vocab", core, vocab_count // core),
            "c": ("vocab", 1, core),
            "dp": ("dp", 1, dp_count),
        }

    def size(self, axis):
        return self.axes[axis][2]

    def place(self, axis):
        group, unit, size = self.axes[axis]
        return (lax.axis_index(group) // unit) % size

    def hop(self, value, axis, step):
        group, unit, _ = self.axes[axis]
        flip = step * unit
        across, along = (flip, 0) if group == "dp" else (0, flip)
        pairs = [
            (d * self.vocab_count + w, (d ^ across) * self.vocab_count + (w ^ along))
            for d in range(self.dp_count)
            for w in range(self.vocab_count)
        ]
        return lax.ppermute(value, ("dp", "vocab"), pairs)

    def heard(self, value, axis):
        return [value] + [self.hop(value, axis, k) for k in range(1, self.size(axis))]

    def ordered(self, pieces, axis):
        place, count = self.place(axis), len(pieces)
        slots = []
        for slot in range(count):
            value = pieces[slot]
            for other in range(1, count):
                value = jnp.where(place == other, pieces[slot ^ other], value)
            slots.append(value)
        return slots

    def stack(self, value, axis):
        return jnp.stack(self.ordered(self.heard(value, axis), axis))

    def fold(self, value, axis, dim):
        place, count = self.place(axis), self.size(axis)
        own = lax.dynamic_index_in_dim(value, place, dim, keepdims=False)
        total = own.astype(wide)
        for k in range(1, count):
            part = lax.dynamic_index_in_dim(value, place ^ k, dim, keepdims=False)
            total = total + self.hop(part, axis, k).astype(wide)
        return total

    def stack_all_small(self, value):
        shape = value.shape
        value = self.stack(value, "z")
        value = self.stack(value, "dp")
        value = self.stack(value, "c")
        value = jnp.moveaxis(value, 0, 2)
        return value.reshape((self.dp_count * self.vocab_count,) + shape)

    def stack_all(self, value, cut):
        rows, width = value.shape
        value = self.stack(value, "z")
        left, right = value[..., :cut], value[..., cut:]
        left = self.stack(self.stack(left, "v"), "u")
        if cut == width:
            return jnp.stack(self.ordered(self.heard(left, "c"), "c"), 3).reshape(-1, width)
        right = jnp.swapaxes(self.stack(self.stack(right, "u"), "v"), 0, 1)
        parts = [jnp.stack(self.ordered(self.heard(part, "c"), "c"), 3) for part in (left, right)]
        return jnp.concatenate(parts, -1).reshape(-1, width)

    def fold_all(self, value, cut):
        rows, width = value.shape
        value = value.reshape(
            self.size("u"), self.size("v"), self.size("z"), self.size("c"), -1, width
        )
        value = self.fold(value, "c", 3).astype(low)
        left, right = value[..., :cut], value[..., cut:]
        left = self.fold(self.fold(left, "u", 0).astype(low), "v", 0)
        right = self.fold(self.fold(right, "v", 1).astype(low), "u", 0)
        value = jnp.concatenate([left, right], -1).astype(low)
        return self.fold(value, "z", 0)

    def exchange(self, pieces):
        came = [pieces(0)] + [self.hop(pieces(k), "dp", k) for k in range(1, self.dp_count)]
        return self.ordered(came, "dp")

    def total(self, value, join):
        for axis in ("z", "dp", "c"):
            value = join(self.heard(value, axis))
        return value


def half_cut(width):
    return max(LANES, (width // (2 * LANES)) * LANES) if width > LANES else width


def features(level, freq_count):
    sigma_level = -jnp.log1p(-(1.0 - 0.001) * level)
    half_count = freq_count // 2
    frequency = jnp.exp(-jnp.log(10000.0) * jnp.arange(half_count, dtype=wide) / half_count)
    angles = sigma_level[..., None] * frequency
    return jnp.concatenate([jnp.cos(angles), jnp.sin(angles)], -1)


def nelbo_weight(level):
    sigma_level = -jnp.log1p(-(1.0 - 0.001) * level)
    rate_value = (1.0 - 0.001) / (1.0 - (1.0 - 0.001) * level)
    return jnp.minimum(rate_value / jnp.expm1(sigma_level), weight_cap)


def norm_mod(values, gain_row, shift_row, scale_row):
    center = values - jnp.mean(values, -1, keepdims=True)
    spread = jnp.mean(center * center, -1, keepdims=True)
    return center * lax.rsqrt(spread + norm_epsilon) * gain_row * (1.0 + scale_row) + shift_row


def times_rows(left_matrix, right_matrix):
    return lax.dot_general(
        left_matrix, right_matrix, (((0,), (0,)), ((), ())), preferred_element_type=wide
    )


def times_transposed(left_matrix, right_matrix):
    return lax.dot_general(
        left_matrix, right_matrix, (((1,), (1,)), ((), ())), preferred_element_type=wide
    )


def look_up_kernel(kept, first_ref, last_ref, base_ref, ids_ref, table_ref, out_ref, rows_ref):
    rows_ref[...] = jnp.zeros_like(rows_ref)
    base = base_ref[0]

    def one_sequence(s, carry):
        first, last = first_ref[s], last_ref[s]

        def some(i, inner):
            for q in range(4):
                at = s * kept + jnp.minimum(first + 4 * i + q, last - 1)
                row = ids_ref[at] - base
                rows_ref[pl.ds(at, 1), :] = table_ref[pl.ds(row, 1), :]
            return inner

        return lax.fori_loop(0, (last - first + 3) // 4, some, carry)

    lax.fori_loop(0, first_ref.shape[0], one_sequence, 0)
    out_ref[...] = rows_ref[...].astype(out_ref.dtype)


def look_up(first, last, base, ids, table, kept):
    count, width = ids.shape[0], table.shape[1]
    smem = pl.BlockSpec(memory_space=pltpu.SMEM)
    vmem = pl.BlockSpec(memory_space=pltpu.VMEM)
    return pl.pallas_call(
        functools.partial(look_up_kernel, kept),
        out_shape=jax.ShapeDtypeStruct((count, width), low),
        in_specs=[smem, smem, smem, smem, vmem],
        out_specs=vmem,
        scratch_shapes=[pltpu.VMEM((count, width), wide)],
        compiler_params=pltpu.CompilerParams(vmem_limit_bytes=56 * 2**20),
    )(first, last, base, ids, table)


def add_up_kernel(kept, first_ref, last_ref, base_ref, ids_ref, grad_ref, out_ref, sum_ref):
    span = out_ref.shape[1]
    sum_ref[...] = jnp.zeros_like(sum_ref)
    base = base_ref[0]

    def one_sequence(s, carry):
        first, last = first_ref[s], last_ref[s]

        def some(i, inner):
            for q in range(4):
                k = first + 4 * i + q
                at = s * kept + jnp.minimum(k, last - 1)
                row = jnp.where(k < last, ids_ref[at] - base, span)
                sum_ref[pl.ds(row, 1), :] = sum_ref[pl.ds(row, 1), :] + grad_ref[pl.ds(at, 1), :]
            return inner

        return lax.fori_loop(0, (last - first + 3) // 4, some, carry)

    lax.fori_loop(0, first_ref.shape[0], one_sequence, 0)
    whole = span // LANES

    def turn(b, carry):
        at = pl.multiple_of(b * LANES, LANES)
        out_ref[:, pl.ds(at, LANES)] = sum_ref[pl.ds(at, LANES), :].T
        return carry

    lax.fori_loop(0, whole, turn, 0)
    if span > whole * LANES:
        rest = span - whole * LANES
        out_ref[:, whole * LANES :] = sum_ref[whole * LANES : (whole + 1) * LANES, :].T[:, :rest]


def add_up(first, last, base, ids, grads, span, kept):
    count, width = grads.shape
    smem = pl.BlockSpec(memory_space=pltpu.SMEM)
    vmem = pl.BlockSpec(memory_space=pltpu.VMEM)
    padded = (span // LANES + 1) * LANES
    return pl.pallas_call(
        functools.partial(add_up_kernel, kept),
        out_shape=jax.ShapeDtypeStruct((width, span), wide),
        in_specs=[smem, smem, smem, smem, vmem],
        out_specs=vmem,
        scratch_shapes=[pltpu.VMEM((padded, width), wide)],
        compiler_params=pltpu.CompilerParams(vmem_limit_bytes=56 * 2**20),
    )(first, last, base, ids, grads)


def attend(queries, keys_all, values_all, segment):
    factor = HEAD_DIM ** (-0.5)
    scores = jnp.einsum("qhd,khd->hqk", queries, keys_all, preferred_element_type=wide) * factor
    scores = jnp.where((segment[:, None] == segment[None, :])[None], scores, -1e30)
    peak_value = jnp.max(scores, -1, keepdims=True)
    expo = jnp.exp(scores - peak_value)
    probs = expo / jnp.sum(expo, -1, keepdims=True)
    result = jnp.einsum("hqk,khd->qhd", probs.astype(low), values_all, preferred_element_type=wide)
    return result.reshape(queries.shape[0], -1), probs


def attend_back(queries, keys_all, values_all, probs, grad_attended):
    factor = HEAD_DIM ** (-0.5)
    grad_values = jnp.einsum(
        "hqk,qhd->khd", probs.astype(low), grad_attended, preferred_element_type=wide
    )
    grad_probs = jnp.einsum("qhd,khd->hqk", grad_attended, values_all, preferred_element_type=wide)
    grad_scores = (probs * (grad_probs - jnp.sum(probs * grad_probs, -1, keepdims=True))).astype(
        low
    )
    grad_query = (
        jnp.einsum("hqk,khd->qhd", grad_scores, keys_all, preferred_element_type=wide) * factor
    )
    grad_keys = (
        jnp.einsum("hqk,qhd->khd", grad_scores, queries, preferred_element_type=wide) * factor
    )
    return (grad_query, grad_keys, grad_values)


def layer_forward(weights, gains, hidden_start, modulation, segment):
    total_rows, model_width = hidden_start.shape
    head_count = model_width // HEAD_DIM
    normed_a = norm_mod(hidden_start, gains[0], modulation[0], modulation[1]).astype(low)
    triple = jnp.dot(normed_a, weights["qkv"], preferred_element_type=wide).astype(low)
    triple = triple.reshape(total_rows, 3, head_count, HEAD_DIM)
    attended, probs = attend(triple[:, 0], triple[:, 1], triple[:, 2], segment)
    attended = attended.astype(low)
    branch_a = jnp.dot(attended, weights["out"], preferred_element_type=wide)
    hidden_mid = hidden_start + modulation[2] * branch_a
    normed_b = norm_mod(hidden_mid, gains[1], modulation[3], modulation[4]).astype(low)
    up_values = jnp.dot(normed_b, weights["up"], preferred_element_type=wide)
    active = jax.nn.gelu(up_values, approximate=True).astype(low)
    branch_m = jnp.dot(active, weights["down"], preferred_element_type=wide)
    hidden_end = hidden_mid + modulation[5] * branch_m
    final_rows = norm_mod(hidden_end, gains[2], modulation[6], modulation[7])
    kept = (
        normed_a,
        triple,
        attended,
        probs,
        branch_a,
        hidden_mid,
        normed_b,
        up_values,
        active,
        branch_m,
        hidden_end,
    )
    return (final_rows, kept)


def layer_backward(weights, gains, hidden_start, modulation, kept, grad_final):
    (
        normed_a,
        triple,
        attended,
        probs,
        branch_a,
        hidden_mid,
        normed_b,
        up_values,
        active,
        branch_m,
        hidden_end,
    ) = kept
    total_rows = hidden_start.shape[0]
    _, back_third = jax.vjp(norm_mod, hidden_end, gains[2], modulation[6], modulation[7])
    grad_end, grad_gain3, grad_shift3, grad_scale3 = back_third(grad_final)
    grad_gate2 = jnp.sum(grad_end * branch_m, 0)
    grad_branch_m = (modulation[5] * grad_end).astype(low)
    grad_down = times_rows(active, grad_branch_m).astype(low)
    grad_active = times_transposed(grad_branch_m, weights["down"])
    _, back_gelu = jax.vjp(lambda inputs: jax.nn.gelu(inputs, approximate=True), up_values)
    grad_upper = back_gelu(grad_active)[0].astype(low)
    grad_up = times_rows(normed_b, grad_upper).astype(low)
    grad_normed_b = times_transposed(grad_upper, weights["up"])
    _, back_second = jax.vjp(norm_mod, hidden_mid, gains[1], modulation[3], modulation[4])
    grad_mid_norm, grad_gain2, grad_shift2, grad_scale2 = back_second(grad_normed_b)
    grad_mid = grad_end + grad_mid_norm
    grad_gate1 = jnp.sum(grad_mid * branch_a, 0)
    grad_branch_a = (modulation[2] * grad_mid).astype(low)
    grad_out = times_rows(attended, grad_branch_a).astype(low)
    grad_attended = times_transposed(grad_branch_a, weights["out"]).astype(low)
    grad_attended = grad_attended.reshape(total_rows, triple.shape[2], HEAD_DIM)
    grad_query, grad_keys, grad_values = attend_back(
        triple[:, 0], triple[:, 1], triple[:, 2], probs, grad_attended
    )
    grad_triple = (
        jnp.stack([grad_query, grad_keys, grad_values], 1).reshape(total_rows, -1).astype(low)
    )
    grad_qkv = times_rows(normed_a, grad_triple).astype(low)
    grad_normed_a = times_transposed(grad_triple, weights["qkv"])
    _, back_first = jax.vjp(norm_mod, hidden_start, gains[0], modulation[0], modulation[1])
    grad_start_norm, grad_gain1, grad_shift1, grad_scale1 = back_first(grad_normed_a)
    grad_start = grad_mid + grad_start_norm
    grad_mod = jnp.concatenate(
        [
            grad_shift1,
            grad_scale1,
            grad_gate1,
            grad_shift2,
            grad_scale2,
            grad_gate2,
            grad_shift3,
            grad_scale3,
        ]
    )
    grad_gains = jnp.concatenate([grad_gain1, grad_gain2, grad_gain3])
    grads = {"qkv": grad_qkv, "out": grad_out, "up": grad_up, "down": grad_down}
    return (grad_start, grad_mod, grad_gains, grads)


def advance(weight_now, moment_now, average_now, gradient, clip_factor, rate_now):
    clipped = gradient * clip_factor
    moment_next = momentum_rate * moment_now + clipped
    weight_next = weight_now - rate_now * (clipped + momentum_rate * moment_next)
    return (
        weight_next,
        moment_next,
        average_rate * average_now + (1.0 - average_rate) * weight_next,
    )


def padded_rows(value, rows_of):
    size = value.shape[0]
    rows = -(-size // (rows_of * LANES)) * rows_of
    return jnp.pad(value, (0, rows * LANES - size)).reshape(rows, LANES)


def join_stats(pieces):
    peak_value = functools.reduce(jnp.maximum, [piece[0] for piece in pieces])
    summed = sum(piece[1] * jnp.exp(piece[0] - peak_value) for piece in pieces)
    return jnp.stack([peak_value, summed, sum(piece[2] for piece in pieces)])


def shards(
    x_clean,
    mask_index,
    segment_ids,
    noise_level,
    embedding,
    head_table,
    w_time,
    w_ada,
    norm_gains,
    w_qkv,
    w_out,
    w_up,
    w_down,
    *states,
):
    vocab_index = lax.axis_index("vocab")
    dp_index = lax.axis_index("dp")
    vocab_count = lax.axis_size("vocab")
    dp_count = lax.axis_size("dp")
    links = Links(dp_count, vocab_count)
    device_count = dp_count * vocab_count
    device_index = dp_index * vocab_count + vocab_index
    length = x_clean.shape[1]
    slot_count = mask_index.shape[1]
    kept_count = length - FEWEST_MASKED
    span = embedding.shape[0]
    columns = head_table.shape[1]
    slice_width = embedding.shape[1]
    model_width = slice_width * dp_count
    cond_width = w_time.shape[1]
    mask_id = VOCAB - 1

    positions = jnp.arange(length)
    own_slots = mask_index[0]
    hit = own_slots[:, None] == positions[None, :]
    masked = jnp.any(hit, axis=0)
    sort_key = jnp.where(masked, mask_id, x_clean[0]) * length + positions
    rank = jnp.sum((sort_key[None, :] < sort_key[:, None]).astype(jnp.int32), 1)
    to_sorted = rank[:, None] == jnp.arange(kept_count)[None, :]
    sorted_ids = jnp.sum(jnp.where(to_sorted, sort_key[:, None], 0), 0) // length
    spots = jnp.minimum(own_slots, length - 1)
    at_spot = spots[:, None] == positions[None, :]
    targets_own = jnp.sum(jnp.where(at_spot, x_clean[0][None, :], 0), 1)
    targets_own = jnp.where(own_slots < length, targets_own, -1)
    numbers = links.stack_all_small(
        padded_rows(jnp.concatenate([sorted_ids, targets_own]), 1)
    ).reshape(device_count, -1)
    ids_all = numbers[:, :kept_count]
    targets = numbers[:, kept_count : kept_count + slot_count].reshape(-1)
    live = (targets >= 0).astype(wide)
    masked_count = jnp.sum(live)

    level = lax.dynamic_index_in_dim(noise_level, vocab_index, keepdims=False)
    mask_local = mask_id - vocab_index * span
    mask_owner = (mask_local >= 0) & (mask_local < span)
    table_flat = embedding.T
    mask_row = lax.dynamic_index_in_dim(
        table_flat, jnp.clip(mask_local, 0, span - 1), 1, keepdims=False
    )
    mask_row = jnp.where(mask_owner, mask_row, 0.0)
    sizes = (w_time.size, norm_gains.size, slice_width, 1)
    small = jnp.concatenate(
        [w_time.reshape(-1), norm_gains.reshape(-1), mask_row]
    ).astype(low).astype(wide)
    small = links.stack_all_small(
        padded_rows(jnp.concatenate([small, level[None]]), 8)
    ).reshape(device_count, -1)
    starts = [sum(sizes[:n]) for n in range(5)]
    time_weight, gains_all, mask_rows, levels = [
        small[:, starts[n] : starts[n + 1]] for n in range(4)
    ]
    time_weight = time_weight.reshape(-1, cond_width)
    gains = jnp.swapaxes(gains_all.reshape(device_count, 3, -1), 0, 1).reshape(3, model_width)
    mask_row_full = jnp.sum(mask_rows.reshape(dp_count, vocab_count, slice_width), 1).reshape(-1)
    levels = levels[:, 0]

    first = jnp.sum((ids_all < vocab_index * span).astype(jnp.int32), 1)
    stop_id = jnp.minimum((vocab_index + 1) * span, mask_id)
    last = jnp.maximum(jnp.sum((ids_all < stop_id).astype(jnp.int32), 1), first)
    base = (vocab_index * span)[None].astype(jnp.int32)
    flat_ids = ids_all.reshape(-1)
    looked = look_up(first, last, base, flat_ids, embedding, kept_count)
    looked = looked.reshape(
        dp_count, links.size("z"), links.size("c"), kept_count, slice_width
    )
    looked = links.fold(looked, "c", 2).astype(low)
    looked = links.fold(looked, "z", 1).astype(low)
    looked = links.exchange(
        lambda k: lax.dynamic_index_in_dim(looked, dp_index ^ k, 0, keepdims=False)
    )
    looked = jnp.concatenate(looked, 1)
    spread = to_sorted.astype(low)
    hidden_start = jnp.dot(spread, looked, preferred_element_type=wide)
    hidden_start = jnp.where(masked[:, None], mask_row_full[None, :], hidden_start)

    shard_of = {"ada": w_ada.T, "qkv": w_qkv, "out": w_out, "up": w_up, "down": w_down}
    cut_of = {name: half_cut(shard.shape[1]) for name, shard in shard_of.items()}
    weights = {
        name: links.stack_all(shard.astype(low), cut_of[name]) for name, shard in shard_of.items()
    }
    piece = -(-columns // (dp_count * LANES)) * LANES
    head_low = jnp.pad(head_table.astype(low), ((0, 0), (0, piece * dp_count - columns)))
    head_columns = jnp.concatenate(
        links.exchange(
            lambda k: lax.dynamic_slice_in_dim(head_low, (dp_index ^ k) * piece, piece, 1)
        ),
        0,
    )

    ada_weight = weights["ada"].astype(wide)
    spectrum_all = features(levels, FREQ)
    spectrum = features(level[None], FREQ)
    before_time = jnp.dot(spectrum, time_weight, precision=highest)
    hidden_time, back_silu = jax.vjp(jax.nn.silu, before_time)
    modulation = lax.dot_general(
        hidden_time, ada_weight, (((1,), (1,)), ((), ())), precision=highest
    ).reshape(8, -1)
    segment = segment_ids[0]
    final_rows, kept = layer_forward(weights, gains, hidden_start, modulation, segment)

    picked = jnp.dot(
        at_spot.astype(low), final_rows.astype(low), preferred_element_type=wide
    ).astype(low)
    rows_all = links.stack_all(picked, half_cut(model_width))
    logits = jnp.dot(rows_all, head_columns, preferred_element_type=wide)
    local_columns = jnp.arange(piece)
    own_columns = dp_index * piece + local_columns
    inside = (own_columns < columns) & (vocab_index * columns + own_columns < VOCAB)
    logits = jnp.where(inside[None, :], logits, -1e30)
    peak_value = jnp.max(logits, 1)
    expo_total = jnp.sum(jnp.exp(logits - peak_value[:, None]), 1)
    target_local = targets - vocab_index * columns - dp_index * piece
    onehot = (local_columns[None, :] == target_local[:, None]) & inside[None, :]
    target_logit = jnp.sum(jnp.where(onehot, logits, 0.0), 1)
    stats = jnp.stack([peak_value, expo_total, target_logit]).reshape(3, -1, LANES)
    stats = links.total(stats, join_stats).reshape(3, -1)
    log_total = stats[0] + jnp.log(stats[1])
    row_weight = jnp.repeat(nelbo_weight(levels), slot_count) * live
    loss_sum = jnp.sum(row_weight * (log_total - stats[2]))
    grad_logits = (row_weight / masked_count)[:, None] * (
        jnp.exp(logits - log_total[:, None]) - onehot.astype(wide)
    )
    grad_logits = grad_logits.astype(low)
    grad_rows = times_transposed(grad_logits, head_columns).astype(low)
    grad_mine = links.fold_all(grad_rows, half_cut(model_width)).astype(low)
    alive_spot = (at_spot & (own_slots < length)[:, None]).astype(low)
    grad_final = times_rows(alive_spot, grad_mine)
    grad_head = times_rows(rows_all, grad_logits).astype(low)
    grad_head = grad_head.reshape(dp_count, slice_width, piece)
    grad_head = jnp.concatenate(
        links.exchange(
            lambda k: lax.dynamic_index_in_dim(grad_head, dp_index ^ k, 0, keepdims=False)
        ),
        1,
    )[:, :columns].astype(wide)

    grad_start, grad_mod, grad_gains, layer_grads = layer_backward(
        weights, gains, hidden_start, modulation, kept, grad_final
    )
    layer_grads = {
        name: links.fold_all(grad, cut_of[name]) for name, grad in layer_grads.items()
    }

    start_low = grad_start.astype(low)
    mask_grad = jnp.sum(jnp.where(masked[:, None], start_low.astype(wide), 0.0), 0)
    sent = times_rows(spread, start_low).astype(low).reshape(kept_count, dp_count, slice_width)
    came = jnp.stack(
        links.exchange(
            lambda k: lax.dynamic_index_in_dim(sent, dp_index ^ k, 1, keepdims=False)
        )
    )
    came = links.stack(links.stack(came, "z"), "c")
    came = came.transpose(2, 1, 0, 3, 4).reshape(-1, slice_width)
    grad_table = add_up(first, last, base, flat_ids, came.astype(wide), span, kept_count)

    grad_hidden_time = jnp.dot(grad_mod[None, :], ada_weight, precision=highest)
    grad_before = back_silu(grad_hidden_time)[0]
    parts = (hidden_time[0], grad_before[0], mask_grad, grad_gains, grad_mod)
    part_sizes = [part.shape[0] for part in parts]
    part_starts = [sum(part_sizes[:n]) for n in range(len(parts) + 1)]
    vectors = links.stack_all_small(padded_rows(jnp.concatenate(parts), 8)).reshape(
        device_count, -1
    )
    hidden_time_all, grad_before_all, mask_grads, gains_each, mods_each = [
        vectors[:, part_starts[n] : part_starts[n + 1]] for n in range(len(parts))
    ]
    time_rows = w_time.shape[0]
    grad_time = lax.dot_general(
        lax.dynamic_slice_in_dim(spectrum_all, device_index * time_rows, time_rows, 1),
        grad_before_all,
        (((0,), (0,)), ((), ())),
        precision=highest,
    )
    ada_columns = w_ada.shape[1]
    grad_ada = lax.dot_general(
        lax.dynamic_slice_in_dim(mods_each, device_index * ada_columns, ada_columns, 1),
        hidden_time_all,
        (((0,), (0,)), ((), ())),
        precision=highest,
    )
    gain_columns = norm_gains.shape[1]
    grad_gain_rows = lax.dynamic_slice_in_dim(
        jnp.sum(gains_each, 0).reshape(3, model_width), device_index * gain_columns, gain_columns, 1
    )
    mask_grad_own = lax.dynamic_slice_in_dim(
        jnp.sum(mask_grads, 0), dp_index * slice_width, slice_width, 0
    )
    mask_column = (jnp.arange(span) == mask_local)[None, :]
    grad_table = grad_table + jnp.where(mask_column, mask_grad_own[:, None], 0.0)

    grads_all = (
        grad_table,
        grad_head,
        grad_time,
        grad_ada,
        grad_gain_rows,
        layer_grads["qkv"],
        layer_grads["out"],
        layer_grads["up"],
        layer_grads["down"],
    )
    squares = sum(jnp.sum(gradient * gradient) for gradient in grads_all)
    square_total = links.total(jnp.broadcast_to(squares, (8, LANES)), sum)[0, 0]
    grad_norm = jnp.sqrt(square_total)
    clip_factor = jnp.minimum(1.0, clip_level / (grad_norm + 1e-06))
    weights_now = (embedding, head_table, w_time, w_ada, norm_gains, w_qkv, w_out, w_up, w_down)
    turned = (0, 3)
    updated = []
    for place, (weight_now, gradient) in enumerate(zip(weights_now, grads_all)):
        state = (weight_now, states[place], states[len(weights_now) + place])
        if place in turned:
            state = tuple(array.T for array in state)
        rate = embed_rate if place == 0 else learn_rate
        result = advance(*state, gradient, clip_factor, rate)
        if place in turned:
            result = tuple(array.T for array in result)
        updated.append(result)
    new_arrays = tuple(result[n] for n in range(3) for result in updated)
    return (*new_arrays, loss_sum, masked_count, grad_norm)


def solution(mesh):
    both = ("dp", "vocab")
    weights_placed = (
        P("vocab", "dp"),
        P("dp", "vocab"),
        P(both, None),
        P(None, both),
        P(None, both),
        P(both, None),
        P(both, None),
        P(both, None),
        P(both, None),
    )
    return jax.shard_map(
        shards,
        mesh=mesh,
        in_specs=(P(both, None), P(both, None), P(both, None), P("dp")) + 3 * weights_placed,
        out_specs=3 * weights_placed + (P(), P(), P()),
        check_vma=False,
    )
```

time: 1880 us -> 803 us (0.43)
  waiting for transfers between devices: 1170 us -> 267 us
  blocking collectives: 277 us -> 0 us
  starting transfers between devices: 1.79 us -> 166 us
  local copies, waits for them, and re-layouts: 144 us -> 81.7 us
  matrix products: 114 us -> 76.8 us
  Pallas kernels: 0 us -> 25.1 us
  other arithmetic: 141 us -> 165 us
    reduce_scatter x8 -> x0, waiting for transfers between devices: 739 us -> none  [the longest x1 140 us: shards(): lax.psum_scatter(grad_up, ('dp', 'vocab'), scatter_dimension=0, tiled=True)]
    all_gather x9 -> x0, waiting for transfers between devices: 327 us -> none  [the longest x1 74.8 us: shards(): lax.all_gather(head_table.astype(jnp.bfloat16), 'dp', axis=0, tiled=True)]
    ppermute x0 -> x146, waiting for transfers between devices: none -> 267 us  [hop(): return lax.ppermute(value, ('dp', 'vocab'), pairs)]
    all_gather x7 -> x0, blocking collectives: 200 us -> none  [the longest x1 43.1 us: shards(): lax.all_gather(mask_index, ('dp', 'vocab'), axis=0, tiled=True)]
    ppermute x0 -> x146, starting transfers between devices: none -> 166 us  [hop(): return lax.ppermute(value, ('dp', 'vocab'), pairs)]
    unnamed x21 -> x0, waiting for transfers between devices: 108 us -> none
    unnamed x262 -> x438, local copies, waits for them, and re-layouts: 70.4 us -> 27.3 us
    another operation x2 -> x102, other arithmetic: 0.15 us -> 40.8 us  [the longest x72 25.5 us: stack(): return jnp.stack(self.ordered(self.heard(value, axis), axis))]
  transfers between devices with their start and end apart: 19 -> 146, of which waited for: 16 -> 65; matrix products, arithmetic and copies ran while one was open for 11% -> 23% of each run, Pallas kernels for 0% -> 3%
where the time goes in v1:
time: 803 us; the launch traced here: 795 us
  waiting for transfers between devices  267 us (33%)
  starting transfers between devices  166 us (21%)
  other arithmetic  165 us (21%)
  local copies, waits for them, and re-layouts  81.7 us (10%)
  matrix products  76.8 us (10%)
  Pallas kernels  25.1 us (3%)
  between operations  13.3 us (2%)
    ppermute x146, waiting for transfers between devices, hop(): return lax.ppermute(value, ('dp', 'vocab'), pairs)  267 us
    ppermute x146, starting transfers between devices, hop(): return lax.ppermute(value, ('dp', 'vocab'), pairs)  166 us
    unnamed x438, local copies, waits for them, and re-layouts  27.3 us
    another operation x72, other arithmetic, stack(): return jnp.stack(self.ordered(self.heard(value, axis), axis))  25.5 us
    dot_general x7, matrix products, times_rows(): lax.dot_general(left_matrix, right_matrix, (((0,), (0,)), ((), ())), pref...  25 us
    dot_general x5, matrix products, times_transposed(): lax.dot_general(left_matrix, right_matrix, (((1,), (1,)), ((), ())), pref...  17.5 us
  transfers between devices with their start and end apart: 146, of which 65 were waited for; matrix products, arithmetic and copies ran while one was open for 23% of the time, Pallas kernels for 3%

profile of v1, /device:TPU:0, one launch (start us, length us, event | category | flops | bytes accessed | tf_op | source)
XLA Modules:
  0.0 794.9 jit_solution(2116471056336060478)
XLA Ops:
  27.8 6.4 copy.294.table_ref
  49.2 9.4 %shard_map.526 = bf16[7168,192]{1,0:T(8,128)(2,1)} custom-call(s32[32]{0:T(128)} %copy-done.173, s32[32]{0:T(128)} %max.60.last_ref, s32[1]{0:T(128)} %bitcast.17.base_ref, s32[7168]{0:T(1024)} %reshape.581.ids_ref, f32[6288,192]{1,0:T(8,128)} %copy.294.table_ref), custom_call_target="tpu_custom_call" | custom-call | tf_op jit(solution)/shard_map/pallas_call | solution.py:188
  85.9 7.8 collective-permute-done.28
  108.0 5.8 collective-permute-done.55
  139.5 5.6 collective-permute-done.60
  164.4 6.3 collective-permute-done.52
  170.9 6.2 collective-permute-done.61
  197.0 7.3 collective-permute-done.17
  204.2 21.4 %collective-permute-done.16 = bf16[4,224,192]{1,2,0:T(8,128)(2,1)S(1)} collective-permute-done((bf16[4,224,192]{1,2,0:T(8,128)(2,1)S(1)}, bf16[4,224,192]{1,2,0:T(8,128)(2,1)S(1)}, u32[]{:S(2)}, u32[]{:S(2)}) %collective-permute-start.16) | collective-permute-done | bytes 344096 | tf_op jit(solution)/shard_map/ppermute | solution.py:60
  268.5 5.3 collective-permute-done.64
  276.3 6.8 collective-permute-done.66
  306.1 16.0 %collective-permute-done.67 = bf16[2,4,96,384]{3,2,1,0:T(8,128)(2,1)} collective-permute-done((bf16[2,4,96,384]{3,2,1,0:T(8,128)(2,1)}, bf16[2,4,96,384]{3,2,1,0:T(8,128)(2,1)}, u32[]{:S(2)}, u32[]{:S(2)}) %collective-permute-start.67) | collective-permute-done | bytes 589856 | tf_op jit(solution)/shard_map/ppermute | solution.py:60
  326.3 7.2 collective-permute-done.73
  343.5 13.9 %select_reduce_fusion.1 = (f32[3072]{0:T(1024)S(1)}, f32[3072,1664]{0,1:T(8,128)}) fusion(pred[1664]{0:T(1024)(128)(4,1)S(1)} %copy-done.145, bf16[3072,768]{1,0:T(8,128)(2,1)S(1)} %bitcast.825, bf16[192,1664]{1,0:T(8,128)(2,1)S(1)} %get-tuple-element.113, bf16[192,1664]{1,0:T(8,128)(2,1)S(1)} %copy-done.103, bf16[192,1664]{1,0:T(8,128)(2,1)S(1)} %copy-done.104, ...), kind=kOutput, calls=%fused_computation.6 | convolution fusion | flops 7872181248 | bytes 27735680 | tf_op jit(solution)/shard_map/dot_general | solution.py:515
  357.4 12.5 %exponential_reduce_fusion = (f32[3072]{0:T(1024)S(1)}, f32[3072]{0:T(1024)S(1)}) fusion(f32[3072,1664]{0,1:T(8,128)} %get-tuple-element.333, f32[3072]{0:T(1024)S(1)} %get-tuple-element.332, pred[1664]{0:T(1024)(128)(4,1)S(1)} %copy-done.145, s32[3072]{0:T(1024)S(1)} %sub.321), kind=kLoop, calls=%fused_computation.4 | loop fusion | flops 35776512 | bytes 20498048 | tf_op jit(solution)/shard_map/reduce_sum | solution.py:521
  387.3 11.9 %multiply_convert_fusion = bf16[3072,1664]{0,1:T(8,128)(2,1)S(1)} fusion(f32[3072,1664]{0,1:T(8,128)} %get-tuple-element.333, f32[3072]{0:T(1024)S(1)} %bitcast.858, s32[3072]{0:T(1024)S(1)} %sub.321, f32[3072]{0:T(1024)S(1)} %div.224, pred[1664]{0:T(1024)(128)(4,1)S(1)} %copy-done.145), kind=kLoop, calls=%fused_computation.1 | loop fusion | flops 40894464 | bytes 30709376 | tf_op jit(solution)/shard_map/convert_element_type | solution.py:533
  399.2 9.6 %convolution_convert_fusion = bf16[3072,768]{1,0:T(8,128)(2,1)S(1)} fusion(bf16[3072,1664]{0,1:T(8,128)(2,1)S(1)} %multiply_convert_fusion, bf16[192,1664]{1,0:T(8,128)(2,1)S(1)} %copy-done.102, bf16[192,1664]{1,0:T(8,128)(2,1)S(1)} %copy-done.103, bf16[192,1664]{1,0:T(8,128)(2,1)S(1)} %copy-done.104, bf16[192,1664]{1,0:T(8,128)(2,1)S(1)} %copy-done.100), kind=kOutput, calls=%fused_computation.12 | convolution fusion | flops 7864320000 | bytes 17498112 | tf_op jit(solution)/shard_map/dot_general | solution.py:159
  422.0 12.0 %convolution_convert_fusion.5 = bf16[768,1664]{1,0:T(8,128)(2,1)} fusion(bf16[3072,768]{1,0:T(8,128)(2,1)} %bitcast.826, bf16[3072,1664]{0,1:T(8,128)(2,1)S(1)} %copy-done.13), kind=kOutput, calls=%fused_computation.43 | convolution fusion | flops 7853015040 | bytes 17498112 | tf_op jit(solution)/shard_map/dot_general | solution.py:153
  441.6 8.7 %collective-permute-done.85 = bf16[2,4,96,384]{3,2,1,0:T(8,128)(2,1)S(1)} collective-permute-done((bf16[2,4,96,384]{3,2,1,0:T(8,128)(2,1)S(1)}, bf16[2,4,96,384]{3,2,1,0:T(8,128)(2,1)S(1)}, u32[]{:S(2)}, u32[]{:S(2)}) %collective-permute-start.85) | collective-permute-done | bytes 589856 | tf_op jit(solution)/shard_map/ppermute | solution.py:60
  451.3 12.9 %collective-permute-done.104 = bf16[192,1664]{1,0:T(8,128)(2,1)S(1)} collective-permute-done((bf16[192,1664]{1,0:T(8,128)(2,1)S(1)}, bf16[192,1664]{1,0:T(8,128)(2,1)S(1)}, u32[]{:S(2)}, u32[]{:S(2)}) %collective-permute-start.104) | collective-permute-done | bytes 639008 | tf_op jit(solution)/shard_map/ppermute | solution.py:60
  469.0 8.8 %collective-permute-done.106 = bf16[192,1664]{1,0:T(8,128)(2,1)S(1)} collective-permute-done((bf16[192,1664]{1,0:T(8,128)(2,1)S(1)}, bf16[192,1664]{1,0:T(8,128)(2,1)S(1)}, u32[]{:S(2)}, u32[]{:S(2)}) %collective-permute-start.106) | collective-permute-done | bytes 639008 | tf_op jit(solution)/shard_map/ppermute | solution.py:60
  492.1 7.0 collective-permute-done.88
  569.7 9.0 %collective-permute-done.93 = bf16[4,224,192]{1,2,0:T(8,128)(2,1)S(1)} collective-permute-done((bf16[4,224,192]{1,2,0:T(8,128)(2,1)S(1)}, bf16[4,224,192]{1,2,0:T(8,128)(2,1)S(1)}, u32[]{:S(2)}, u32[]{:S(2)}) %collective-permute-start.93) | collective-permute-done | bytes 344096 | tf_op jit(solution)/shard_map/ppermute | solution.py:60
  578.7 20.1 %collective-permute-done.94 = bf16[4,224,192]{1,2,0:T(8,128)(2,1)S(1)} collective-permute-done((bf16[4,224,192]{1,2,0:T(8,128)(2,1)S(1)}, bf16[4,224,192]{1,2,0:T(8,128)(2,1)S(1)}, u32[]{:S(2)}, u32[]{:S(2)}) %collective-permute-start.94) | collective-permute-done | bytes 344096 | tf_op jit(solution)/shard_map/ppermute | solution.py:60
  638.3 9.1 %copy.329 = f32[4,4,2,224,192]{4,3,2,1,0:T(8,128)} copy(f32[4,4,2,224,192]{3,4,0,1,2:T(8,128)} %convert_bitcast_fusion) | data formatting | bytes 11010048 | tf_op jit(solution)/shard_map/convert_element_type | solution.py:564
  647.3 15.7 %shard_map.527 = f32[192,6288]{1,0:T(8,128)} custom-call(s32[32]{0:T(128)} %copy-done.173, s32[32]{0:T(128)} %max.60.last_ref, s32[1]{0:T(128)} %bitcast.17.base_ref, s32[7168]{0:T(1024)} %reshape.581.ids_ref, f32[7168,192]{1,0:T(8,128)} %bitcast.793), custom_call_target="tpu_custom_call" | custom-call | tf_op jit(solution)/shard_map/pallas_call | solution.py:235
  694.0 5.7 collective-permute-done.113
  710.8 5.4 collective-permute-done.134
  730.2 6.7 collective-permute-start.136
  736.9 5.8 collective-permute-done.129
  764.6 12.8 %fusion.8 = (f32[6288,192]{0,1:T(8,128)}, f32[192,6288]{1,0:T(8,128)}, f32[6288,192]{0,1:T(8,128)}) fusion(f32[6288,192]{0,1:T(8,128)} %param.53, f32[6288,192]{0,1:T(8,128)} %param.44, f32[]{:T(128)S(6)} %min.32, f32[192,6288]{1,0:T(8,128)} %shard_map.527, f32[192]{0:T(256)S(1)} %dynamic_slice.352, pred[6288]{0:T(1024)(128)(4,1)S(1)} %copy-done.138, ...), kind=kLoop, calls=%fused_computation.21 | loop fusion | flops 13280256 | bytes 33811348 | tf_op jit(solution)/shard_map/transpose | solution.py:626
  778.0 8.7 %add_multiply_fusion = (f32[192,6288]{1,0:T(8,128)}, f32[192,6288]{1,0:T(8,128)}, f32[192,6288]{1,0:T(8,128)}) fusion(f32[192,6288]{1,0:T(8,128)} %param.54, f32[192,6288]{1,0:T(8,128)S(1)} %bitcast.797, f32[]{:T(128)S(6)} %min.32, bf16[192,1664]{1,0:T(8,128)(2,1)S(1)} %copy-done.24, bf16[192,1664]{1,0:T(8,128)(2,1)S(1)} %copy-done.26, ...), kind=kLoop, calls=%fused_computation.24 | loop fusion | flops 20524032 | bytes 31531012 | tf_op jit(solution)/shard_map/add | solution.py:374
  (1043 shorter events, 473.7 us)
Async XLA Ops:
  37.5 39.9 %collective-permute-start.21 = (bf16[192,128]{1,0:T(8,128)(2,1)}, bf16[192,128]{1,0:T(8,128)(2,1)}, u32[]{:S(2)}, u32[]{:S(2)}) collective-permute-start(bf16[192,128]{1,0:T(8,128)(2,1)} %convert_bitcast_fusion.1), channel_id=1, source_target_pairs={{0,6},{1,7},{2,4},{3,5},{4,2},{5,3},{6,0},{7,1},{8,14},{9,15},{10,... | collective-permute-start | bytes 147464 | tf_op jit(solution)/shard_map/ppermute | solution.py:60
  41.2 37.6 %collective-permute-start.22 = (bf16[192,128]{1,0:T(8,128)(2,1)}, bf16[192,128]{1,0:T(8,128)(2,1)}, u32[]{:S(2)}, u32[]{:S(2)}) collective-permute-start(bf16[192,128]{1,0:T(8,128)(2,1)} %convert_bitcast_fusion.1), channel_id=1, source_target_pairs={{0,4},{1,5},{2,6},{3,7},{4,0},{5,1},{6,2},{7,3},{8,12},{9,13},{10,... | collective-permute-start | bytes 147464 | tf_op jit(solution)/shard_map/ppermute | solution.py:60
  41.3 26.1 %collective-permute-start.36 = (bf16[24,768]{1,0:T(8,128)(2,1)}, bf16[24,768]{1,0:T(8,128)(2,1)}, u32[]{:S(2)}, u32[]{:S(2)}) collective-permute-start(bf16[24,768]{1,0:T(8,128)(2,1)} %convert_element_type.559), channel_id=1, source_target_pairs={{0,6},{1,7},{2,4},{3,5},{4,2},{5,3},{6,0},{7,1},{8,14},{9,15},{10,... | collective-permute-start | bytes 110600 | tf_op jit(solution)/shard_map/ppermute | solution.py:60
  42.9 27.0 %collective-permute-start.37 = (bf16[24,768]{1,0:T(8,128)(2,1)}, bf16[24,768]{1,0:T(8,128)(2,1)}, u32[]{:S(2)}, u32[]{:S(2)}) collective-permute-start(bf16[24,768]{1,0:T(8,128)(2,1)} %convert_element_type.559), channel_id=1, source_target_pairs={{0,4},{1,5},{2,6},{3,7},{4,0},{5,1},{6,2},{7,3},{8,12},{9,13},{10,... | collective-permute-start | bytes 110600 | tf_op jit(solution)/shard_map/ppermute | solution.py:60
  104.9 83.0 %collective-permute-start.14 = (bf16[4,4,224,192]{2,3,1,0:T(8,128)(2,1)}, bf16[4,4,224,192]{2,3,1,0:T(8,128)(2,1)}, u32[]{:S(2)}, u32[]{:S(2)}) collective-permute-start(bf16[4,4,224,192]{2,3,1,0:T(8,128)(2,1)} %bitcast.35), channel_id=1, source_target_pairs={{0,1},{1,0},{2,3},{3,2},{4,5},{5,4},{6,7},{7,6},{8,9},{9,8},{10,11... | collective-permute-start | bytes 4128776 | tf_op jit(solution)/shard_map/ppermute | solution.py:60
  153.5 31.4 %collective-permute-start.49 = (bf16[2,4,24,1536]{3,2,1,0:T(8,128)(2,1)S(1)}, bf16[2,4,24,1536]{3,2,1,0:T(8,128)(2,1)S(1)}, u32[]{:S(2)}, u32[]{:S(2)}) collective-permute-start(bf16[2,4,24,1536]{3,2,1,0:T(8,128)(2,1)S(1)} %pad_maximum_fusion.17), channel_id=1, source_target_pairs={{0,16},{1,17},{2,18},{3,19},{4,20},{5,21},{6,22},{7,23},{8,24},{9,... | collective-permute-start | bytes 1769480 | tf_op jit(solution)/shard_map/ppermute | solution.py:60
  184.9 63.1 %collective-permute-start.53 = (bf16[2,2,4,24,1536]{4,3,2,1,0:T(8,128)(2,1)}, bf16[2,2,4,24,1536]{4,3,2,1,0:T(8,128)(2,1)}, u32[]{:S(2)}, u32[]{:S(2)}) collective-permute-start(bf16[2,2,4,24,1536]{4,3,2,1,0:T(8,128)(2,1)} %maximum_bitcast_fusion), channel_id=1, source_target_pairs={{0,1},{1,0},{2,3},{3,2},{4,5},{5,4},{6,7},{7,6},{8,9},{9,8},{10,11... | collective-permute-start | bytes 3538952 | tf_op jit(solution)/shard_map/ppermute | solution.py:60
  188.0 63.4 %collective-permute-start.50 = (bf16[2,2,4,24,1536]{4,3,2,1,0:T(8,128)(2,1)}, bf16[2,2,4,24,1536]{4,3,2,1,0:T(8,128)(2,1)}, u32[]{:S(2)}, u32[]{:S(2)}) collective-permute-start(bf16[2,2,4,24,1536]{4,3,2,1,0:T(8,128)(2,1)} %pad_maximum_fusion.9), channel_id=1, source_target_pairs={{0,1},{1,0},{2,3},{3,2},{4,5},{5,4},{6,7},{7,6},{8,9},{9,8},{10,11... | collective-permute-start | bytes 3538952 | tf_op jit(solution)/shard_map/ppermute | solution.py:60
  194.0 31.6 %collective-permute-start.16 = (bf16[4,224,192]{1,2,0:T(8,128)(2,1)S(1)}, bf16[4,224,192]{1,2,0:T(8,128)(2,1)S(1)}, u32[]{:S(2)}, u32[]{:S(2)}) collective-permute-start(bf16[4,224,192]{1,2,0:T(8,128)(2,1)S(1)} %get-tuple-element.157), channel_id=1, source_target_pairs={{0,4},{1,5},{2,6},{3,7},{4,0},{5,1},{6,2},{7,3},{8,12},{9,13},{10,... | collective-permute-start | bytes 1032200 | tf_op jit(solution)/shard_map/ppermute | solution.py:60
  194.3 31.3 %collective-permute-start.15 = (bf16[4,224,192]{1,2,0:T(8,128)(2,1)S(1)}, bf16[4,224,192]{1,2,0:T(8,128)(2,1)S(1)}, u32[]{:S(2)}, u32[]{:S(2)}) collective-permute-start(bf16[4,224,192]{1,2,0:T(8,128)(2,1)S(1)} %get-tuple-element.155), channel_id=1, source_target_pairs={{0,2},{1,3},{2,0},{3,1},{4,6},{5,7},{6,4},{7,5},{8,10},{9,11},{10,... | collective-permute-start | bytes 1032200 | tf_op jit(solution)/shard_map/ppermute | solution.py:60
  291.9 30.3 %collective-permute-start.67 = (bf16[2,4,96,384]{3,2,1,0:T(8,128)(2,1)}, bf16[2,4,96,384]{3,2,1,0:T(8,128)(2,1)}, u32[]{:S(2)}, u32[]{:S(2)}) collective-permute-start(bf16[2,4,96,384]{3,2,1,0:T(8,128)(2,1)} %pad_maximum_fusion.23), channel_id=1, source_target_pairs={{0,16},{1,17},{2,18},{3,19},{4,20},{5,21},{6,22},{7,23},{8,24},{9,... | collective-permute-start | bytes 1769480 | tf_op jit(solution)/shard_map/ppermute | solution.py:60
  294.5 31.8 %collective-permute-start.72 = (bf16[192,1664]{1,0:T(8,128)(2,1)}, bf16[192,1664]{1,0:T(8,128)(2,1)}, u32[]{:S(2)}, u32[]{:S(2)}) collective-permute-start(bf16[192,1664]{1,0:T(8,128)(2,1)} %get-tuple-element.125), channel_id=1, source_target_pairs={{0,24},{1,25},{2,26},{3,27},{4,28},{5,29},{6,30},{7,31},{8,16},{9,... | collective-permute-start | bytes 1916936 | tf_op jit(solution)/shard_map/ppermute | solution.py:60
  296.3 37.2 %collective-permute-start.73 = (bf16[192,1664]{1,0:T(8,128)(2,1)}, bf16[192,1664]{1,0:T(8,128)(2,1)}, u32[]{:S(2)}, u32[]{:S(2)}) collective-permute-start(bf16[192,1664]{1,0:T(8,128)(2,1)} %get-tuple-element.126), channel_id=1, source_target_pairs={{0,16},{1,17},{2,18},{3,19},{4,20},{5,21},{6,22},{7,23},{8,24},{9,... | collective-permute-start | bytes 1916936 | tf_op jit(solution)/shard_map/ppermute | solution.py:60
  296.8 36.6 %collective-permute-start.74 = (bf16[192,1664]{1,0:T(8,128)(2,1)}, bf16[192,1664]{1,0:T(8,128)(2,1)}, u32[]{:S(2)}, u32[]{:S(2)}) collective-permute-start(bf16[192,1664]{1,0:T(8,128)(2,1)} %get-tuple-element.127), channel_id=1, source_target_pairs={{0,8},{1,9},{2,10},{3,11},{4,12},{5,13},{6,14},{7,15},{8,0},{9,1},... | collective-permute-start | bytes 1916936 | tf_op jit(solution)/shard_map/ppermute | solution.py:60
  306.1 30.7 %collective-permute-start.71 = (bf16[2,2,4,96,384]{4,3,2,1,0:T(8,128)(2,1)}, bf16[2,2,4,96,384]{4,3,2,1,0:T(8,128)(2,1)}, u32[]{:S(2)}, u32[]{:S(2)}) collective-permute-start(bf16[2,2,4,96,384]{4,3,2,1,0:T(8,128)(2,1)} %copy.318), channel_id=1, source_target_pairs={{0,1},{1,0},{2,3},{3,2},{4,5},{5,4},{6,7},{7,6},{8,9},{9,8},{10,11... | collective-permute-start | bytes 3538952 | tf_op jit(solution)/shard_map/ppermute | solution.py:60
  436.4 27.8 %collective-permute-start.104 = (bf16[192,1664]{1,0:T(8,128)(2,1)S(1)}, bf16[192,1664]{1,0:T(8,128)(2,1)S(1)}, u32[]{:S(2)}, u32[]{:S(2)}) collective-permute-start(bf16[192,1664]{1,0:T(8,128)(2,1)S(1)} %get-tuple-element.122), channel_id=1, source_target_pairs={{0,24},{1,25},{2,26},{3,27},{4,28},{5,29},{6,30},{7,31},{8,16},{9,... | collective-permute-start | bytes 1916936 | tf_op jit(solution)/shard_map/ppermute | solution.py:60
  438.0 31.0 %collective-permute-start.105 = (bf16[192,1664]{1,0:T(8,128)(2,1)S(1)}, bf16[192,1664]{1,0:T(8,128)(2,1)S(1)}, u32[]{:S(2)}, u32[]{:S(2)}) collective-permute-start(bf16[192,1664]{1,0:T(8,128)(2,1)S(1)} %get-tuple-element.124), channel_id=1, source_target_pairs={{0,16},{1,17},{2,18},{3,19},{4,20},{5,21},{6,22},{7,23},{8,24},{9,... | collective-permute-start | bytes 1916936 | tf_op jit(solution)/shard_map/ppermute | solution.py:60
  439.3 38.4 %collective-permute-start.106 = (bf16[192,1664]{1,0:T(8,128)(2,1)S(1)}, bf16[192,1664]{1,0:T(8,128)(2,1)S(1)}, u32[]{:S(2)}, u32[]{:S(2)}) collective-permute-start(bf16[192,1664]{1,0:T(8,128)(2,1)S(1)} %get-tuple-element.123), channel_id=1, source_target_pairs={{0,8},{1,9},{2,10},{3,11},{4,12},{5,13},{6,14},{7,15},{8,0},{9,1},... | collective-permute-start | bytes 1916936 | tf_op jit(solution)/shard_map/ppermute | solution.py:60
  440.1 43.1 %collective-permute-start.84 = (bf16[4,96,384]{2,1,0:T(8,128)(2,1)S(1)}, bf16[4,96,384]{2,1,0:T(8,128)(2,1)S(1)}, u32[]{:S(2)}, u32[]{:S(2)}) collective-permute-start(bf16[4,96,384]{2,1,0:T(8,128)(2,1)S(1)} %dynamic-slice_bitcast_fusion.20), channel_id=1, source_target_pairs={{0,8},{1,9},{2,10},{3,11},{4,12},{5,13},{6,14},{7,15},{8,0},{9,1},... | collective-permute-start | bytes 884744 | tf_op jit(solution)/shard_map/ppermute | solution.py:60
  450.5 32.8 %collective-permute-start.86 = (bf16[4,96,384]{2,1,0:T(8,128)(2,1)S(1)}, bf16[4,96,384]{2,1,0:T(8,128)(2,1)S(1)}, u32[]{:S(2)}, u32[]{:S(2)}) collective-permute-start(bf16[4,96,384]{2,1,0:T(8,128)(2,1)S(1)} %dynamic-slice_bitcast_fusion.19), channel_id=1, source_target_pairs={{0,16},{1,17},{2,18},{3,19},{4,20},{5,21},{6,22},{7,23},{8,24},{9,... | collective-permute-start | bytes 884744 | tf_op jit(solution)/shard_map/ppermute | solution.py:60
  520.9 33.0 %collective-permute-start.97 = (f32[80,128]{1,0:T(8,128)}, f32[80,128]{1,0:T(8,128)}, u32[]{:S(2)}, u32[]{:S(2)}) collective-permute-start(f32[80,128]{1,0:T(8,128)} %pad_bitcast_fusion), channel_id=1, source_target_pairs={{0,6},{1,7},{2,4},{3,5},{4,2},{5,3},{6,0},{7,1},{8,14},{9,15},{10,... | collective-permute-start | bytes 122888 | tf_op jit(solution)/shard_map/ppermute | solution.py:60
  522.6 32.8 %collective-permute-start.98 = (f32[80,128]{1,0:T(8,128)}, f32[80,128]{1,0:T(8,128)}, u32[]{:S(2)}, u32[]{:S(2)}) collective-permute-start(f32[80,128]{1,0:T(8,128)} %pad_bitcast_fusion), channel_id=1, source_target_pairs={{0,4},{1,5},{2,6},{3,7},{4,0},{5,1},{6,2},{7,3},{8,12},{9,13},{10,... | collective-permute-start | bytes 122888 | tf_op jit(solution)/shard_map/ppermute | solution.py:60
  522.6 32.8 %collective-permute-start.99 = (f32[80,128]{1,0:T(8,128)}, f32[80,128]{1,0:T(8,128)}, u32[]{:S(2)}, u32[]{:S(2)}) collective-permute-start(f32[80,128]{1,0:T(8,128)} %pad_bitcast_fusion), channel_id=1, source_target_pairs={{0,2},{1,3},{2,0},{3,1},{4,6},{5,7},{6,4},{7,5},{8,10},{9,11},{10,... | collective-permute-start | bytes 122888 | tf_op jit(solution)/shard_map/ppermute | solution.py:60
  555.3 71.4 %collective-permute-start.107 = (bf16[2,2,4,24,2304]{4,3,2,0,1:T(8,128)(2,1)}, bf16[2,2,4,24,2304]{4,3,2,0,1:T(8,128)(2,1)}, u32[]{:S(2)}, u32[]{:S(2)}) collective-permute-start(bf16[2,2,4,24,2304]{4,3,2,0,1:T(8,128)(2,1)} %bitcast.788), channel_id=1, source_target_pairs={{0,1},{1,0},{2,3},{3,2},{4,5},{5,4},{6,7},{7,6},{8,9},{9,8},{10,11... | collective-permute-start | bytes 5308424 | tf_op jit(solution)/shard_map/ppermute | solution.py:60
  555.3 43.8 %collective-permute-start.115 = (bf16[2,2,4,24,768]{4,3,2,0,1:T(8,128)(2,1)S(1)}, bf16[2,2,4,24,768]{4,3,2,0,1:T(8,128)(2,1)S(1)}, u32[]{:S(2)}, u32[]{:S(2)}) collective-permute-start(bf16[2,2,4,24,768]{4,3,2,0,1:T(8,128)(2,1)S(1)} %bitcast.846), channel_id=1, source_target_pairs={{0,1},{1,0},{2,3},{3,2},{4,5},{5,4},{6,7},{7,6},{8,9},{9,8},{10,11... | collective-permute-start | bytes 1769480 | tf_op jit(solution)/shard_map/ppermute | solution.py:60
  567.3 31.5 %collective-permute-start.94 = (bf16[4,224,192]{1,2,0:T(8,128)(2,1)S(1)}, bf16[4,224,192]{1,2,0:T(8,128)(2,1)S(1)}, u32[]{:S(2)}, u32[]{:S(2)}) collective-permute-start(bf16[4,224,192]{1,2,0:T(8,128)(2,1)S(1)} %pad_maximum_fusion.31), channel_id=1, source_target_pairs={{0,4},{1,5},{2,6},{3,7},{4,0},{5,1},{6,2},{7,3},{8,12},{9,13},{10,... | collective-permute-start | bytes 1032200 | tf_op jit(solution)/shard_map/ppermute | solution.py:60
  567.5 31.3 %collective-permute-start.95 = (bf16[4,224,192]{1,2,0:T(8,128)(2,1)S(1)}, bf16[4,224,192]{1,2,0:T(8,128)(2,1)S(1)}, u32[]{:S(2)}, u32[]{:S(2)}) collective-permute-start(bf16[4,224,192]{1,2,0:T(8,128)(2,1)S(1)} %pad_maximum_fusion.31), channel_id=1, source_target_pairs={{0,2},{1,3},{2,0},{3,1},{4,6},{5,7},{6,4},{7,5},{8,10},{9,11},{10,... | collective-permute-start | bytes 1032200 | tf_op jit(solution)/shard_map/ppermute | solution.py:60
  578.7 40.5 %collective-permute-start.103 = (f32[4,4,80,128]{3,2,1,0:T(8,128)S(1)}, f32[4,4,80,128]{3,2,1,0:T(8,128)S(1)}, u32[]{:S(2)}, u32[]{:S(2)}) collective-permute-start(f32[4,4,80,128]{3,2,1,0:T(8,128)S(1)} %pad_maximum_fusion.14), channel_id=1, source_target_pairs={{0,1},{1,0},{2,3},{3,2},{4,5},{5,4},{6,7},{7,6},{8,9},{9,8},{10,11... | collective-permute-start | bytes 1966088 | tf_op jit(solution)/shard_map/ppermute | solution.py:60
  616.7 58.8 %collective-permute-start.123 = (bf16[2,2,4,24,3072]{4,3,2,0,1:T(8,128)(2,1)}, bf16[2,2,4,24,3072]{4,3,2,0,1:T(8,128)(2,1)}, u32[]{:S(2)}, u32[]{:S(2)}) collective-permute-start(bf16[2,2,4,24,3072]{4,3,2,0,1:T(8,128)(2,1)} %bitcast.787), channel_id=1, source_target_pairs={{0,1},{1,0},{2,3},{3,2},{4,5},{5,4},{6,7},{7,6},{8,9},{9,8},{10,11... | collective-permute-start | bytes 7077896 | tf_op jit(solution)/shard_map/ppermute | solution.py:60
  617.4 64.7 %collective-permute-start.131 = (bf16[2,2,4,96,768]{4,3,2,0,1:T(8,128)(2,1)}, bf16[2,2,4,96,768]{4,3,2,0,1:T(8,128)(2,1)}, u32[]{:S(2)}, u32[]{:S(2)}) collective-permute-start(bf16[2,2,4,96,768]{4,3,2,0,1:T(8,128)(2,1)} %bitcast.786), channel_id=1, source_target_pairs={{0,1},{1,0},{2,3},{3,2},{4,5},{5,4},{6,7},{7,6},{8,9},{9,8},{10,11... | collective-permute-start | bytes 7077896 | tf_op jit(solution)/shard_map/ppermute | solution.py:60
  630.2 40.5 %collective-permute-start.108 = (bf16[2,4,24,1152]{3,2,1,0:T(8,128)(2,1)}, bf16[2,4,24,1152]{3,2,1,0:T(8,128)(2,1)}, u32[]{:S(2)}, u32[]{:S(2)}) collective-permute-start(bf16[2,4,24,1152]{3,2,1,0:T(8,128)(2,1)} %dynamic-slice_bitcast_fusion.11), channel_id=1, source_target_pairs={{0,16},{1,17},{2,18},{3,19},{4,20},{5,21},{6,22},{7,23},{8,24},{9,... | collective-permute-start | bytes 1327112 | tf_op jit(solution)/shard_map/ppermute | solution.py:60
  631.8 41.3 %collective-permute-start.110 = (bf16[2,4,24,1152]{3,2,1,0:T(8,128)(2,1)}, bf16[2,4,24,1152]{3,2,1,0:T(8,128)(2,1)}, u32[]{:S(2)}, u32[]{:S(2)}) collective-permute-start(bf16[2,4,24,1152]{3,2,1,0:T(8,128)(2,1)} %dynamic-slice_bitcast_fusion.10), channel_id=1, source_target_pairs={{0,8},{1,9},{2,10},{3,11},{4,12},{5,13},{6,14},{7,15},{8,0},{9,1},... | collective-permute-start | bytes 1327112 | tf_op jit(solution)/shard_map/ppermute | solution.py:60
  (321 other events, 3641.4 us)

commit v2 on v1

v2 whole, which is shorter than its diff:
```python
import functools

import jax
import jax.numpy as jnp
from jax import lax
from jax.experimental import pallas as pl
from jax.experimental.pallas import tpu as pltpu
from jax.sharding import PartitionSpec as P

HEAD_DIM = 64
VOCAB = 50258
FREQ = 256
FEWEST_MASKED = 32
LANES = 128


norm_epsilon = 1e-06
weight_cap = 20.0
clip_level = 1.0
learn_rate = 30.0
embed_rate = 2000.0
momentum_rate = 0.9
average_rate = 0.5
highest = lax.Precision.HIGHEST
low = jnp.bfloat16
wide = jnp.float32


def tie(*values):
    return lax.optimization_barrier(values)


class Links:
    def __init__(self, dp_count, vocab_count):
        core = 2 if vocab_count % 2 == 0 else 1
        side = 1
        while side * side < dp_count:
            side *= 2
        self.dp_count, self.vocab_count = dp_count, vocab_count
        self.axes = {
            "u": ("dp", side, dp_count // side),
            "v": ("dp", 1, side),
            "z": ("vocab", core, vocab_count // core),
            "c": ("vocab", 1, core),
            "dp": ("dp", 1, dp_count),
        }

    def size(self, axis):
        return self.axes[axis][2]

    def place(self, axis):
        group, unit, size = self.axes[axis]
        return (lax.axis_index(group) // unit) % size

    def hop(self, value, axis, step):
        group, unit, _ = self.axes[axis]
        flip = step * unit
        across, along = (flip, 0) if group == "dp" else (0, flip)
        pairs = [
            (d * self.vocab_count + w, (d ^ across) * self.vocab_count + (w ^ along))
            for d in range(self.dp_count)
            for w in range(self.vocab_count)
        ]
        return lax.ppermute(value, ("dp", "vocab"), pairs)

    def heard(self, value, axis):
        return [value] + [self.hop(value, axis, k) for k in range(1, self.size(axis))]

    def ordered(self, pieces, axis):
        place, count = self.place(axis), len(pieces)
        slots = []
        for slot in range(count):
            value = pieces[slot]
            for other in range(1, count):
                value = jnp.where(place == other, pieces[slot ^ other], value)
            slots.append(value)
        return slots

    def near(self, value, axis):
        return [value[0]] + [self.hop(value[k], axis, k) for k in range(1, self.size(axis))]

    def piled(self, pieces, axis, dim=0):
        return jnp.stack(self.ordered(pieces, axis), dim)

    def own(self, value, axis, dim=0):
        return lax.dynamic_index_in_dim(value, self.place(axis), dim, keepdims=False)

    def given(self, value, axis, dim=0):
        place = self.place(axis)
        return [
            self.hop(lax.dynamic_index_in_dim(value, place ^ k, dim, keepdims=False), axis, k)
            for k in range(1, self.size(axis))
        ]

    def slot(self, n, place):
        step = n ^ place
        along = self.size("v")
        return (step % along) * self.size("u") + step // along

    def exchange(self, value):
        value = value.reshape((self.size("v"), self.size("u")) + value.shape[1:])
        return self.near(value, "v")

    def exchanged(self, came):
        pieces = [piece[0] for piece in came]
        for step in range(1, self.size("u")):
            further = self.hop(jnp.stack([piece[step] for piece in came]), "u", step)
            pieces += [further[n] for n in range(self.size("v"))]
        return pieces

    def doubled(self, value, axis):
        place, step, shape = self.place(axis), 1, value.shape
        value = value[None]
        while step < self.size(axis):
            came = self.hop(value, axis, step)
            upper = (place // step) % 2 == 1
            value = jnp.concatenate(
                [jnp.where(upper, came, value), jnp.where(upper, value, came)], 0
            )
            step *= 2
        return value.reshape((self.size(axis),) + shape)


    def half(self, value, other=False):
        width = value.shape[-1] // 2
        place = self.place("c")
        place = 1 - place if other else place
        return lax.dynamic_slice_in_dim(value, place * width, width, value.ndim - 1)

    def halves_back(self, mine, other):
        first = self.place("c") == 0
        return jnp.concatenate(
            [jnp.where(first, mine, other), jnp.where(first, other, mine)], -1
        )

    def pair_rows(self, mine, theirs):
        came = self.hop(theirs, "c", 1)
        return self.piled([mine, came], "c").reshape(-1, mine.shape[-1])

    def wide_across(self, pieces):
        block = lax.all_gather(self.piled(pieces, "z"), "dp", axis=0, tiled=False)
        return block.reshape(-1, block.shape[-1])

    def across_first(self, pieces, cut):
        block = self.piled(pieces, "z")
        return self.heard(block[..., :cut], "v"), self.heard(block[..., cut:], "u")

    def across_second(self, sides):
        return self.heard(self.piled(sides[0], "v"), "u"), self.heard(
            self.piled(sides[1], "u"), "v"
        )

    def across_done(self, sides):
        block = jnp.concatenate([self.piled(sides[0], "u"), self.piled(sides[1], "v", 1)], -1)
        return block.reshape(-1, block.shape[-1])


    def summed(self, state):
        return sum([piece.astype(wide) for piece in state[1]], state[0].astype(wide))

    def by_place(self, block):
        return block.reshape(
            self.size("u"), self.size("v"), self.size("z"), -1, block.shape[-1]
        )

    def fold_first(self, block, cut):
        left, right = block[..., :cut], block[..., cut:]
        return [
            (self.own(left, "u", 0), self.given(left, "u", 0)),
            (self.own(right, "v", 1), self.given(right, "v", 1)),
        ]

    def fold_second(self, states):
        left, right = [self.summed(state).astype(low) for state in states]
        return [
            (self.own(left, "v", 0), self.given(left, "v", 0)),
            (self.own(right, "u", 0), self.given(right, "u", 0)),
        ]

    def fold_third(self, states):
        return jnp.concatenate([self.summed(state).astype(low) for state in states], -1)

    def fold_z(self, block):
        return self.own(block, "z"), self.given(block, "z")

    def fold_across(self, block):
        block = block.reshape((self.dp_count,) + block.shape[2:])
        return lax.psum_scatter(block, "dp", scatter_dimension=0, tiled=False)

    def own_rows(self, state):
        block = state
        block = block.reshape(2, -1, block.shape[-1])
        return self.halves_back(self.own(block, "c"), self.given(block, "c")[0])

    def small_done(self, pieces):
        return self.piled(pieces, "c", 2).reshape(self.dp_count * self.vocab_count, -1)

    def total(self, value, join):
        for axis in ("z", "dp", "c"):
            value = join(self.heard(value, axis))
        return value


def half_cut(width):
    return max(LANES, (width // (2 * LANES)) * LANES) if width > LANES else width // 2


def features(level, freq_count):
    sigma_level = -jnp.log1p(-(1.0 - 0.001) * level)
    half_count = freq_count // 2
    frequency = jnp.exp(-jnp.log(10000.0) * jnp.arange(half_count, dtype=wide) / half_count)
    angles = sigma_level[..., None] * frequency
    return jnp.concatenate([jnp.cos(angles), jnp.sin(angles)], -1)


def nelbo_weight(level):
    sigma_level = -jnp.log1p(-(1.0 - 0.001) * level)
    rate_value = (1.0 - 0.001) / (1.0 - (1.0 - 0.001) * level)
    return jnp.minimum(rate_value / jnp.expm1(sigma_level), weight_cap)


def norm_mod(values, gain_row, shift_row, scale_row):
    center = values - jnp.mean(values, -1, keepdims=True)
    spread = jnp.mean(center * center, -1, keepdims=True)
    return center * lax.rsqrt(spread + norm_epsilon) * gain_row * (1.0 + scale_row) + shift_row


def times_rows(left_matrix, right_matrix):
    return lax.dot_general(
        left_matrix, right_matrix, (((0,), (0,)), ((), ())), preferred_element_type=wide
    )


def times_transposed(left_matrix, right_matrix):
    return lax.dot_general(
        left_matrix, right_matrix, (((1,), (1,)), ((), ())), preferred_element_type=wide
    )


def cost(megabytes):
    return pl.CostEstimate(flops=0, transcendentals=0, bytes_accessed=megabytes * 2**20)


def turn_kernel(in_ref, out_ref):
    out_ref[...] = in_ref[...].T


def turned(array):
    rows, columns = array.shape
    block = 8 * LANES
    return pl.pallas_call(
        turn_kernel,
        grid=(-(-columns // block),),
        out_shape=jax.ShapeDtypeStruct((columns, rows), array.dtype),
        in_specs=[pl.BlockSpec((rows, block), lambda i: (0, i))],
        out_specs=pl.BlockSpec((block, rows), lambda i: (i, 0)),
        cost_estimate=cost(24),
    )(array)


def block_of(s, grid, spot_ref):
    dp_count, z_count, core = grid
    along = lax.rem(s, z_count * core)
    across = lax.div(s, z_count * core) ^ spot_ref[0]
    deep = lax.div(along, core) ^ spot_ref[1]
    near = lax.rem(along, core) ^ spot_ref[2]
    return (near * z_count + deep) * dp_count + across


def look_up_kernel(
    grid, spot_ref, first_ref, last_ref, ids_ref, table_ref, mine_ref, theirs_ref, rows_ref, pair_ref
):
    half, width = mine_ref.shape[1], mine_ref.shape[2] // 2
    kept = 2 * half
    rows_ref[...] = jnp.zeros_like(rows_ref)
    base = spot_ref[3]

    def one_sequence(s, carry):
        first, last = first_ref[s], last_ref[s]
        to = block_of(s, grid, spot_ref) * kept

        def some(i, inner):
            places = [jnp.minimum(first + 8 * i + q, last - 1) for q in range(8)]
            found = [table_ref[pl.ds(ids_ref[s, k] - base, 1), :] for k in places]
            for k, row in zip(places, found):
                rows_ref[pl.ds(to + k, 1), :] = row
            return inner

        return lax.fori_loop(0, lax.div(last - first + 7, 8), some, carry)

    lax.fori_loop(0, first_ref.shape[0], one_sequence, 0)
    count = mine_ref.shape[0]
    for n, out_ref in enumerate((mine_ref, theirs_ref)):

        def rounded(b, carry):
            at = pl.multiple_of((n * count + b) * kept, 16)
            pair_ref[:, :width] = rows_ref[pl.ds(at, half), :]
            pair_ref[:, width:] = rows_ref[pl.ds(at + half, half), :]
            out_ref[b] = pair_ref[...].astype(out_ref.dtype)
            return carry

        lax.fori_loop(0, count, rounded, 0)


def fits(count, kept):
    return count * kept <= 16384


def by_steps(values, spot, grid):
    for axis, size in enumerate(grid):
        values = jnp.take(values, jnp.arange(size) ^ spot[axis], axis=axis)
    return values


def owned(first, last, ids):
    place = jnp.arange(ids.shape[1])[None]
    return (place >= first[:, None]) & (place < last[:, None])


def look_up_plain(spot, first, last, ids, table, grid):
    count, kept = ids.shape
    rows = table[jnp.clip(ids - spot[3], 0, table.shape[0] - 1)]
    rows = jnp.where(owned(first, last, ids)[..., None], rows, 0).astype(low)
    rows = jnp.swapaxes(rows.reshape(count, 2, kept // 2, -1), 1, 2).reshape(count, kept // 2, -1)
    rows = by_steps(rows.reshape(grid + rows.shape[1:]), spot, grid)
    rows = rows.transpose(2, 1, 0, 3, 4).reshape((2, count // 2) + rows.shape[3:])
    return rows[0], rows[1]


def add_up_plain(spot, first, last, ids, mine, theirs, span, grid):
    count, kept = ids.shape
    rows = jnp.stack([mine, theirs]).reshape(grid[::-1] + mine.shape[1:])
    rows = by_steps(rows.transpose(2, 1, 0, 3, 4), spot, grid)
    rows = jnp.swapaxes(rows.reshape(count, kept // 2, 2, -1), 1, 2).astype(wide)
    places = jnp.where(owned(first, last, ids), ids - spot[3], span).reshape(-1)
    rows = rows.reshape(count * kept, -1)
    sums = jax.ops.segment_sum(rows, places, num_segments=span + 1)[:span].T
    return sums, jnp.sum(sums * sums, 0, keepdims=True)


def look_up(spot, first, last, ids, table, grid):
    count, kept = ids.shape
    width = 2 * table.shape[1]
    if not fits(count, kept):
        return look_up_plain(spot, first, last, ids, table, grid)
    smem = pl.BlockSpec(memory_space=pltpu.SMEM)
    vmem = pl.BlockSpec(memory_space=pltpu.VMEM)
    out = jax.ShapeDtypeStruct((count // 2, kept // 2, width), low)
    return pl.pallas_call(
        functools.partial(look_up_kernel, grid),
        out_shape=(out, out),
        in_specs=[smem, smem, smem, smem, vmem],
        out_specs=(vmem, vmem),
        scratch_shapes=[
            pltpu.VMEM((count * kept, width // 2), wide),
            pltpu.VMEM((kept // 2, width), wide),
        ],
        compiler_params=pltpu.CompilerParams(vmem_limit_bytes=56 * 2**20),
        cost_estimate=cost(36),
    )(spot, first, last, ids, table)


def add_up_kernel(
    grid,
    spot_ref,
    first_ref,
    last_ref,
    ids_ref,
    mine_ref,
    theirs_ref,
    out_ref,
    square_ref,
    sum_ref,
    wide_ref,
):
    span = out_ref.shape[1]
    sum_ref[...] = jnp.zeros_like(sum_ref)
    base = spot_ref[3]
    half, width, count = mine_ref.shape[1], mine_ref.shape[2] // 2, mine_ref.shape[0]
    kept = 2 * half
    for n, in_ref in enumerate((mine_ref, theirs_ref)):

        def widen(b, carry):
            at = pl.multiple_of((n * count + b) * kept, 16)
            rows = in_ref[b].astype(wide)
            wide_ref[pl.ds(at, half), :] = rows[:, :width]
            wide_ref[pl.ds(at + half, half), :] = rows[:, width:]
            return carry

        lax.fori_loop(0, count, widen, 0)

    def one_sequence(s, carry):
        first, last = first_ref[s], last_ref[s]
        start = block_of(s, grid, spot_ref) * kept

        def some(i, inner):
            places = [first + 8 * i + q for q in range(8)]
            near = [jnp.minimum(k, last - 1) for k in places]
            rows = [
                jnp.where(k < last, ids_ref[s, m] - base, span) for k, m in zip(places, near)
            ]
            parts = [wide_ref[pl.ds(start + m, 1), :] for m in near]
            for row, part in zip(rows, parts):
                sum_ref[pl.ds(row, 1), :] = sum_ref[pl.ds(row, 1), :] + part
            return inner

        return lax.fori_loop(0, lax.div(last - first + 7, 8), some, carry)

    lax.fori_loop(0, first_ref.shape[0], one_sequence, 0)
    whole = span // LANES

    def turn(b, squares):
        at = pl.multiple_of(b * LANES, LANES)
        part = sum_ref[pl.ds(at, LANES), :].T
        out_ref[:, pl.ds(at, LANES)] = part
        return squares + jnp.sum(part * part, 0, keepdims=True)

    squares = lax.fori_loop(0, whole, turn, jnp.zeros((1, LANES), wide))
    if span > whole * LANES:
        rest = span - whole * LANES
        part = sum_ref[whole * LANES : (whole + 1) * LANES, :].T
        out_ref[:, whole * LANES :] = part[:, :rest]
        lane = lax.broadcasted_iota(jnp.int32, part.shape, 1)
        part = jnp.where(lane < rest, part, 0.0)
        squares = squares + jnp.sum(part * part, 0, keepdims=True)
    square_ref[...] = squares


def add_up(spot, first, last, ids, mine, theirs, span, grid):
    count, kept = ids.shape
    if not fits(count, kept):
        return add_up_plain(spot, first, last, ids, mine, theirs, span, grid)
    width = mine.shape[2] // 2
    smem = pl.BlockSpec(memory_space=pltpu.SMEM)
    vmem = pl.BlockSpec(memory_space=pltpu.VMEM)
    padded = (span // LANES + 1) * LANES
    return pl.pallas_call(
        functools.partial(add_up_kernel, grid),
        out_shape=(
            jax.ShapeDtypeStruct((width, span), wide),
            jax.ShapeDtypeStruct((1, LANES), wide),
        ),
        in_specs=[smem, smem, smem, smem, vmem, vmem],
        out_specs=(vmem, vmem),
        scratch_shapes=[
            pltpu.VMEM((padded, width), wide),
            pltpu.VMEM((count * kept, width), wide),
        ],
        compiler_params=pltpu.CompilerParams(vmem_limit_bytes=56 * 2**20),
        cost_estimate=cost(50),
    )(spot, first, last, ids, mine, theirs)


def pack_kernel(core_ref, *refs):
    *in_refs, mine_ref, theirs_ref = refs
    first = core_ref[0] == 0
    at = 0
    rows = mine_ref.shape[0]
    for ref, tall in in_refs_of(in_refs):
        width = ref.shape[1]
        blocks = [(n * rows, (n + 1) * rows) for n in range(ref.shape[0] // rows)]
        if tall:
            sides = [
                [(blocks[n], (0, width)) for n in range(k, k + len(blocks) // 2)]
                for k in (0, len(blocks) // 2)
            ]
        else:
            sides = [
                [(block, (k, k + width // 2)) for block in blocks] for k in (0, width // 2)
            ]
        for left, right in zip(*sides):
            values = [
                ref[row[0] : row[1], column[0] : column[1]] for row, column in (left, right)
            ]
            to = slice(at, at + values[0].shape[1])
            mine_ref[:, to] = jnp.where(first, values[0], values[1]).astype(low)
            theirs_ref[:, to] = jnp.where(first, values[1], values[0]).astype(low)
            at = to.stop


def in_refs_of(refs):
    return [(ref, n == 2) for n, ref in enumerate(refs)]


def packed(core, w_qkv, w_out, ada_turned, w_up, w_down):
    rows = w_up.shape[0]
    arrays = (w_qkv, w_out, ada_turned, w_up, w_down)
    width = sum(array.size for array in arrays) // rows // 2
    out = jax.ShapeDtypeStruct((rows, width), low)
    vmem = pl.BlockSpec(memory_space=pltpu.VMEM)
    return pl.pallas_call(
        pack_kernel,
        out_shape=(out, out),
        in_specs=[pl.BlockSpec(memory_space=pltpu.SMEM)] + [vmem] * 5,
        out_specs=(vmem, vmem),
    )(core, *arrays)


def prepare_kernel(
    mask_id,
    place_ref,
    level_ref,
    clean_ref,
    slots_ref,
    time_ref,
    gains_ref,
    mask_row_ref,
    small_ref,
    first_ref,
    second_ref,
    collect_ref,
    spot_ref,
    alive_ref,
    masked_ref,
):
    length, slots = clean_ref.shape[1], slots_ref.shape[1]
    kept = collect_ref.shape[0]

    def iota(shape, dim):
        return lax.broadcasted_iota(jnp.int32, shape, dim)

    def stood(row):
        size = row.shape[1]
        same = iota((size, size), 0) == iota((size, size), 1)
        return jnp.sum(jnp.where(same, row, 0.0), 1, keepdims=True)

    def laid(column):
        size = column.shape[0]
        same = iota((size, size), 0) == iota((size, size), 1)
        return jnp.sum(jnp.where(same, column, 0.0), 0, keepdims=True)

    clean = clean_ref[...].astype(wide)
    slot = stood(slots_ref[...].astype(wide))
    across = iota((slots, length), 1).astype(wide)
    masked = jnp.sum((across == slot).astype(wide), 0, keepdims=True)
    ids = jnp.where(masked > 0, wide(mask_id), clean)
    key = ids * length + iota((1, length), 1).astype(wide)
    key_column = stood(key)
    rank_column = jnp.sum((key < key_column).astype(wide), 1, keepdims=True)
    rank = jnp.sum((key_column < key).astype(wide), 0, keepdims=True)
    spread = (rank_column == iota((length, kept), 1).astype(wide)).astype(wide)
    half = kept // 2
    first_ref[...] = (rank_column == iota((length, half), 1).astype(wide)).astype(low)
    second_ref[...] = (rank_column == (iota((length, half), 1) + half).astype(wide)).astype(low)
    collect_ref[...] = (rank == iota((kept, length), 0).astype(wide)).astype(low)
    masked_ref[...] = stood(masked)
    at_spot = across == jnp.minimum(slot, length - 1.0)
    spot_ref[...] = at_spot.astype(low)
    alive_ref[...] = (across == slot).astype(low)
    target = jnp.sum(jnp.where(at_spot, clean, 0.0), 1, keepdims=True)
    target = laid(jnp.where(slot < length, target, -1.0))
    small_ref[...] = jnp.zeros_like(small_ref)
    small_ref[0:1, :kept] = jnp.sum(spread * stood(ids), 0, keepdims=True)
    small_ref[1:2, :slots] = target
    small_ref[2:3, :] = jnp.full((1, small_ref.shape[1]), level_ref[place_ref[0]], wide)
    small_ref[3:4, : mask_row_ref.shape[1]] = mask_row_ref[...].astype(low).astype(wide)
    small_ref[4:7, : gains_ref.shape[1]] = gains_ref[...].astype(low).astype(wide)
    small_ref[8 : 8 + time_ref.shape[0], : time_ref.shape[1]] = time_ref[...].astype(low).astype(wide)


def prepare(mask_id, place, level, clean, slots, w_time, gains, mask_row, kept):
    length, slot_count = clean.shape[1], slots.shape[1]
    smem = pl.BlockSpec(memory_space=pltpu.SMEM)
    vmem = pl.BlockSpec(memory_space=pltpu.VMEM)
    rows = 8 + -(-w_time.shape[0] // 8) * 8
    shapes = (
        ((rows, length), wide),
        ((length, kept // 2), low),
        ((length, kept // 2), low),
        ((kept, length), low),
        ((slot_count, length), low),
        ((slot_count, length), low),
        ((length, 1), wide),
    )
    return pl.pallas_call(
        functools.partial(prepare_kernel, mask_id),
        out_shape=tuple(jax.ShapeDtypeStruct(*shape) for shape in shapes),
        in_specs=[smem, smem] + [vmem] * 5,
        out_specs=(vmem,) * len(shapes),
    )(place, level, clean, slots, w_time, gains, mask_row)


def enter_kernel(first_ref, second_ref, masked_ref, mask_row_ref, *refs):
    *piece_refs, out_ref = refs
    width = piece_refs[0].shape[1] // 2
    for n, piece_ref in enumerate(piece_refs):
        at = slice(n * width, (n + 1) * width)
        left = jnp.dot(first_ref[...], piece_ref[...], preferred_element_type=wide)
        right = jnp.dot(second_ref[...], piece_ref[...], preferred_element_type=wide)
        rows = left[:, :width] + right[:, width:]
        out_ref[:, at] = rows + masked_ref[...] * mask_row_ref[:, at]


def enter(first, second, masked, mask_row, pieces):
    width = pieces[0].shape[1] // 2
    return pl.pallas_call(
        enter_kernel,
        out_shape=jax.ShapeDtypeStruct((first.shape[0], width * len(pieces)), wide),
    )(first, second, masked, mask_row[None, :], *pieces)


def tell_kernel(core_ref, sums_1, sums_2, sums_3, ada_ref, hidden_ref, before_ref, out_ref):
    sums_1, sums_2, sums_3 = sums_1[...], sums_2[...], sums_3[...]
    rows = [sums_1[n : n + 1] for n in (1, 2)] + [sums_2[n : n + 1] for n in (3, 1, 2)]
    rows += [sums_3[n : n + 1] for n in (3, 1, 2)]
    which = iota(sums_1.shape, 0)
    mods = jnp.zeros(sums_1.shape, wide)
    for n, row in enumerate(rows):
        mods = jnp.where(which == n, row, mods)
    columns, width = mods.T, mods.shape[1]
    total = jnp.zeros((8, ada_ref.shape[1]), wide)
    for n in range(8):
        part = columns[:, n : n + 1] * ada_ref[n * width : (n + 1) * width, :].astype(wide)
        total = total + jnp.sum(part.reshape(-1, 8, part.shape[1]), 0)
    slope = jnp.sum(total, 0, keepdims=True)
    before = before_ref[...]
    gate = 1.0 / (1.0 + jnp.exp(-before))
    slope = slope * (gate + before * gate * (1.0 - gate))
    out_ref[...] = jnp.zeros_like(out_ref)
    out_ref[0:8, :] = mods
    out_ref[8:12, :] = sums_1[0:4]
    out_ref[12:16, :] = sums_2[0:4]
    out_ref[16:20, :] = sums_3[0:4]
    out_ref[20:21, : slope.shape[1]] = hidden_ref[...]
    out_ref[21:22, : slope.shape[1]] = slope


def tell(sums_1, sums_2, sums_3, ada, hidden_time, before_time):
    (rows,) = kernel_call(
        tell_kernel,
        jnp.zeros((1,), jnp.int32),
        (sums_1, sums_2, sums_3, ada, hidden_time, before_time),
        (((24, sums_1.shape[1]), wide),),
    )
    return rows


def finish_kernel(
    scalar_ref, vectors_ref, spectrum_ref, ada_ref, time_ref, gains_ref, mask_ref, square_ref
):
    device, width = scalar_ref[0], vectors_ref.shape[2]
    size = ada_ref.shape[0]
    row = lax.div(device, width // size)
    mods = vectors_ref[:, 0, :]
    for n in range(1, 8):
        mods = jnp.where(row == n, vectors_ref[:, n, :], mods)

    def chosen(values, at, count):
        place = (iota((width, count), 0) == iota((width, count), 1) + at).astype(wide)
        return jnp.dot(values, place, precision=highest, preferred_element_type=wide)

    def times(left, right):
        return lax.dot_general(
            left,
            right,
            (((0,), (0,)), ((), ())),
            precision=highest,
            preferred_element_type=wide,
        )

    cond = ada_ref.shape[1]
    mods = chosen(mods, lax.rem(device, width // size) * size, size)
    ada_ref[...] = times(mods, vectors_ref[:, 20, :cond])
    time_ref[...] = times(spectrum_ref[...], vectors_ref[:, 21, :cond])
    rows = [jnp.sum(vectors_ref[:, n, :], 0, keepdims=True) for n in (8, 12, 16, 11)]
    which = iota((8, width), 0)
    block = jnp.zeros((8, width), wide)
    for n, values in enumerate(rows):
        block = jnp.where(which == n, values, block)
    gains_ref[...] = chosen(block, device * gains_ref.shape[1], gains_ref.shape[1])[:3]
    mask = chosen(block, scalar_ref[1] * mask_ref.shape[1], mask_ref.shape[1])[3:4]
    mask_ref[...] = mask * scalar_ref[2].astype(wide)
    total = sum(
        jnp.sum(jnp.sum(ref[...] * ref[...], 0, keepdims=True), 1, keepdims=True)
        for ref in (ada_ref, time_ref, gains_ref, mask_ref)
    )
    square_ref[...] = jnp.broadcast_to(total, square_ref.shape)


def finish(scalars, vectors, spectrum, ada_rows, cond, gain_width, mask_width):
    return kernel_call(
        finish_kernel,
        scalars,
        (vectors, spectrum),
        (
            ((ada_rows, cond), wide),
            ((spectrum.shape[1], cond), wide),
            ((3, gain_width), wide),
            ((1, mask_width), wide),
            ((1, LANES), wide),
        ),
    )


def laid_out(block, count, rows, width):
    parts = [
        block[:, at : at + width].reshape(count, 1, rows, width)
        for at in range(0, block.shape[1], width)
    ]
    return jnp.concatenate(parts, 1).reshape(-1, width)


def beside_blocks(block, count, rows):
    width = block.shape[1]
    block = block.reshape(count, -1, rows, width)
    return [block[:, n].reshape(count * rows, width) for n in range(block.shape[1])]


def column_of(info, n):
    return info[:, n : n + 1]


ROW_BLOCK = 256


def split_kernel(columns, place_ref, in_ref, out_ref):
    values = in_ref[...]
    column = lax.broadcasted_iota(jnp.int32, values.shape, 1)
    column = column + pl.program_id(0) * values.shape[1]
    out_ref[0] = jnp.where(column < columns, values, 0.0).astype(out_ref.dtype)


def split_head(links, place, table, piece):
    rows, columns = table.shape
    return pl.pallas_call(
        functools.partial(split_kernel, columns),
        out_shape=jax.ShapeDtypeStruct((links.dp_count, rows, piece), low),
        grid_spec=pltpu.PrefetchScalarGridSpec(
            num_scalar_prefetch=1,
            grid=(links.dp_count,),
            in_specs=[pl.BlockSpec((rows, piece), lambda i, at: (0, i))],
            out_specs=pl.BlockSpec(
                (1, rows, piece), lambda i, at: (links.slot(i, at[0]), 0, 0)
            ),
        ),
        cost_estimate=cost(8),
    )(place, table)


def stood(rows):
    which = lax.broadcasted_iota(jnp.int32, (8, rows[0].shape[1]), 0)
    block = jnp.broadcast_to(rows[0], which.shape)
    for n, row in enumerate(rows[1:]):
        block = jnp.where(which == n + 1, row, block)
    return block.T


def row_place():
    half = pl.num_programs(0) // 2
    return lambda core: lax.rem(pl.program_id(0) + core * half, 2 * half)


def logits_kernel(scalar_ref, mine_ref, theirs_ref, head_ref, info_ref, out_ref, stats_ref):
    is_mine = pl.program_id(0) < pl.num_programs(0) // 2
    block = row_place()(scalar_ref[0])
    limit = scalar_ref[1]
    rows = jnp.where(is_mine, mine_ref[...], theirs_ref[...])
    target = column_of(stood([info_ref[pl.ds(block, 1), :]]), 0).astype(jnp.int32)
    parts = []
    for at in head_parts(head_ref.shape[1]):
        values = jnp.dot(rows, head_ref[:, at], preferred_element_type=wide)
        column = lax.broadcasted_iota(jnp.int32, values.shape, 1) + at.start
        values = jnp.where(column < limit, values, -1e30)
        out_ref[:, at] = values
        found = jnp.sum(jnp.where(column == target, values, 0.0), 1, keepdims=True)
        peak = jnp.max(values, 1, keepdims=True)
        parts.append((peak, jnp.sum(jnp.exp(values - peak), 1, keepdims=True), found))
    peak = functools.reduce(jnp.maximum, [part[0] for part in parts])
    summed = sum(part[1] * jnp.exp(part[0] - peak) for part in parts)
    found = sum(part[2] for part in parts)
    lane = lax.broadcasted_iota(jnp.int32, (peak.shape[0], LANES), 1)
    columns = jnp.where(lane == 0, peak, jnp.where(lane == 1, summed, found)).T
    for n in range(3):
        stats_ref[n, pl.ds(block, 1), :] = columns[n : n + 1]


def head_parts(width):
    size = 4 * LANES
    return [slice(at, min(at + size, width)) for at in range(0, width, size)]


def head_specs(half, rows=ROW_BLOCK):
    by_step = lambda width: pl.BlockSpec((rows, width), lambda i, at: (i, 0))
    mine = lambda width: pl.BlockSpec((rows, width), lambda i, at: (jnp.minimum(i, half - 1), 0))
    theirs = lambda width: pl.BlockSpec((rows, width), lambda i, at: (jnp.maximum(i - half, 0), 0))
    whole = lambda shape: pl.BlockSpec(shape, lambda i, at: (0,) * len(shape))
    return by_step, mine, theirs, whole


def head_call(kernel, half, out_shape, in_specs, out_specs, scratch=(), cost=None):
    return pl.pallas_call(
        kernel,
        out_shape=out_shape,
        grid_spec=pltpu.PrefetchScalarGridSpec(
            num_scalar_prefetch=1,
            grid=(2 * half,),
            in_specs=in_specs,
            out_specs=out_specs,
            scratch_shapes=scratch,
        ),
        compiler_params=pltpu.CompilerParams(vmem_limit_bytes=50 * 2**20),
        cost_estimate=cost,
    )


def head_cost(rows, width, columns):
    return pl.CostEstimate(
        flops=2 * rows * width * columns,
        bytes_accessed=4 * rows * columns,
        transcendentals=rows * columns,
    )


def head_logits(scalars, mine, theirs, head, target):
    count, width = mine.shape
    half, columns = count // ROW_BLOCK, head.shape[1]
    by_step, by_mine, by_theirs, whole = head_specs(half)
    stats = (3, 2 * half, ROW_BLOCK)
    return head_call(
        logits_kernel,
        half,
        (
            jax.ShapeDtypeStruct((2 * count, columns), wide),
            jax.ShapeDtypeStruct(stats, wide),
        ),
        [by_mine(width), by_theirs(width), whole(head.shape), whole(target.shape)],
        (by_step(columns), whole(stats)),
        cost=head_cost(2 * count, width, columns),
    )(scalars, mine, theirs, head, target)


def slopes_kernel(
    scalar_ref, value_ref, head_ref, info_ref, slope_ref, mine_ref, theirs_ref
):
    block = row_place()(scalar_ref[0])
    info = stood([info_ref[n, pl.ds(block, 1), :] for n in range(3)])
    target, total, weight = [column_of(info, n) for n in range(3)]
    target = target.astype(jnp.int32)
    back = 0.0
    for at in head_parts(value_ref.shape[1]):
        values = value_ref[:, at]
        column = lax.broadcasted_iota(jnp.int32, values.shape, 1) + at.start
        odds = jnp.exp(values - total)
        slope = (jnp.where(column == target, odds - 1.0, odds) * weight).astype(low)
        slope_ref[:, at] = slope
        back = back + times_transposed(slope, head_ref[:, at])
    back = back.astype(mine_ref.dtype)
    is_mine = pl.program_id(0) < pl.num_programs(0) // 2

    @pl.when(is_mine)
    def _():
        mine_ref[...] = back

    @pl.when(jnp.logical_not(is_mine))
    def _():
        theirs_ref[...] = back


def head_slopes(scalars, values, head, info):
    count, (width, columns) = values.shape[0] // 2, head.shape
    half = count // ROW_BLOCK
    by_step, by_mine, by_theirs, whole = head_specs(half)
    return head_call(
        slopes_kernel,
        half,
        (
            jax.ShapeDtypeStruct((2 * count, columns), low),
            jax.ShapeDtypeStruct((count, width), low),
            jax.ShapeDtypeStruct((count, width), low),
        ),
        [by_step(columns), whole(head.shape), whole(info.shape)],
        (by_step(columns), by_mine(width), by_theirs(width)),
        cost=head_cost(2 * count, width, columns),
    )(scalars, values, head, info)


def head_grads_kernel(
    links, scalar_ref, mine_ref, theirs_ref, slope_ref, out_ref, square_ref, sum_ref
):
    step = pl.program_id(0)
    rows = jnp.where(step < pl.num_programs(0) // 2, mine_ref[...], theirs_ref[...])

    @pl.when(step == 0)
    def _():
        sum_ref[...] = jnp.zeros_like(sum_ref)

    for at in head_parts(slope_ref.shape[1]):
        sum_ref[:, at] += times_rows(rows, slope_ref[:, at])

    @pl.when(step == pl.num_programs(0) - 1)
    def _():
        size = out_ref.shape[1]
        squares = 0.0
        for n in range(out_ref.shape[0]):
            part = sum_ref[n * size : (n + 1) * size, :].astype(out_ref.dtype)
            out_ref[links.slot(n, scalar_ref[2])] = part
            part = part.astype(wide)
            squares = squares + jnp.sum(part * part, 0, keepdims=True)
        square_ref[...] = squares


def head_grads(links, scalars, mine, theirs, slopes):
    (count, width), columns = mine.shape, slopes.shape[1]
    rows = 3 * ROW_BLOCK if count % (3 * ROW_BLOCK) == 0 else ROW_BLOCK
    by_step, by_mine, by_theirs, whole = head_specs(count // rows, rows)
    out = (links.dp_count, width // links.dp_count, columns)
    return head_call(
        functools.partial(head_grads_kernel, links),
        count // rows,
        (jax.ShapeDtypeStruct(out, low), jax.ShapeDtypeStruct((1, columns), wide)),
        [by_mine(width), by_theirs(width), by_step(columns)],
        (whole(out), whole((1, columns))),
        [pltpu.VMEM((width, columns), wide)],
        head_cost(2 * count, width, columns),
    )(scalars, mine, theirs, slopes)


def iota(shape, dim):
    return lax.broadcasted_iota(jnp.int32, shape, dim)


def as_column(row):
    size = row.shape[1]
    same = iota((size, size), 0) == iota((size, size), 1)
    return jnp.sum(jnp.where(same, row, 0.0), 1, keepdims=True)


def kernel_call(kernel, scalar, arrays, shapes, scratch=(), megabytes=8):
    vmem = pl.BlockSpec(memory_space=pltpu.VMEM)
    out = [jax.ShapeDtypeStruct(*shape) for shape in shapes]
    return pl.pallas_call(
        kernel,
        out_shape=out,
        in_specs=[pl.BlockSpec(memory_space=pltpu.SMEM)] + [vmem] * len(arrays),
        out_specs=[vmem] * len(out),
        scratch_shapes=list(scratch),
        compiler_params=pltpu.CompilerParams(vmem_limit_bytes=50 * 2**20),
        cost_estimate=cost(megabytes),
    )(scalar, *arrays)


def part_of(core_ref, width, other=False):
    core = 1 - core_ref[0] if other else core_ref[0]
    return pl.ds(pl.multiple_of(core * width, LANES), width)


def product(core_ref, left, mine, theirs, out_ref):
    width = mine.shape[1]
    for matrix, other in ((mine, False), (theirs, True)):
        values = jnp.dot(left, matrix, preferred_element_type=wide)
        out_ref[:, part_of(core_ref, width, other)] = values.astype(out_ref.dtype)


def product_back(core_ref, slope_ref, mine, theirs):
    width = mine.shape[1]
    return times_transposed(slope_ref[:, part_of(core_ref, width)], mine) + times_transposed(
        slope_ref[:, part_of(core_ref, width, True)], theirs
    )


def norm_parts(values):
    center = values - jnp.mean(values, -1, keepdims=True)
    spread = jnp.mean(center * center, -1, keepdims=True)
    factor = lax.rsqrt(spread + norm_epsilon)
    return center * factor, factor


def norm_rows(values, mods, gains, n, shift):
    hat, _ = norm_parts(values)
    gain, at = gains[n : n + 1, :], slice(shift + 1, shift + 2)
    return hat * gain * (1.0 + mods[at, :]) + mods[shift : shift + 1, :]


def norm_back(values, slope, mods, gains, n, shift):
    hat, factor = norm_parts(values)
    gain, scale = gains[n : n + 1, :], 1.0 + mods[shift + 1 : shift + 2, :]
    along = jnp.sum(slope * hat, 0, keepdims=True)
    inner = slope * gain * scale
    inner = inner - jnp.mean(inner, -1, keepdims=True) - hat * jnp.mean(inner * hat, -1, keepdims=True)
    return inner * factor, (along * scale, jnp.sum(slope, 0, keepdims=True), along * gain)


def store_rows(out_ref, rows):
    which = iota(out_ref.shape, 0)
    block = jnp.zeros(out_ref.shape, wide)
    for n, row in enumerate(rows):
        block = jnp.where(which == n, row, block)
    out_ref[...] = block


ROOT = (2.0 / 3.141592653589793) ** 0.5


def gelu_parts(values):
    bend = jnp.tanh(ROOT * (values + 0.044715 * values * values * values))
    return 0.5 * values * (1.0 + bend), bend


def gelu_slope(values):
    _, bend = gelu_parts(values)
    inner = ROOT * (1.0 + 3.0 * 0.044715 * values * values)
    return 0.5 * (1.0 + bend) + 0.5 * values * (1.0 - bend * bend) * inner


def qkv_kernel(cut, core_ref, hidden_ref, mods, gains, mine, theirs, normed_ref, triple_ref):
    normed_ref[...] = norm_rows(hidden_ref[...], mods, gains, 0, 0).astype(low)
    product(core_ref, normed_ref[...], mine[:, :cut], theirs[:, :cut], triple_ref)


def head_pair(at, triple_ref):
    third = triple_ref.shape[1] // 3
    return [triple_ref[:, n * third + at : n * third + at + 2 * HEAD_DIM] for n in range(3)]


def head_probs(query, key, same):
    scores = times_transposed(query, key) * HEAD_DIM ** (-0.5)
    scores = jnp.where(same, scores, -1e30)
    expo = jnp.exp(scores - jnp.max(scores, -1, keepdims=True))
    return expo / jnp.sum(expo, -1, keepdims=True)


def masks_of(segment_ref, triple_ref):
    segment = segment_ref[...].astype(wide)
    same = as_column(segment) == segment
    lane = iota((triple_ref.shape[0], 2 * HEAD_DIM), 1)
    return same, (lane < HEAD_DIM, lane >= HEAD_DIM)


def attend_kernel(core_ref, triple_ref, segment_ref, out_ref):
    same, sides = masks_of(segment_ref, triple_ref)
    for at in range(0, out_ref.shape[1], 2 * HEAD_DIM):
        query, key, value = head_pair(at, triple_ref)
        results = []
        for side in sides:
            probs = head_probs(jnp.where(side, query, 0.0).astype(low), key, same)
            results.append(jnp.dot(probs.astype(low), value, preferred_element_type=wide))
        out_ref[:, at : at + 2 * HEAD_DIM] = jnp.where(sides[0], *results).astype(low)


def attend_back_kernel(core_ref, triple_ref, grad_ref, segment_ref, out_ref):
    same, sides = masks_of(segment_ref, triple_ref)
    third = triple_ref.shape[1] // 3
    factor = HEAD_DIM ** (-0.5)
    for at in range(0, third, 2 * HEAD_DIM):
        query, key, value = head_pair(at, triple_ref)
        grad = grad_ref[:, at : at + 2 * HEAD_DIM]
        queries, key_back, value_back = [], 0.0, 0.0
        for side in sides:
            own_query = jnp.where(side, query, 0.0).astype(low)
            own_grad = jnp.where(side, grad, 0.0).astype(low)
            probs = head_probs(own_query, key, same)
            value_back = value_back + times_rows(probs.astype(low), own_grad)
            slope = times_transposed(own_grad, value)
            slope = probs * (slope - jnp.sum(probs * slope, -1, keepdims=True))
            slope = slope.astype(low)
            queries.append(jnp.dot(slope, key, preferred_element_type=wide))
            key_back = key_back + times_rows(slope, own_query)
        parts = (jnp.where(sides[0], *queries) * factor, key_back * factor, value_back)
        for n, part in enumerate(parts):
            out_ref[:, n * third + at : n * third + at + 2 * HEAD_DIM] = part.astype(low)


def out_kernel(
    cuts, core_ref, attended_ref, hidden_ref, mods, gains, mine, theirs, branch_ref, mid_ref, normed_ref
):
    at = slice(*cuts)
    product(core_ref, attended_ref[...], mine[:, at], theirs[:, at], branch_ref)
    mid_ref[...] = hidden_ref[...] + mods[2:3, :] * branch_ref[...]
    normed_ref[...] = norm_rows(mid_ref[...], mods, gains, 1, 3).astype(low)


def up_kernel(core_ref, normed_ref, mine, theirs, up_ref, active_ref):
    product(core_ref, normed_ref[...], mine[...], theirs[...], up_ref)
    active_ref[...] = gelu_parts(up_ref[...])[0].astype(low)


def down_kernel(
    core_ref, active_ref, mid_ref, mods, gains, spot_ref, mine, theirs, branch_ref, end_ref, picked_ref
):
    product(core_ref, active_ref[...], mine[...], theirs[...], branch_ref)
    end_ref[...] = mid_ref[...] + mods[5:6, :] * branch_ref[...]
    final = norm_rows(end_ref[...], mods, gains, 2, 6).astype(low)
    picked_ref[...] = jnp.dot(spot_ref[...], final, preferred_element_type=wide).astype(low)


def down_back_kernel(
    core_ref,
    picked_ref,
    alive_ref,
    end_ref,
    branch_ref,
    mods,
    gains,
    up_ref,
    mine,
    theirs,
    end_back_ref,
    branch_back_ref,
    up_back_ref,
    sums_ref,
):
    slope = times_rows(alive_ref[...], picked_ref[...])
    slope, sums = norm_back(end_ref[...], slope, mods, gains, 2, 6)
    end_back_ref[...] = slope
    gate = jnp.sum(slope * branch_ref[...], 0, keepdims=True)
    store_rows(sums_ref, sums + (gate,))
    branch_back_ref[...] = (mods[5:6, :] * slope).astype(low)
    active = product_back(core_ref, branch_back_ref, mine[...], theirs[...])
    up_back_ref[...] = (active * gelu_slope(up_ref[...])).astype(low)


def up_back_kernel(
    cuts,
    core_ref,
    up_back_ref,
    mid_ref,
    end_back_ref,
    branch_ref,
    mods,
    gains,
    mine,
    theirs,
    mine_out,
    theirs_out,
    mid_back_ref,
    branch_back_ref,
    attended_back_ref,
    sums_ref,
):
    slope = product_back(core_ref, up_back_ref, mine[...], theirs[...])
    slope, sums = norm_back(mid_ref[...], slope, mods, gains, 1, 3)
    slope = end_back_ref[...] + slope
    mid_back_ref[...] = slope
    gate = jnp.sum(slope * branch_ref[...], 0, keepdims=True)
    store_rows(sums_ref, sums + (gate,))
    branch_back_ref[...] = (mods[2:3, :] * slope).astype(low)
    at = slice(*cuts)
    back = product_back(core_ref, branch_back_ref, mine_out[:, at], theirs_out[:, at])
    attended_back_ref[...] = back.astype(low)


def start_back_kernel(
    cut,
    core_ref,
    triple_back_ref,
    start_ref,
    mid_back_ref,
    mods,
    gains,
    mine,
    theirs,
    collect_ref,
    masked_ref,
    sent_ref,
    sums_ref,
    pair_ref,
):
    slope = product_back(core_ref, triple_back_ref, mine[:, :cut], theirs[:, :cut])
    slope, sums = norm_back(start_ref[...], slope, mods, gains, 0, 0)
    slope = (mid_back_ref[...] + slope).astype(low)
    mask = jnp.sum(masked_ref[...] * slope.astype(wide), 0, keepdims=True)
    store_rows(sums_ref, sums + (mask,))
    rows = jnp.dot(collect_ref[...], slope, preferred_element_type=wide)
    half, width = sent_ref.shape[1], sent_ref.shape[2] // 2
    for n in range(sent_ref.shape[0]):
        pair_ref[:, :width] = rows[:half, n * width : (n + 1) * width]
        pair_ref[:, width:] = rows[half:, n * width : (n + 1) * width]
        sent_ref[core_ref[1] ^ n] = pair_ref[...].astype(low)


def advance(weight_now, moment_now, average_now, gradient, clip_factor, rate_now):
    clipped = gradient * clip_factor
    moment_next = momentum_rate * moment_now + clipped
    weight_next = weight_now - rate_now * (clipped + momentum_rate * moment_next)
    return (
        weight_next,
        moment_next,
        average_rate * average_now + (1.0 - average_rate) * weight_next,
    )


def join_stats(pieces):
    peak_value = functools.reduce(jnp.maximum, [piece[0] for piece in pieces])
    summed = sum(piece[1] * jnp.exp(piece[0] - peak_value) for piece in pieces)
    return jnp.stack([peak_value, summed, sum(piece[2] for piece in pieces)])


def shards(
    x_clean,
    mask_index,
    segment_ids,
    noise_level,
    embedding,
    head_table,
    w_time,
    w_ada,
    norm_gains,
    w_qkv,
    w_out,
    w_up,
    w_down,
    *states,
):
    vocab_index = lax.axis_index("vocab")
    dp_index = lax.axis_index("dp")
    vocab_count = lax.axis_size("vocab")
    dp_count = lax.axis_size("dp")
    links = Links(dp_count, vocab_count)
    device_count = dp_count * vocab_count
    device_index = dp_index * vocab_count + vocab_index
    length = x_clean.shape[1]
    slot_count = mask_index.shape[1]
    kept_count = length - FEWEST_MASKED
    span = embedding.shape[0]
    columns = head_table.shape[1]
    slice_width = embedding.shape[1]
    model_width = slice_width * dp_count
    cond_width = w_time.shape[1]
    mask_id = VOCAB - 1

    place = vocab_index.astype(jnp.int32)[None]
    mask_local = mask_id - vocab_index * span
    mask_owner = (mask_local >= 0) & (mask_local < span)
    mask_row = lax.dynamic_slice_in_dim(embedding.T, jnp.clip(mask_local, 0, span - 1), 1, 1)
    mask_row = jnp.where(mask_owner, mask_row, 0.0).reshape(1, -1)
    small, first_half, second_half, collect, at_spot, alive_spot, masked = prepare(
        mask_id, place, noise_level, x_clean, mask_index, w_time, norm_gains, mask_row, kept_count
    )
    core = links.place("c").astype(jnp.int32)
    pack_mine, pack_theirs = packed(core[None], w_qkv, w_out, w_ada.T, w_up, w_down)
    pair = links.pair_rows(pack_mine, pack_theirs)
    rows = w_up.shape[0]
    qkv_width, ada_width = w_qkv.shape[1], w_ada.shape[1] // rows * cond_width
    ends = [0]
    for width in (qkv_width, model_width, ada_width, w_up.shape[1], w_down.size // rows):
        ends.append(ends[-1] + width // 2)
    pair_a, pair_bc = pair[:, : ends[3]], pair[:, ends[3] :]
    width_c = model_width // 2

    piece = -(-columns // (dp_count * LANES)) * LANES
    dp_place = dp_index.astype(jnp.int32)[None]
    small_z = links.heard(small, "z")
    head_slots = split_head(links, dp_place, head_table, piece)
    small_z, head_slots, table = tie(small_z, head_slots, embedding)
    small_dp = links.doubled(links.piled(small_z, "z"), "dp")
    a_z = links.heard(pair_a, "z")
    table = turned(table.T)
    small_dp, table, a_z = tie(small_dp, table, a_z)
    a_mine = links.wide_across(a_z)
    small_c = links.heard(small_dp, "c")
    head_came = links.exchange(head_slots)
    small_c, pair_bc = tie(small_c, pair_bc)
    bc_z = links.heard(pair_bc, "z")

    numbers = links.piled(small_c, "c", 2).reshape((device_count,) + small.shape)
    ids_all = numbers[:, 0, :kept_count].astype(jnp.int32)
    targets = numbers[:, 1, :slot_count].astype(jnp.int32)
    levels = numbers[:, 2, 0]
    mask_row_full = jnp.sum(
        numbers[:, 3, :slice_width].reshape(dp_count, vocab_count, slice_width), 1
    ).reshape(-1)
    gains = jnp.swapaxes(numbers[:, 4:7, : norm_gains.shape[1]], 0, 1).reshape(3, model_width)
    time_weight = numbers[:, 8 : 8 + w_time.shape[0], :cond_width].reshape(-1, cond_width)
    live = (targets >= 0).astype(wide)
    masked_count = jnp.sum(live)

    first = jnp.sum((ids_all < vocab_index * span).astype(jnp.int32), 1)
    stop_id = jnp.minimum((vocab_index + 1) * span, mask_id)
    last = jnp.maximum(jnp.sum((ids_all < stop_id).astype(jnp.int32), 1), first)
    spot = jnp.stack(
        [dp_index, links.place("z"), links.place("c"), vocab_index * span]
    ).astype(jnp.int32)
    grid = (dp_count, links.size("z"), links.size("c"))
    looked = look_up(spot, first, last, ids_all, table, grid)
    looked, bc_z, head_came = tie(looked, bc_z, head_came)
    looked_c = looked[0], [links.hop(looked[1], "c", 1)]
    looked = links.summed(looked_c).astype(low)
    looked = looked.reshape((grid[1], grid[0]) + looked.shape[1:])
    looked_z = links.near(looked, "z")
    half_up = w_up.shape[1] // 2
    b_first = links.across_first([piece[:, :half_up] for piece in bc_z], half_cut(half_up))
    c_mine = links.wide_across([laid_out(piece[:, half_up:], 2, rows, width_c) for piece in bc_z])

    by_core = lambda values: jnp.moveaxis(
        values.reshape(dp_count * links.size("z"), links.size("c"), -1), 1, 0
    ).reshape(-1, ROW_BLOCK)
    limit = jnp.minimum(columns, VOCAB - vocab_index * columns) - dp_index * piece
    target_local = by_core(targets) - vocab_index * columns - dp_index * piece
    target_local = jnp.where((target_local >= 0) & (target_local < limit), target_local, -1)
    target_local = target_local.astype(wide)
    row_weight = by_core(nelbo_weight(levels)[:, None] * live)
    row_share = row_weight / masked_count
    scalars = jnp.stack([core, limit.astype(jnp.int32), dp_place[0]])

    level = lax.dynamic_index_in_dim(noise_level, vocab_index, keepdims=False)
    spectrum = features(level[None], FREQ)
    before_time = jnp.dot(spectrum, time_weight, precision=highest)
    hidden_time = jax.nn.silu(before_time)
    time_rows = w_time.shape[0]
    spectrum_rows = lax.dynamic_slice_in_dim(
        features(levels, FREQ), device_index * time_rows, time_rows, 1
    )
    spectrum_rows = spectrum_rows.reshape(grid + (time_rows,))
    spectrum_rows = jnp.swapaxes(spectrum_rows, 1, 2).reshape(device_count, time_rows)
    early = (hidden_time, gains, mask_row_full, target_local, row_share, scalars, spectrum_rows)
    looked_z, early, b_first = tie(looked_z, early, b_first)
    b_second = links.across_second(b_first)
    hidden_time, gains, mask_row_full, target_local, row_share, scalars, spectrum_rows = early
    looked = links.summed((looked_z[0], looked_z[1:])).astype(low)
    looked_dp = links.near(looked, "dp")
    looked_dp, a_mine = tie(looked_dp, a_mine)
    a_other = links.hop(a_mine, "c", 1)
    hidden_start = enter(
        first_half, second_half, masked, mask_row_full, links.ordered(looked_dp, "dp")
    )

    ada_weight = links.halves_back(a_mine[:, ends[2] :], a_other[:, ends[2] :])
    ada_weight = ada_weight.reshape(device_count, rows, -1, cond_width)
    ada_weight = jnp.swapaxes(ada_weight, 1, 2).reshape(-1, cond_width)
    mods = lax.dot_general(
        hidden_time, ada_weight.astype(wide), (((1,), (1,)), ((), ())), precision=highest
    ).reshape(8, -1)
    here = jnp.stack([core, dp_place[0]])
    square, inner = (length, model_width), (length, w_up.shape[1])
    normed_a, triple = kernel_call(
        functools.partial(qkv_kernel, ends[1]),
        here,
        (hidden_start, mods, gains, a_mine, a_other),
        ((square, low), ((length, qkv_width), low)),
    )
    (attended,) = kernel_call(attend_kernel, here, (triple, segment_ids), ((square, low),))
    attended, b_second = tie(attended, b_second)
    branch_a, hidden_mid, normed_b = kernel_call(
        functools.partial(out_kernel, ends[1:3]),
        here,
        (attended, hidden_start, mods, gains, a_mine, a_other),
        ((square, wide), (square, wide), (square, low)),
    )
    b_mine = links.across_done(b_second)
    b_other = links.hop(b_mine, "c", 1)
    c_other = links.hop(c_mine, "c", 1)
    up_values, active = kernel_call(
        up_kernel, here, (normed_b, b_mine, b_other), ((inner, wide), (inner, low))
    )
    branch_m, hidden_end, picked = kernel_call(
        down_kernel,
        here,
        (active, hidden_mid, mods, gains, at_spot, c_mine, c_other),
        ((square, wide), (square, wide), ((slot_count, model_width), low)),
    )

    cut_rows = half_cut(model_width)
    picked, head_came = tie(picked, head_came)
    picked_z = links.heard(picked, "z")
    head_pieces = links.exchanged(head_came)
    picked_z, head_pieces = tie(picked_z, head_pieces)
    head = jnp.concatenate(links.ordered(head_pieces, "dp"), 0)
    rows_first = links.across_first(picked_z, cut_rows)
    rows_second = links.across_second(rows_first)
    rows_mine = links.across_done(rows_second)
    rows_theirs = links.hop(rows_mine, "c", 1)
    values, stats = head_logits(scalars, rows_mine, rows_theirs, head, target_local)
    stats = links.total(stats, join_stats)
    log_total = stats[0] + jnp.log(stats[1])
    slopes, rows_own, rows_given = head_slopes(
        scalars, values, head, jnp.stack([target_local, log_total, row_share])
    )
    loss_sum = jnp.sum(row_share * (log_total - stats[2])) * masked_count
    rows_fold = rows_own, [links.hop(rows_given, "c", 1)]
    rows_fold, slopes = tie(rows_fold, slopes)
    rows_fold = links.by_place(links.summed(rows_fold).astype(low))
    rows_fold = links.fold_first(rows_fold, cut_rows)
    grad_head, head_squares = head_grads(links, scalars, rows_mine, rows_theirs, slopes)
    rows_fold, grad_head = tie(rows_fold, grad_head)
    rows_fold = links.fold_second(rows_fold)
    rows_fold, grad_head = tie(rows_fold, grad_head)
    back_came = links.exchange(grad_head)
    grad_mine = links.summed(links.fold_z(links.fold_third(rows_fold))).astype(low)

    def weight_given(left_matrix, slopes):
        return times_rows(left_matrix, links.half(slopes, True)).astype(low)

    def weight_own(left_matrix, slopes):
        return times_rows(left_matrix, links.half(slopes))

    grad_end, grad_branch_m, grad_upper, sums_3 = kernel_call(
        down_back_kernel,
        here,
        (
            grad_mine,
            alive_spot,
            hidden_end,
            branch_m,
            mods,
            gains,
            up_values,
            c_mine,
            c_other,
        ),
        ((square, wide), (square, low), (inner, low), ((8, model_width), wide)),
        megabytes=16,
    )
    grad_upper, back_came = tie(grad_upper, back_came)
    down_came = links.hop(weight_given(active, grad_branch_m), "c", 1)
    up_came = links.hop(weight_given(normed_b, grad_upper), "c", 1)
    grad_mid, grad_branch_a, grad_attended, sums_2 = kernel_call(
        functools.partial(up_back_kernel, ends[1:3]),
        here,
        (
            grad_upper,
            hidden_mid,
            grad_end,
            branch_a,
            mods,
            gains,
            b_mine,
            b_other,
            a_mine,
            a_other,
        ),
        ((square, wide), (square, low), (square, low), ((8, model_width), wide)),
        megabytes=16,
    )
    grad_attended, down_came, up_came = tie(grad_attended, down_came, up_came)
    up_sum = (weight_own(normed_b, grad_upper) + up_came.astype(wide)).astype(low)
    down_sum = (weight_own(active, grad_branch_m) + down_came.astype(wide)).astype(low)
    layer_sum = jnp.concatenate([up_sum] + beside_blocks(down_sum, device_count, rows), 1)
    layer_wide = links.fold_across(links.by_place(layer_sum))
    (grad_triple,) = kernel_call(
        attend_back_kernel,
        here,
        (triple, grad_attended, segment_ids),
        (((length, qkv_width), low),),
        megabytes=16,
    )
    sent, sums_1 = kernel_call(
        functools.partial(start_back_kernel, ends[1]),
        here,
        (
            grad_triple,
            hidden_start,
            grad_mid,
            mods,
            gains,
            a_mine,
            a_other,
            collect,
            masked,
        ),
        (
            ((dp_count, kept_count // 2, 2 * slice_width), low),
            ((8, model_width), wide),
        ),
        [pltpu.VMEM((kept_count // 2, 2 * slice_width), wide)],
        megabytes=16,
    )

    start_dp = links.near(sent, "dp")
    a_given = [weight_given(normed_a, grad_triple), weight_given(attended, grad_branch_a)]
    a_came = links.hop(jnp.concatenate(a_given, 1), "c", 1)
    vector = tell(sums_1, sums_2, sums_3, ada_weight, hidden_time, before_time)
    vector = links.doubled(vector, "z")
    start_dp, a_came, vector = tie(start_dp, a_came, vector)
    start_z = links.heard(jnp.stack(start_dp), "z")
    a_own = [weight_own(normed_a, grad_triple), weight_own(attended, grad_branch_a)]
    a_sum = (jnp.concatenate(a_own, 1) + a_came.astype(wide)).astype(low)
    a_fold = links.fold_first(links.by_place(a_sum), half_cut(a_sum.shape[1]))
    start_z, a_fold = tie(start_z, a_fold)
    start_mine = jnp.concatenate(start_z, 0)
    start_theirs = links.hop(start_mine, "c", 1)
    a_fold = links.fold_second(a_fold)
    vector = links.heard(vector, "c")
    start_theirs, a_fold, layer_wide, back_came, vector = tie(
        start_theirs, a_fold, layer_wide, back_came, vector
    )
    vectors = links.doubled(links.piled(vector, "c"), "dp")
    vectors = vectors.reshape((device_count,) + vectors.shape[3:])
    back_pieces = links.exchanged(back_came)
    a_block = links.fold_third(a_fold)
    all_fold = links.fold_z(jnp.concatenate([a_block, layer_wide], 2))
    grad_table, table_squares = add_up(
        spot, first, last, ids_all, start_mine, start_theirs, span, grid
    )
    grad_table, all_fold, vectors, back_pieces = tie(grad_table, all_fold, vectors, back_pieces)
    all_sums = links.summed(all_fold)
    cuts = (0, a_block.shape[2], a_block.shape[2] + half_up, all_sums.shape[1])
    sum_a, sum_up, sum_down = [all_sums[:, cuts[n] : cuts[n + 1]] for n in range(3)]
    sum_down = laid_out(sum_down, 2, rows, width_c)
    sums = [sum_a, sum_up, sum_down]
    grad_a, grad_up, grad_down = [links.own_rows(block) for block in sums]
    grad_a = [grad_a[:, : grad_a.shape[1] // 2], grad_a[:, grad_a.shape[1] // 2 :]]
    grad_qkv = jnp.concatenate([side[:, : ends[1]] for side in grad_a], 1)
    grad_out = jnp.concatenate([side[:, ends[1] :] for side in grad_a], 1)
    grad_head = jnp.concatenate(links.ordered(back_pieces, "dp"), 1)[:, :columns].astype(wide)
    grad_ada, grad_time, grad_gain_rows, mask_grad_own, small_square = finish(
        jnp.stack([device_index, dp_index, mask_owner.astype(jnp.int32)]).astype(jnp.int32),
        vectors,
        spectrum_rows,
        w_ada.shape[1],
        cond_width,
        norm_gains.shape[1],
        slice_width,
    )
    mask_column = (jnp.arange(span) == mask_local)[None, :]
    grad_table = grad_table + jnp.where(mask_column, mask_grad_own.reshape(-1, 1), 0.0)

    grads_all = (
        grad_table,
        grad_head,
        grad_time,
        grad_ada,
        grad_gain_rows,
        grad_qkv,
        grad_out,
        grad_up,
        grad_down,
    )
    squares = jnp.sum(table_squares) + jnp.sum(head_squares) + small_square[0, 0]
    squares = squares + jnp.sum(all_sums * all_sums)
    square_total = links.total(jnp.broadcast_to(squares, (8, LANES)), sum)[0, 0]
    grad_norm = jnp.sqrt(square_total)
    clip_factor = jnp.minimum(1.0, clip_level / (grad_norm + 1e-06))
    weights_now = (embedding, head_table, w_time, w_ada, norm_gains, w_qkv, w_out, w_up, w_down)
    on_side = (0, 3)
    updated = []
    for place, (weight_now, gradient) in enumerate(zip(weights_now, grads_all)):
        state = (weight_now, states[place], states[len(weights_now) + place])
        if place in on_side:
            state = tuple(array.T for array in state)
        rate = embed_rate if place == 0 else learn_rate
        result = advance(*state, gradient, clip_factor, rate)
        if place in on_side:
            result = tuple(array.T for array in result)
        updated.append(result)
    new_arrays = tuple(result[n] for n in range(3) for result in updated)
    return (*new_arrays, loss_sum, masked_count, grad_norm)


def solution(mesh):
    both = ("dp", "vocab")
    weights_placed = (
        P("vocab", "dp"),
        P("dp", "vocab"),
        P(both, None),
        P(None, both),
        P(None, both),
        P(both, None),
        P(both, None),
        P(both, None),
        P(both, None),
    )
    return jax.shard_map(
        shards,
        mesh=mesh,
        in_specs=(P(both, None), P(both, None), P(both, None), P("dp")) + 3 * weights_placed,
        out_specs=3 * weights_placed + (P(), P(), P()),
        check_vma=False,
    )
```

time: 803 us -> 651 us (0.81)
  Pallas kernels: 25.1 us -> 164 us
  other arithmetic: 165 us -> 75.9 us
  waiting for transfers between devices: 267 us -> 199 us
  starting transfers between devices: 166 us -> 104 us
  matrix products: 76.8 us -> 16.2 us
  local copies, waits for them, and re-layouts: 81.7 us -> 59.2 us
  between operations: 13.3 us -> 23.5 us
    pallas_call x2 -> x21, Pallas kernels: 25.1 us -> 164 us  [the longest x11 54.2 us: kernel_call(): pl.pallas_call(kernel, out_shape=out, in_specs=[pl.BlockSpec(memory_space...]
    ppermute x146 -> x86, waiting for transfers between devices: 267 us -> 176 us  [hop(): return lax.ppermute(value, ('dp', 'vocab'), pairs)]
    ppermute x146 -> x86, starting transfers between devices: 166 us -> 104 us  [hop(): return lax.ppermute(value, ('dp', 'vocab'), pairs)]
    dot_general x22 -> x1, matrix products: 51.7 us -> 1.32 us  [shards(): lax.dot_general(hidden_time, ada_weight.astype(wide), (((1,), (1,)), ((),...]
    another operation x100 -> x32, other arithmetic: 40.8 us -> 10.8 us  [the longest x24 8.65 us: piled(): return jnp.stack(self.ordered(pieces, axis), dim)]
    convert_element_type x28 -> x15, other arithmetic: 42.9 us -> 14 us  [the longest x4 3.2 us: fold_third(): self.summed(state).astype(low)]
    reduce_sum x23 -> x6, other arithmetic: 30 us -> 5.33 us  [the longest x1 2.18 us: shards(): squares = squares + jnp.sum(all_sums * all_sums)]
    all_gather x0 -> x2, waiting for transfers between devices: none -> 22.8 us  [wide_across(): block = lax.all_gather(self.piled(pieces, 'z'), 'dp', axis=0, tiled=False)]
  transfers between devices with their start and end apart: 146 -> 89, of which waited for: 65 -> 43; matrix products, arithmetic and copies ran while one was open for 23% -> 15% of each run, Pallas kernels for 3% -> 18%
where the time goes in v2:
time: 651 us; the launch traced here: 642 us
  waiting for transfers between devices  199 us (31%)
  Pallas kernels  164 us (25%)
  starting transfers between devices  104 us (16%)
  other arithmetic  75.9 us (12%)
  local copies, waits for them, and re-layouts  59.2 us (9%)
  between operations  23.5 us (4%)
  matrix products  16.2 us (2%)
    ppermute x86, waiting for transfers between devices, hop(): return lax.ppermute(value, ('dp', 'vocab'), pairs)  176 us
    ppermute x86, starting transfers between devices, hop(): return lax.ppermute(value, ('dp', 'vocab'), pairs)  104 us
    pallas_call x11, Pallas kernels, kernel_call(): pl.pallas_call(kernel, out_shape=out, in_specs=[pl.BlockSpec(memory_space...  54.2 us
    unnamed x259, local copies, waits for them, and re-layouts  28.2 us
    all_gather x2, waiting for transfers between devices, wide_across(): block = lax.all_gather(self.piled(pieces, 'z'), 'dp', axis=0, tiled=False)  22.8 us
    pallas_call x1, Pallas kernels, head_slopes(): head_call(slopes_kernel, half, (jax.ShapeDtypeStruct((2 * count, columns)...  21.8 us
    pallas_call x1, Pallas kernels, add_up(): pl.pallas_call(functools.partial(add_up_kernel, grid), out_shape=(jax.Sha...  20.8 us
    pallas_call x1, Pallas kernels, head_logits(): head_call(logits_kernel, half, (jax.ShapeDtypeStruct((2 * count, columns)...  18.2 us
  transfers between devices with their start and end apart: 89, of which 43 were waited for; matrix products, arithmetic and copies ran while one was open for 15% of the time, Pallas kernels for 18%

profile of v2, /device:TPU:0, one launch (start us, length us, event | category | flops | bytes accessed | tf_op | source)
XLA Modules:
  0.0 642.1 jit_solution(5924614147871601994)
XLA Ops:
  30.4 7.7 %shard_map.528.table_ref = f32[6288,192]{1,0:T(8,128)} custom-call(f32[192,6288]{1,0:T(8,128)} %bitcast.569), custom_call_target="tpu_custom_call" | custom-call | bytes 25165824 | tf_op jit(solution)/shard_map/pallas_call | solution.py:251
  45.0 5.4 collective-permute-done.6
  50.4 8.5 %collective-permute-done.7 = bf16[48,2048]{1,0:T(8,128)(2,1)S(1)} collective-permute-done((bf16[48,2048]{1,0:T(8,128)(2,1)S(1)}, bf16[48,2048]{1,0:T(8,128)(2,1)S(1)}, u32[]{:S(2)}, u32[]{:S(2)}) %collective-permute-start.7) | collective-permute-done | bytes 196640 | tf_op jit(solution)/shard_map/ppermute | solution.py:64
  71.7 14.3 %shard_map.530 = (bf16[16,112,384]{2,1,0:T(8,128)(2,1)}, bf16[16,112,384]{2,1,0:T(8,128)(2,1)}) custom-call(s32[4]{0:T(128)} %pad_add_fusion.spot_ref, s32[32]{0:T(128)} %copy-done.115, s32[32]{0:T(128)} %max.68.last_ref, s32[32,224]{1,0:T(8,128)} %fusion.32.ids_ref, f32[6288,192]{1,0:T(8,128)} %shard_map.528.table_ref), custom_call_target="tpu_custom_call" | custom-call | bytes 37748736 | tf_op jit(solution)/shard_map/pallas_call | solution.py:349
  93.6 5.9 collective-permute-start.15
  104.2 7.3 %collective-permute-done.18 = bf16[4,48,768]{2,1,0:T(8,128)(2,1)S(1)} collective-permute-done((bf16[4,48,768]{2,1,0:T(8,128)(2,1)S(1)}, bf16[4,48,768]{2,1,0:T(8,128)(2,1)S(1)}, u32[]{:S(2)}, u32[]{:S(2)}) %collective-permute-start.18) | collective-permute-done | bytes 294944 | tf_op jit(solution)/shard_map/ppermute | solution.py:64
  114.8 11.5 %collective-permute-done.16 = bf16[4,112,384]{2,1,0:T(8,128)(2,1)S(1)} collective-permute-done((bf16[4,112,384]{2,1,0:T(8,128)(2,1)}, bf16[4,112,384]{2,1,0:T(8,128)(2,1)S(1)}, u32[]{:S(2)}, u32[]{:S(2)}) %collective-permute-start.16) | collective-permute-done | bytes 344096 | tf_op jit(solution)/shard_map/ppermute | solution.py:64
  163.3 22.8 %all-gather.7.cloned.1.call-done = bf16[16,192,384]{2,1,0:T(8,128)(2,1)} async-done(((bf16[4,192,384]{2,1,0:T(8,128)(2,1)}), bf16[16,192,384]{2,1,0:T(8,128)(2,1)}) %all-gather.7.cloned.1.call-update) | async-done | bytes 2359312 | tf_op jit(solution)/shard_map/all_gather | solution.py:141
  190.8 6.2 shard_map.535
  199.6 5.7 shard_map.536
  213.2 24.6 %collective-permute-done.31 = bf16[2,192,1664]{2,1,0:T(8,128)(2,1)S(1)} collective-permute-done((bf16[2,192,1664]{2,1,0:T(8,128)(2,1)S(1)}, bf16[2,192,1664]{2,1,0:T(8,128)(2,1)S(1)}, u32[]{:S(2)}, u32[]{:S(2)}) %collective-permute-start.31) | collective-permute-done | bytes 1277984 | tf_op jit(solution)/shard_map/ppermute | solution.py:64
  240.3 6.6 %collective-permute-done.32 = bf16[4,96,384]{2,1,0:T(8,128)(2,1)S(1)} collective-permute-done((bf16[4,96,384]{2,1,0:T(8,128)(2,1)S(1)}, bf16[4,96,384]{2,1,0:T(8,128)(2,1)S(1)}, u32[]{:S(2)}, u32[]{:S(2)}) %collective-permute-start.32) | collective-permute-done | bytes 294944 | tf_op jit(solution)/shard_map/ppermute | solution.py:64
  250.6 11.6 %collective-permute-done.33 = bf16[2,4,96,384]{3,2,1,0:T(8,128)(2,1)S(1)} collective-permute-done((bf16[2,4,96,384]{3,2,1,0:T(8,128)(2,1)S(1)}, bf16[2,4,96,384]{3,2,1,0:T(8,128)(2,1)S(1)}, u32[]{:S(2)}, u32[]{:S(2)}) %collective-permute-start.33) | collective-permute-done | bytes 589856 | tf_op jit(solution)/shard_map/ppermute | solution.py:64
  269.2 18.2 %shard_map.537 = (f32[3072,1664]{1,0:T(8,128)}, f32[3,12,256]{2,1,0:T(8,128)S(1)}) custom-call(s32[3]{0:T(128)S(1)} %pad_add_fusion.2.scalar_ref, bf16[1536,768]{1,0:T(8,128)(2,1)S(1)} %bitcast.550, bf16[1536,768]{1,0:T(8,128)(2,1)} %copy-done.118, bf16[768,1664]{1,0:T(8,128)(2,1)} %pad_maximum_fusion.head_ref, f32[12,256]{1,0:T(8,128)S(1)} %select_convert_fusion.info_ref), custom_call_target="tpu_custom_call" | custom-call | flops 7851737088 | bytes 20447232 | tf_op jit(solution)/shard_map/pallas_call | solution.py:819
  305.8 21.8 %shard_map.538 = (bf16[3072,1664]{1,0:T(8,128)(2,1)}, bf16[1536,768]{1,0:T(8,128)(2,1)S(1)}, bf16[1536,768]{1,0:T(8,128)(2,1)}) custom-call(s32[3]{0:T(128)S(1)} %pad_add_fusion.2.scalar_ref, f32[3072,1664]{1,0:T(8,128)} %get-tuple-element.258.value_ref, bf16[768,1664]{1,0:T(8,128)(2,1)} %pad_maximum_fusion.head_ref, ...), custom_call_target="tpu_custom_call" | custom-call | flops 7851737088 | bytes 20447232 | tf_op jit(solution)/shard_map/pallas_call | solution.py:863
  329.2 4.7 collective-permute-done.44
  339.6 15.5 %shard_map.539 = (bf16[4,192,1664]{2,1,0:T(8,128)(2,1)}, f32[1,1664]{1,0:T(1,128)S(1)}) custom-call(s32[3]{0:T(128)S(1)} %pad_add_fusion.2.scalar_ref, bf16[1536,768]{1,0:T(8,128)(2,1)S(1)} %bitcast.551, bf16[1536,768]{1,0:T(8,128)(2,1)} %copy-done.118, bf16[3072,1664]{1,0:T(8,128)(2,1)} %get-tuple-element.266.slope_ref), custom_call_target="tpu_custom_call" | custom-call | flops 7851737088 | bytes 20447232 | tf_op jit(solution)/shard_map/pallas_call | solution.py:907
  358.5 6.5 %collective-permute-done.48 = bf16[4,96,384]{2,1,0:T(8,128)(2,1)} collective-permute-done((bf16[4,96,384]{2,1,0:T(8,128)(2,1)}, bf16[4,96,384]{2,1,0:T(8,128)(2,1)}, u32[]{:S(2)}, u32[]{:S(2)}) %collective-permute-start.48) | collective-permute-done | bytes 294944 | tf_op jit(solution)/shard_map/ppermute | solution.py:64
  378.5 5.8 collective-permute-done.50
  388.2 8.4 %shard_map.540 = (f32[256,768]{1,0:T(8,128)S(1)}, bf16[256,768]{1,0:T(8,128)(2,1)S(1)}, bf16[256,3072]{1,0:T(8,128)(2,1)}, f32[8,768]{1,0:T(8,128)S(1)}) custom-call(s32[2]{0:T(128)S(1)} %pad_add_fusion.1.core_ref, bf16[96,768]{1,0:T(8,128)(2,1)S(1)} %fusion.11.picked_ref, bf16[96,256]{1,0:T(8,128)(2,1)S(1)} %copy-done.42, f32[256,768]{1,0:T(8,128)S(1)} %copy-done.29, ...), custom_call_target="tpu_custom_call" | custom-call | bytes 16777216 | tf_op jit(solution)/shard_map/pallas_call | solution.py:931
  406.0 7.7 %shard_map.541 = (f32[256,768]{1,0:T(8,128)S(1)}, bf16[256,768]{1,0:T(8,128)(2,1)S(1)}, bf16[256,768]{1,0:T(8,128)(2,1)S(1)}, f32[8,768]{1,0:T(8,128)S(1)}) custom-call(s32[2]{0:T(128)S(1)} %pad_add_fusion.1.core_ref, bf16[256,3072]{1,0:T(8,128)(2,1)} %get-tuple-element.283.up_back_ref, f32[256,768]{1,0:T(8,128)S(1)} %copy-done.12, ...), custom_call_target="tpu_custom_call" | custom-call | bytes 16777216 | tf_op jit(solution)/shard_map/pallas_call | solution.py:931
  429.3 6.3 shard_map.542.triple_back_ref
  440.8 5.2 shard_map.543
  472.3 10.5 %collective-permute-done.61 = bf16[4,112,384]{2,1,0:T(8,128)(2,1)S(1)} collective-permute-done((bf16[4,112,384]{2,1,0:T(8,128)(2,1)S(1)}, bf16[4,112,384]{2,1,0:T(8,128)(2,1)S(1)}, u32[]{:S(2)}, u32[]{:S(2)}) %collective-permute-start.61) | collective-permute-done | bytes 344096 | tf_op jit(solution)/shard_map/ppermute | solution.py:64
  482.8 13.2 %collective-permute-done.62 = bf16[4,112,384]{2,1,0:T(8,128)(2,1)S(1)} collective-permute-done((bf16[4,112,384]{2,1,0:T(8,128)(2,1)S(1)}, bf16[4,112,384]{2,1,0:T(8,128)(2,1)S(1)}, u32[]{:S(2)}, u32[]{:S(2)}) %collective-permute-start.62) | collective-permute-done | bytes 344096 | tf_op jit(solution)/shard_map/ppermute | solution.py:64
  520.3 8.7 %collective-permute-done.73 = f32[1,2,4,24,768]{4,3,2,1,0:T(8,128)S(1)} collective-permute-done((f32[1,2,4,24,768]{4,3,2,1,0:T(8,128)S(1)}, f32[1,2,4,24,768]{4,3,2,1,0:T(8,128)S(1)}, u32[]{:S(2)}, u32[]{:S(2)}) %collective-permute-start.73) | collective-permute-done | bytes 589856 | tf_op jit(solution)/shard_map/ppermute | solution.py:64
  531.7 5.7 collective-permute-start.70
  539.9 20.8 %shard_map.545 = (f32[192,6288]{1,0:T(8,128)}, f32[1,128]{1,0:T(1,128)}) custom-call(s32[4]{0:T(128)} %pad_add_fusion.spot_ref, s32[32]{0:T(128)} %copy-done.115, s32[32]{0:T(128)} %max.68.last_ref, s32[32,224]{1,0:T(8,128)} %fusion.32.ids_ref, bf16[16,112,384]{2,1,0:T(8,128)(2,1)} %copy-done.63, bf16[16,112,384]{2,1,0:T(8,128)(2,1)} %collective-permute-done.66.theirs_ref), custom_call_target="tpu_custom_call" | custom-call | bytes 52428800 | tf_op jit(solution)/shard_map/pallas_call | solution.py:437
  565.6 6.0 collective-permute-done.74
  579.4 5.5 collective-permute-start.76
  603.5 13.8 %fusion.1 = (f32[6288,192]{0,1:T(8,128)}, f32[192,6288]{1,0:T(8,128)}, f32[6288,192]{0,1:T(8,128)}) fusion(f32[6288,192]{0,1:T(8,128)} %param.53, f32[6288,192]{0,1:T(8,128)} %param.44, f32[]{:T(128)S(6)} %min.28, f32[192,6288]{1,0:T(8,128)} %get-tuple-element.326, f32[192]{0:T(256)S(1)} %bitcast.561, pred[6288]{0:T(1024)(128)(4,1)} %iota_compare_fusion, ...), kind=kLoop, calls=%fused_computation.2 | loop fusion | flops 13280256 | bytes 33811348 | tf_op jit(solution)/shard_map/transpose | solution.py:1533
  619.4 6.1 add_multiply_fusion
  (624 shorter events, 290.0 us)
Async XLA Ops:
  7.2 127.8 %all-gather.5.cloned.1.call-start = ((), (), s32[]{:S(2)}) async-start(), calls=%async_computation.1 | async-start | bytes 3932160 | tf_op jit(solution)/shard_map/all_gather | solution.py:141
  18.5 21.8 %collective-permute-start.5 = (bf16[24,5120]{1,0:T(8,128)(2,1)}, bf16[24,5120]{1,0:T(8,128)(2,1)S(1)}, u32[]{:S(2)}, u32[]{:S(2)}) collective-permute-start(bf16[24,5120]{1,0:T(8,128)(2,1)} %get-tuple-element.193), channel_id=1, source_target_pairs={{0,1},{1,0},{2,3},{3,2},{4,5},{5,4},{6,7},{7,6},{8,9},{9,8},{10,11... | collective-permute-start | bytes 737288 | tf_op jit(solution)/shard_map/ppermute | solution.py:64
  38.1 49.3 %collective-permute-start.13 = (bf16[2,192,1664]{2,1,0:T(8,128)(2,1)S(1)}, bf16[2,192,1664]{2,1,0:T(8,128)(2,1)}, u32[]{:S(2)}, u32[]{:S(2)}) collective-permute-start(bf16[2,192,1664]{2,1,0:T(8,128)(2,1)S(1)} %get-tuple-element.394), channel_id=1, source_target_pairs={{0,8},{1,9},{2,10},{3,11},{4,12},{5,13},{6,14},{7,15},{8,0},{9,1},... | collective-permute-start | bytes 3833864 | tf_op jit(solution)/shard_map/ppermute | solution.py:64
  60.0 126.1 %all-gather.7.cloned.1.call-start = ((), (), s32[]{:S(2)}) async-start(), calls=%async_computation.2 | async-start | bytes 2949120 | tf_op jit(solution)/shard_map/all_gather | solution.py:141
  60.4 25.5 %collective-permute-start.10 = (bf16[48,3072]{1,0:T(8,128)(2,1)S(1)}, bf16[48,3072]{1,0:T(8,128)(2,1)}, u32[]{:S(2)}, u32[]{:S(2)}) collective-permute-start(bf16[48,3072]{1,0:T(8,128)(2,1)S(1)} %slice.470), channel_id=1, source_target_pairs={{0,2},{1,3},{2,0},{3,1},{4,6},{5,7},{6,4},{7,5},{8,10},{9,11},{10,... | collective-permute-start | bytes 884744 | tf_op jit(solution)/shard_map/ppermute | solution.py:64
  63.9 23.5 %collective-permute-start.11 = (bf16[48,3072]{1,0:T(8,128)(2,1)S(1)}, bf16[48,3072]{1,0:T(8,128)(2,1)}, u32[]{:S(2)}, u32[]{:S(2)}) collective-permute-start(bf16[48,3072]{1,0:T(8,128)(2,1)S(1)} %slice.470), channel_id=1, source_target_pairs={{0,4},{1,5},{2,6},{3,7},{4,0},{5,1},{6,2},{7,3},{8,12},{9,13},{10,... | collective-permute-start | bytes 884744 | tf_op jit(solution)/shard_map/ppermute | solution.py:64
  64.9 22.6 %collective-permute-start.12 = (bf16[48,3072]{1,0:T(8,128)(2,1)S(1)}, bf16[48,3072]{1,0:T(8,128)(2,1)}, u32[]{:S(2)}, u32[]{:S(2)}) collective-permute-start(bf16[48,3072]{1,0:T(8,128)(2,1)S(1)} %slice.470), channel_id=1, source_target_pairs={{0,6},{1,7},{2,4},{3,5},{4,2},{5,3},{6,0},{7,1},{8,14},{9,15},{10,... | collective-permute-start | bytes 884744 | tf_op jit(solution)/shard_map/ppermute | solution.py:64
  93.6 21.2 %collective-permute-start.15 = (bf16[4,112,384]{2,1,0:T(8,128)(2,1)}, bf16[4,112,384]{2,1,0:T(8,128)(2,1)S(1)}, u32[]{:S(2)}, u32[]{:S(2)}) collective-permute-start(bf16[4,112,384]{2,1,0:T(8,128)(2,1)} %get-tuple-element.412), channel_id=1, source_target_pairs={{0,2},{1,3},{2,0},{3,1},{4,6},{5,7},{6,4},{7,5},{8,10},{9,11},{10,... | collective-permute-start | bytes 1032200 | tf_op jit(solution)/shard_map/ppermute | solution.py:64
  99.5 26.8 %collective-permute-start.16 = (bf16[4,112,384]{2,1,0:T(8,128)(2,1)}, bf16[4,112,384]{2,1,0:T(8,128)(2,1)S(1)}, u32[]{:S(2)}, u32[]{:S(2)}) collective-permute-start(bf16[4,112,384]{2,1,0:T(8,128)(2,1)} %get-tuple-element.411), channel_id=1, source_target_pairs={{0,4},{1,5},{2,6},{3,7},{4,0},{5,1},{6,2},{7,3},{8,12},{9,13},{10,... | collective-permute-start | bytes 1032200 | tf_op jit(solution)/shard_map/ppermute | solution.py:64
  100.5 25.8 %collective-permute-start.17 = (bf16[4,112,384]{2,1,0:T(8,128)(2,1)}, bf16[4,112,384]{2,1,0:T(8,128)(2,1)}, u32[]{:S(2)}, u32[]{:S(2)}) collective-permute-start(bf16[4,112,384]{2,1,0:T(8,128)(2,1)} %get-tuple-element.410), channel_id=1, source_target_pairs={{0,6},{1,7},{2,4},{3,5},{4,2},{5,3},{6,0},{7,1},{8,14},{9,15},{10,... | collective-permute-start | bytes 1032200 | tf_op jit(solution)/shard_map/ppermute | solution.py:64
  138.1 373.3 %reduce-scatter.4.cloned.1.call-start = ((), (), s32[]{:S(2)}) async-start(), calls=%async_computation.3 | async-start | bytes 5898240
  138.7 19.1 %collective-permute-start.25 = (bf16[2,4,48,768]{3,2,1,0:T(8,128)(2,1)S(1)}, bf16[2,4,48,768]{3,2,1,0:T(8,128)(2,1)}, u32[]{:S(2)}, u32[]{:S(2)}) collective-permute-start(bf16[2,4,48,768]{3,2,1,0:T(8,128)(2,1)S(1)} %pad_maximum_fusion.13), channel_id=1, source_target_pairs={{0,8},{1,9},{2,10},{3,11},{4,12},{5,13},{6,14},{7,15},{8,0},{9,1},... | collective-permute-start | bytes 1769480 | tf_op jit(solution)/shard_map/ppermute | solution.py:64
  140.2 18.8 %collective-permute-start.24 = (bf16[2,4,48,768]{3,2,1,0:T(8,128)(2,1)}, bf16[2,4,48,768]{3,2,1,0:T(8,128)(2,1)}, u32[]{:S(2)}, u32[]{:S(2)}) collective-permute-start(bf16[2,4,48,768]{3,2,1,0:T(8,128)(2,1)} %pad_maximum_fusion.12), channel_id=1, source_target_pairs={{0,16},{1,17},{2,18},{3,19},{4,20},{5,21},{6,22},{7,23},{8,24},{9,... | collective-permute-start | bytes 1769480 | tf_op jit(solution)/shard_map/ppermute | solution.py:64
  163.3 27.5 %collective-permute-start.26 = (bf16[768,1536]{1,0:T(8,128)(2,1)}, bf16[768,1536]{1,0:T(8,128)(2,1)}, u32[]{:S(2)}, u32[]{:S(2)}) collective-permute-start(bf16[768,1536]{1,0:T(8,128)(2,1)} %bitcast.61.mine), channel_id=1, source_target_pairs={{0,1},{1,0},{2,3},{3,2},{4,5},{5,4},{6,7},{7,6},{8,9},{9,8},{10,11... | collective-permute-start | bytes 7077896 | tf_op jit(solution)/shard_map/ppermute | solution.py:64
  207.3 30.5 %collective-permute-start.31 = (bf16[2,192,1664]{2,1,0:T(8,128)(2,1)S(1)}, bf16[2,192,1664]{2,1,0:T(8,128)(2,1)S(1)}, u32[]{:S(2)}, u32[]{:S(2)}) collective-permute-start(bf16[2,192,1664]{2,1,0:T(8,128)(2,1)S(1)} %pad_maximum_fusion.7), channel_id=1, source_target_pairs={{0,16},{1,17},{2,18},{3,19},{4,20},{5,21},{6,22},{7,23},{8,24},{9,... | collective-permute-start | bytes 3833864 | tf_op jit(solution)/shard_map/ppermute | solution.py:64
  208.9 29.1 %collective-permute-start.28 = (bf16[96,768]{1,0:T(8,128)(2,1)S(1)}, bf16[96,768]{1,0:T(8,128)(2,1)S(1)}, u32[]{:S(2)}, u32[]{:S(2)}) collective-permute-start(bf16[96,768]{1,0:T(8,128)(2,1)S(1)} %get-tuple-element.252), channel_id=1, source_target_pairs={{0,2},{1,3},{2,0},{3,1},{4,6},{5,7},{6,4},{7,5},{8,10},{9,11},{10,... | collective-permute-start | bytes 442376 | tf_op jit(solution)/shard_map/ppermute | solution.py:64
  210.3 27.7 %collective-permute-start.29 = (bf16[96,768]{1,0:T(8,128)(2,1)S(1)}, bf16[96,768]{1,0:T(8,128)(2,1)S(1)}, u32[]{:S(2)}, u32[]{:S(2)}) collective-permute-start(bf16[96,768]{1,0:T(8,128)(2,1)S(1)} %get-tuple-element.252), channel_id=1, source_target_pairs={{0,4},{1,5},{2,6},{3,7},{4,0},{5,1},{6,2},{7,3},{8,12},{9,13},{10,... | collective-permute-start | bytes 442376 | tf_op jit(solution)/shard_map/ppermute | solution.py:64
  212.7 25.3 %collective-permute-start.30 = (bf16[96,768]{1,0:T(8,128)(2,1)S(1)}, bf16[96,768]{1,0:T(8,128)(2,1)S(1)}, u32[]{:S(2)}, u32[]{:S(2)}) collective-permute-start(bf16[96,768]{1,0:T(8,128)(2,1)S(1)} %get-tuple-element.252), channel_id=1, source_target_pairs={{0,6},{1,7},{2,4},{3,5},{4,2},{5,3},{6,0},{7,1},{8,14},{9,15},{10,... | collective-permute-start | bytes 442376 | tf_op jit(solution)/shard_map/ppermute | solution.py:64
  369.6 29.5 %collective-permute-start.52 = (bf16[2,192,1664]{2,1,0:T(8,128)(2,1)}, bf16[2,192,1664]{2,1,0:T(8,128)(2,1)}, u32[]{:S(2)}, u32[]{:S(2)}) collective-permute-start(bf16[2,192,1664]{2,1,0:T(8,128)(2,1)} %get-tuple-element.388), channel_id=1, source_target_pairs={{0,8},{1,9},{2,10},{3,11},{4,12},{5,13},{6,14},{7,15},{8,0},{9,1},... | collective-permute-start | bytes 3833864 | tf_op jit(solution)/shard_map/ppermute | solution.py:64
  438.1 25.9 %collective-permute-start.58 = (bf16[768,1536]{1,0:T(8,128)(2,1)}, bf16[768,1536]{1,0:T(8,128)(2,1)}, u32[]{:S(2)}, u32[]{:S(2)}) collective-permute-start(bf16[768,1536]{1,0:T(8,128)(2,1)} %pad_maximum_fusion.4), channel_id=1, source_target_pairs={{0,1},{1,0},{2,3},{3,2},{4,5},{5,4},{6,7},{7,6},{8,9},{9,8},{10,11... | collective-permute-start | bytes 7077896 | tf_op jit(solution)/shard_map/ppermute | solution.py:64
  466.4 29.7 %collective-permute-start.65 = (bf16[2,4,48,768]{3,2,1,0:T(8,128)(2,1)S(1)}, bf16[2,4,48,768]{3,2,1,0:T(8,128)(2,1)S(1)}, u32[]{:S(2)}, u32[]{:S(2)}) collective-permute-start(bf16[2,4,48,768]{3,2,1,0:T(8,128)(2,1)S(1)} %get-tuple-element.428), channel_id=1, source_target_pairs={{0,8},{1,9},{2,10},{3,11},{4,12},{5,13},{6,14},{7,15},{8,0},{9,1},... | collective-permute-start | bytes 1769480 | tf_op jit(solution)/shard_map/ppermute | solution.py:64
  467.2 28.9 %collective-permute-start.64 = (bf16[2,4,48,768]{3,2,1,0:T(8,128)(2,1)S(1)}, bf16[2,4,48,768]{3,2,1,0:T(8,128)(2,1)S(1)}, u32[]{:S(2)}, u32[]{:S(2)}) collective-permute-start(bf16[2,4,48,768]{3,2,1,0:T(8,128)(2,1)S(1)} %get-tuple-element.430), channel_id=1, source_target_pairs={{0,16},{1,17},{2,18},{3,19},{4,20},{5,21},{6,22},{7,23},{8,24},{9,... | collective-permute-start | bytes 1769480 | tf_op jit(solution)/shard_map/ppermute | solution.py:64
  469.4 26.6 %collective-permute-start.62 = (bf16[4,112,384]{2,1,0:T(8,128)(2,1)S(1)}, bf16[4,112,384]{2,1,0:T(8,128)(2,1)S(1)}, u32[]{:S(2)}, u32[]{:S(2)}) collective-permute-start(bf16[4,112,384]{2,1,0:T(8,128)(2,1)S(1)} %pad_maximum_fusion.20), channel_id=1, source_target_pairs={{0,4},{1,5},{2,6},{3,7},{4,0},{5,1},{6,2},{7,3},{8,12},{9,13},{10,... | collective-permute-start | bytes 1032200 | tf_op jit(solution)/shard_map/ppermute | solution.py:64
  471.8 24.3 %collective-permute-start.63 = (bf16[4,112,384]{2,1,0:T(8,128)(2,1)S(1)}, bf16[4,112,384]{2,1,0:T(8,128)(2,1)S(1)}, u32[]{:S(2)}, u32[]{:S(2)}) collective-permute-start(bf16[4,112,384]{2,1,0:T(8,128)(2,1)S(1)} %pad_maximum_fusion.20), channel_id=1, source_target_pairs={{0,6},{1,7},{2,4},{3,5},{4,2},{5,3},{6,0},{7,1},{8,14},{9,15},{10,... | collective-permute-start | bytes 1032200 | tf_op jit(solution)/shard_map/ppermute | solution.py:64
  517.6 45.6 %collective-permute-start.75 = (bf16[2,192,1664]{2,1,0:T(8,128)(2,1)}, bf16[2,192,1664]{2,1,0:T(8,128)(2,1)}, u32[]{:S(2)}, u32[]{:S(2)}) collective-permute-start(bf16[2,192,1664]{2,1,0:T(8,128)(2,1)} %pad_maximum_fusion.8), channel_id=1, source_target_pairs={{0,16},{1,17},{2,18},{3,19},{4,20},{5,21},{6,22},{7,23},{8,24},{9,... | collective-permute-start | bytes 3833864 | tf_op jit(solution)/shard_map/ppermute | solution.py:64
  530.2 41.5 %collective-permute-start.74 = (f32[2,2,4,24,768]{4,3,2,1,0:T(8,128)}, f32[2,2,4,24,768]{4,3,2,1,0:T(8,128)}, u32[]{:S(2)}, u32[]{:S(2)}) collective-permute-start(f32[2,2,4,24,768]{4,3,2,1,0:T(8,128)} %pad_maximum_fusion.9), channel_id=1, source_target_pairs={{0,16},{1,17},{2,18},{3,19},{4,20},{5,21},{6,22},{7,23},{8,24},{9,... | collective-permute-start | bytes 3538952 | tf_op jit(solution)/shard_map/ppermute | solution.py:64
  531.7 41.6 %collective-permute-start.70 = (bf16[48,4608]{1,0:T(8,128)(2,1)}, bf16[48,4608]{1,0:T(8,128)(2,1)}, u32[]{:S(2)}, u32[]{:S(2)}) collective-permute-start(bf16[48,4608]{1,0:T(8,128)(2,1)} %get-tuple-element.408), channel_id=1, source_target_pairs={{0,2},{1,3},{2,0},{3,1},{4,6},{5,7},{6,4},{7,5},{8,10},{9,11},{10,... | collective-permute-start | bytes 1327112 | tf_op jit(solution)/shard_map/ppermute | solution.py:64
  537.5 35.9 %collective-permute-start.71 = (bf16[48,4608]{1,0:T(8,128)(2,1)S(1)}, bf16[48,4608]{1,0:T(8,128)(2,1)}, u32[]{:S(2)}, u32[]{:S(2)}) collective-permute-start(bf16[48,4608]{1,0:T(8,128)(2,1)S(1)} %get-tuple-element.407), channel_id=1, source_target_pairs={{0,4},{1,5},{2,6},{3,7},{4,0},{5,1},{6,2},{7,3},{8,12},{9,13},{10,... | collective-permute-start | bytes 1327112 | tf_op jit(solution)/shard_map/ppermute | solution.py:64
  538.3 35.1 %collective-permute-start.72 = (bf16[48,4608]{1,0:T(8,128)(2,1)S(1)}, bf16[48,4608]{1,0:T(8,128)(2,1)}, u32[]{:S(2)}, u32[]{:S(2)}) collective-permute-start(bf16[48,4608]{1,0:T(8,128)(2,1)S(1)} %get-tuple-element.406), channel_id=1, source_target_pairs={{0,6},{1,7},{2,4},{3,5},{4,2},{5,3},{6,0},{7,1},{8,14},{9,15},{10,... | collective-permute-start | bytes 1327112 | tf_op jit(solution)/shard_map/ppermute | solution.py:64
  588.3 38.9 %collective-permute-start.85 = (f32[96,384]{1,0:T(8,128)}, f32[96,384]{1,0:T(8,128)}, u32[]{:S(2)}, u32[]{:S(2)}) collective-permute-start(f32[96,384]{1,0:T(8,128)} %dynamic-slice_bitcast_fusion.20), channel_id=1, source_target_pairs={{0,1},{1,0},{2,3},{3,2},{4,5},{5,4},{6,7},{7,6},{8,9},{9,8},{10,11... | collective-permute-start | bytes 442376 | tf_op jit(solution)/shard_map/ppermute | solution.py:64
  588.3 41.0 %collective-permute-start.84 = (f32[24,1536]{1,0:T(8,128)S(1)}, f32[24,1536]{1,0:T(8,128)}, u32[]{:S(2)}, u32[]{:S(2)}) collective-permute-start(f32[24,1536]{1,0:T(8,128)S(1)} %dynamic-slice_bitcast_fusion.21), channel_id=1, source_target_pairs={{0,1},{1,0},{2,3},{3,2},{4,5},{5,4},{6,7},{7,6},{8,9},{9,8},{10,11... | collective-permute-start | bytes 442376 | tf_op jit(solution)/shard_map/ppermute | solution.py:64
  595.0 31.2 %collective-permute-start.83 = (f32[24,1536]{1,0:T(8,128)}, f32[24,1536]{1,0:T(8,128)}, u32[]{:S(2)}, u32[]{:S(2)}) collective-permute-start(f32[24,1536]{1,0:T(8,128)} %dynamic-slice_bitcast_fusion.22), channel_id=1, source_target_pairs={{0,1},{1,0},{2,3},{3,2},{4,5},{5,4},{6,7},{7,6},{8,9},{9,8},{10,11... | collective-permute-start | bytes 442376 | tf_op jit(solution)/shard_map/ppermute | solution.py:64
  (182 other events, 1411.7 us)
Sparse Core Ops, SparseCore 0:
  60.1 45.9 all-gather.4
  138.3 47.7 all-gather.6
  426.3 69.4 reduce-scatter.3

commit v3 on v2

--- a/solution.py
+++ b/solution.py
@@ -108,17 +108,10 @@
             pieces += [further[n] for n in range(self.size("v"))]
         return pieces
 
-    def doubled(self, value, axis):
-        place, step, shape = self.place(axis), 1, value.shape
-        value = value[None]
-        while step < self.size(axis):
-            came = self.hop(value, axis, step)
-            upper = (place // step) % 2 == 1
-            value = jnp.concatenate(
-                [jnp.where(upper, came, value), jnp.where(upper, value, came)], 0
-            )
-            step *= 2
-        return value.reshape((self.size(axis),) + shape)
+    def doubled(self, value, axis, step):
+        came = self.hop(value, axis, step)
+        upper = (self.place(axis) // step) % 2 == 1
+        return jnp.concatenate([jnp.where(upper, came, value), jnp.where(upper, value, came)], 0)
 
 
     def half(self, value, other=False):
@@ -151,8 +144,8 @@
         )
 
     def across_done(self, sides):
-        block = jnp.concatenate([self.piled(sides[0], "u"), self.piled(sides[1], "v", 1)], -1)
-        return block.reshape(-1, block.shape[-1])
+        blocks = self.piled(sides[0], "u"), self.piled(sides[1], "v", 1)
+        return [block.reshape(-1, block.shape[-1]) for block in blocks]
 
 
     def summed(self, state):
@@ -329,7 +322,8 @@
 
 def add_up_plain(spot, first, last, ids, mine, theirs, span, grid):
     count, kept = ids.shape
-    rows = jnp.stack([mine, theirs]).reshape(grid[::-1] + mine.shape[1:])
+    rows = jnp.stack([mine, theirs])[:, :, : kept // 2]
+    rows = rows.reshape(grid[::-1] + rows.shape[2:])
     rows = by_steps(rows.transpose(2, 1, 0, 3, 4), spot, grid)
     rows = jnp.swapaxes(rows.reshape(count, kept // 2, 2, -1), 1, 2).astype(wide)
     places = jnp.where(owned(first, last, ids), ids - spot[3], span).reshape(-1)
@@ -376,15 +370,15 @@
     span = out_ref.shape[1]
     sum_ref[...] = jnp.zeros_like(sum_ref)
     base = spot_ref[3]
-    half, width, count = mine_ref.shape[1], mine_ref.shape[2] // 2, mine_ref.shape[0]
+    half, width, count = ids_ref.shape[1] // 2, mine_ref.shape[2] // 2, mine_ref.shape[0]
     kept = 2 * half
     for n, in_ref in enumerate((mine_ref, theirs_ref)):
 
         def widen(b, carry):
             at = pl.multiple_of((n * count + b) * kept, 16)
             rows = in_ref[b].astype(wide)
-            wide_ref[pl.ds(at, half), :] = rows[:, :width]
-            wide_ref[pl.ds(at + half, half), :] = rows[:, width:]
+            wide_ref[pl.ds(at, half), :] = rows[:half, :width]
+            wide_ref[pl.ds(at + half, half), :] = rows[:half, width:]
             return carry
 
         lax.fori_loop(0, count, widen, 0)
@@ -599,55 +593,33 @@
     )(first, second, masked, mask_row[None, :], *pieces)
 
 
-def tell_kernel(core_ref, sums_1, sums_2, sums_3, ada_ref, hidden_ref, before_ref, out_ref):
-    sums_1, sums_2, sums_3 = sums_1[...], sums_2[...], sums_3[...]
-    rows = [sums_1[n : n + 1] for n in (1, 2)] + [sums_2[n : n + 1] for n in (3, 1, 2)]
-    rows += [sums_3[n : n + 1] for n in (3, 1, 2)]
-    which = iota(sums_1.shape, 0)
-    mods = jnp.zeros(sums_1.shape, wide)
-    for n, row in enumerate(rows):
-        mods = jnp.where(which == n, row, mods)
-    columns, width = mods.T, mods.shape[1]
-    total = jnp.zeros((8, ada_ref.shape[1]), wide)
-    for n in range(8):
-        part = columns[:, n : n + 1] * ada_ref[n * width : (n + 1) * width, :].astype(wide)
-        total = total + jnp.sum(part.reshape(-1, 8, part.shape[1]), 0)
-    slope = jnp.sum(total, 0, keepdims=True)
-    before = before_ref[...]
-    gate = 1.0 / (1.0 + jnp.exp(-before))
-    slope = slope * (gate + before * gate * (1.0 - gate))
-    out_ref[...] = jnp.zeros_like(out_ref)
-    out_ref[0:8, :] = mods
-    out_ref[8:12, :] = sums_1[0:4]
-    out_ref[12:16, :] = sums_2[0:4]
-    out_ref[16:20, :] = sums_3[0:4]
-    out_ref[20:21, : slope.shape[1]] = hidden_ref[...]
-    out_ref[21:22, : slope.shape[1]] = slope
-
-
-def tell(sums_1, sums_2, sums_3, ada, hidden_time, before_time):
-    (rows,) = kernel_call(
-        tell_kernel,
-        jnp.zeros((1,), jnp.int32),
-        (sums_1, sums_2, sums_3, ada, hidden_time, before_time),
-        (((24, sums_1.shape[1]), wide),),
-    )
-    return rows
+def tail_rows(width, cond):
+    return -(-(6 + (1 if 2 * cond <= width else 2 * -(-cond // width))) // 8) * 8
+
+
+def tail_places(width, cond):
+    if 2 * cond <= width:
+        return [[(6, slice(n * cond, (n + 1) * cond), 0)] for n in range(2)]
+    per = -(-cond // width)
+    return [
+        [
+            (6 + n * per + k, slice(0, min(width, cond - k * width)), k * width)
+            for k in range(per)
+        ]
+        for n in range(2)
+    ]
 
 
 def finish_kernel(
-    scalar_ref, vectors_ref, spectrum_ref, ada_ref, time_ref, gains_ref, mask_ref, square_ref
+    scalar_ref, tails_ref, spectrum_ref, ada_ref, time_ref, gains_ref, mask_ref, square_ref
 ):
-    device, width = scalar_ref[0], vectors_ref.shape[2]
-    size = ada_ref.shape[0]
-    row = lax.div(device, width // size)
-    mods = vectors_ref[:, 0, :]
-    for n in range(1, 8):
-        mods = jnp.where(row == n, vectors_ref[:, n, :], mods)
+    place, width = scalar_ref[0], tails_ref.shape[2]
+    size, cond, half = ada_ref.shape[0], ada_ref.shape[1], mask_ref.shape[1]
 
     def chosen(values, at, count):
-        place = (iota((width, count), 0) == iota((width, count), 1) + at).astype(wide)
-        return jnp.dot(values, place, precision=highest, preferred_element_type=wide)
+        span = values.shape[1]
+        spot = (iota((span, count), 0) == iota((span, count), 1) + at).astype(wide)
+        return jnp.dot(values, spot, precision=highest, preferred_element_type=wide)
 
     def times(left, right):
         return lax.dot_general(
@@ -658,18 +630,24 @@
             preferred_element_type=wide,
         )
 
-    cond = ada_ref.shape[1]
-    mods = chosen(mods, lax.rem(device, width // size) * size, size)
-    ada_ref[...] = times(mods, vectors_ref[:, 20, :cond])
-    time_ref[...] = times(spectrum_ref[...], vectors_ref[:, 21, :cond])
-    rows = [jnp.sum(vectors_ref[:, n, :], 0, keepdims=True) for n in (8, 12, 16, 11)]
-    which = iota((8, width), 0)
-    block = jnp.zeros((8, width), wide)
+    def vector(n):
+        parts = [tails_ref[:, row, lanes] for row, lanes, _ in tail_places(width, cond)[n]]
+        return parts[0] if len(parts) == 1 else jnp.concatenate(parts, 1)
+
+    row = lax.div(place * size, width)
+    mods = tails_ref[:, 0, :]
+    for n in range(1, 4):
+        mods = jnp.where(row == n, tails_ref[:, n, :], mods)
+    ada_ref[...] = times(chosen(mods, lax.rem(place * size, width), size), vector(0))
+    time_ref[...] = times(spectrum_ref[...], vector(1))
+    sums = [jnp.sum(tails_ref[:, n, :], 0, keepdims=True) for n in (4, 5)]
+    rows = (sums[0][:, :half], sums[0][:, half:], sums[1][:, :half])
+    which = iota((8, half), 0)
+    block = jnp.zeros((8, half), wide)
     for n, values in enumerate(rows):
         block = jnp.where(which == n, values, block)
-    gains_ref[...] = chosen(block, device * gains_ref.shape[1], gains_ref.shape[1])[:3]
-    mask = chosen(block, scalar_ref[1] * mask_ref.shape[1], mask_ref.shape[1])[3:4]
-    mask_ref[...] = mask * scalar_ref[2].astype(wide)
+    gains_ref[...] = chosen(block, place * gains_ref.shape[1], gains_ref.shape[1])[:3]
+    mask_ref[...] = sums[1][:, half:] * scalar_ref[1].astype(wide)
     total = sum(
         jnp.sum(jnp.sum(ref[...] * ref[...], 0, keepdims=True), 1, keepdims=True)
         for ref in (ada_ref, time_ref, gains_ref, mask_ref)
@@ -677,11 +655,11 @@
     square_ref[...] = jnp.broadcast_to(total, square_ref.shape)
 
 
-def finish(scalars, vectors, spectrum, ada_rows, cond, gain_width, mask_width):
+def finish(scalars, tails, spectrum, ada_rows, cond, gain_width, mask_width):
     return kernel_call(
         finish_kernel,
         scalars,
-        (vectors, spectrum),
+        (tails, spectrum),
         (
             ((ada_rows, cond), wide),
             ((spectrum.shape[1], cond), wide),
@@ -710,7 +688,7 @@
     return info[:, n : n + 1]
 
 
-ROW_BLOCK = 256
+ROW_BLOCK = 512
 
 
 def split_kernel(columns, place_ref, in_ref, out_ref):
@@ -1151,20 +1129,54 @@
     theirs,
     collect_ref,
     masked_ref,
+    sums_2,
+    sums_3,
+    ada_ref,
+    hidden_ref,
+    before_ref,
     sent_ref,
-    sums_ref,
     pair_ref,
 ):
     slope = product_back(core_ref, triple_back_ref, mine[:, :cut], theirs[:, :cut])
     slope, sums = norm_back(start_ref[...], slope, mods, gains, 0, 0)
     slope = (mid_back_ref[...] + slope).astype(low)
     mask = jnp.sum(masked_ref[...] * slope.astype(wide), 0, keepdims=True)
-    store_rows(sums_ref, sums + (mask,))
     rows = jnp.dot(collect_ref[...], slope, preferred_element_type=wide)
-    half, width = sent_ref.shape[1], sent_ref.shape[2] // 2
+    half, width = collect_ref.shape[0] // 2, sent_ref.shape[2] // 2
+
+    sums_2, sums_3 = sums_2[...], sums_3[...]
+    parts = list(sums[1:3]) + [sums_2[n : n + 1] for n in (3, 1, 2)]
+    parts += [sums_3[n : n + 1] for n in (3, 1, 2)]
+    which = iota(sums_2.shape, 0)
+    grad_mods = jnp.zeros(sums_2.shape, wide)
+    for n, part in enumerate(parts):
+        grad_mods = jnp.where(which == n, part, grad_mods)
+    columns, model_width = grad_mods.T, grad_mods.shape[1]
+    total = jnp.zeros((8, ada_ref.shape[1]), wide)
+    for n in range(8):
+        part = columns[:, n : n + 1] * ada_ref[n * model_width : (n + 1) * model_width, :].astype(wide)
+        total = total + jnp.sum(part.reshape(-1, 8, part.shape[1]), 0)
+    before = before_ref[...]
+    gate = 1.0 / (1.0 + jnp.exp(-before))
+    back = jnp.sum(total, 0, keepdims=True) * (gate + before * gate * (1.0 - gate))
+    ends = (hidden_ref[...], back)
+    fours = (sums[0], sums_2[0:1], sums_3[0:1], mask)
+    pair_ref[...] = jnp.zeros_like(pair_ref)
+    for values, places in zip(ends, tail_places(2 * width, back.shape[1])):
+        for row, lanes, start in places:
+            size = lanes.stop - lanes.start
+            pair_ref[half + row : half + row + 1, lanes] = values[:, start : start + size]
     for n in range(sent_ref.shape[0]):
-        pair_ref[:, :width] = rows[:half, n * width : (n + 1) * width]
-        pair_ref[:, width:] = rows[half:, n * width : (n + 1) * width]
+        at = slice(n * width, (n + 1) * width)
+        pair_ref[:half, :width] = rows[:half, at]
+        pair_ref[:half, width:] = rows[half:, at]
+        for k in range(4):
+            start = (4 * n + k) * 2 * width
+            row, lane = start // model_width, start % model_width
+            pair_ref[half + k : half + k + 1, :] = grad_mods[row : row + 1, lane : lane + 2 * width]
+            lanes = slice((k % 2) * width, (k % 2 + 1) * width)
+            row = half + 4 + k // 2
+            pair_ref[row : row + 1, lanes] = fours[k][:, at]
         sent_ref[core_ref[1] ^ n] = pair_ref[...].astype(low)
 
 
@@ -1241,12 +1253,13 @@
     dp_place = dp_index.astype(jnp.int32)[None]
     small_z = links.heard(small, "z")
     head_slots = split_head(links, dp_place, head_table, piece)
-    small_z, head_slots, table = tie(small_z, head_slots, embedding)
-    small_dp = links.doubled(links.piled(small_z, "z"), "dp")
     a_z = links.heard(pair_a, "z")
-    table = turned(table.T)
-    small_dp, table, a_z = tie(small_dp, table, a_z)
+    table = turned(embedding.T)
+    small_z, head_slots, a_z, table = tie(small_z, head_slots, a_z, table)
     a_mine = links.wide_across(a_z)
+    small_dp, step = links.piled(small_z, "z")[None], 1
+    while step < dp_count:
+        small_dp, step = links.doubled(small_dp, "dp", step), 2 * step
     small_c = links.heard(small_dp, "c")
     head_came = links.exchange(head_slots)
     small_c, pair_bc = tie(small_c, pair_bc)
@@ -1254,6 +1267,23 @@
 
     numbers = links.piled(small_c, "c", 2).reshape((device_count,) + small.shape)
     ids_all = numbers[:, 0, :kept_count].astype(jnp.int32)
+
+    first = jnp.sum((ids_all < vocab_index * span).astype(jnp.int32), 1)
+    stop_id = jnp.minimum((vocab_index + 1) * span, mask_id)
+    last = jnp.maximum(jnp.sum((ids_all < stop_id).astype(jnp.int32), 1), first)
+    spot = jnp.stack(
+        [dp_index, links.place("z"), links.place("c"), vocab_index * span]
+    ).astype(jnp.int32)
+    grid = (dp_count, links.size("z"), links.size("c"))
+    looked = look_up(spot, first, last, ids_all, table, grid)
+    looked, bc_z, head_came, numbers = tie(looked, bc_z, head_came, numbers)
+    looked_c = looked[0], [links.hop(looked[1], "c", 1)]
+    looked = links.summed(looked_c).astype(low)
+    looked = looked.reshape((grid[1], grid[0]) + looked.shape[1:])
+    looked_z = links.near(looked, "z")
+    half_up = w_up.shape[1] // 2
+    bc_first = links.across_first(bc_z, half_up)
+
     targets = numbers[:, 1, :slot_count].astype(jnp.int32)
     levels = numbers[:, 2, 0]
     mask_row_full = jnp.sum(
@@ -1263,23 +1293,6 @@
     time_weight = numbers[:, 8 : 8 + w_time.shape[0], :cond_width].reshape(-1, cond_width)
     live = (targets >= 0).astype(wide)
     masked_count = jnp.sum(live)
-
-    first = jnp.sum((ids_all < vocab_index * span).astype(jnp.int32), 1)
-    stop_id = jnp.minimum((vocab_index + 1) * span, mask_id)
-    last = jnp.maximum(jnp.sum((ids_all < stop_id).astype(jnp.int32), 1), first)
-    spot = jnp.stack(
-        [dp_index, links.place("z"), links.place("c"), vocab_index * span]
-    ).astype(jnp.int32)
-    grid = (dp_count, links.size("z"), links.size("c"))
-    looked = look_up(spot, first, last, ids_all, table, grid)
-    looked, bc_z, head_came = tie(looked, bc_z, head_came)
-    looked_c = looked[0], [links.hop(looked[1], "c", 1)]
-    looked = links.summed(looked_c).astype(low)
-    looked = looked.reshape((grid[1], grid[0]) + looked.shape[1:])
-    looked_z = links.near(looked, "z")
-    half_up = w_up.shape[1] // 2
-    b_first = links.across_first([piece[:, :half_up] for piece in bc_z], half_cut(half_up))
-    c_mine = links.wide_across([laid_out(piece[:, half_up:], 2, rows, width_c) for piece in bc_z])
 
     by_core = lambda values: jnp.moveaxis(
         values.reshape(dp_count * links.size("z"), links.size("c"), -1), 1, 0
@@ -1300,11 +1313,11 @@
     spectrum_rows = lax.dynamic_slice_in_dim(
         features(levels, FREQ), device_index * time_rows, time_rows, 1
     )
-    spectrum_rows = spectrum_rows.reshape(grid + (time_rows,))
-    spectrum_rows = jnp.swapaxes(spectrum_rows, 1, 2).reshape(device_count, time_rows)
+    spectrum_rows = by_steps(spectrum_rows.reshape(grid + (time_rows,)), spot, grid)
+    spectrum_rows = spectrum_rows.transpose(2, 1, 0, 3).reshape(device_count, time_rows)
     early = (hidden_time, gains, mask_row_full, target_local, row_share, scalars, spectrum_rows)
-    looked_z, early, b_first = tie(looked_z, early, b_first)
-    b_second = links.across_second(b_first)
+    looked_z, early, bc_first = tie(looked_z, early, bc_first)
+    bc_second = links.across_second(bc_first)
     hidden_time, gains, mask_row_full, target_local, row_share, scalars, spectrum_rows = early
     looked = links.summed((looked_z[0], looked_z[1:])).astype(low)
     looked_dp = links.near(looked, "dp")
@@ -1329,14 +1342,15 @@
         ((square, low), ((length, qkv_width), low)),
     )
     (attended,) = kernel_call(attend_kernel, here, (triple, segment_ids), ((square, low),))
-    attended, b_second = tie(attended, b_second)
+    attended, bc_second = tie(attended, bc_second)
+    b_mine, c_mine = links.across_done(bc_second)
+    c_mine = laid_out(c_mine, device_count, rows, width_c)
     branch_a, hidden_mid, normed_b = kernel_call(
         functools.partial(out_kernel, ends[1:3]),
         here,
         (attended, hidden_start, mods, gains, a_mine, a_other),
         ((square, wide), (square, wide), (square, low)),
     )
-    b_mine = links.across_done(b_second)
     b_other = links.hop(b_mine, "c", 1)
     c_other = links.hop(c_mine, "c", 1)
     up_values, active = kernel_call(
@@ -1357,7 +1371,7 @@
     head = jnp.concatenate(links.ordered(head_pieces, "dp"), 0)
     rows_first = links.across_first(picked_z, cut_rows)
     rows_second = links.across_second(rows_first)
-    rows_mine = links.across_done(rows_second)
+    rows_mine = jnp.concatenate(links.across_done(rows_second), 1)
     rows_theirs = links.hop(rows_mine, "c", 1)
     values, stats = head_logits(scalars, rows_mine, rows_theirs, head, target_local)
     stats = links.total(stats, join_stats)
@@ -1373,9 +1387,9 @@
     grad_head, head_squares = head_grads(links, scalars, rows_mine, rows_theirs, slopes)
     rows_fold, grad_head = tie(rows_fold, grad_head)
     rows_fold = links.fold_second(rows_fold)
-    rows_fold, grad_head = tie(rows_fold, grad_head)
+    rows_fold, grad_head = tie(links.fold_third(rows_fold), grad_head)
+    grad_mine = links.summed(links.fold_z(rows_fold)).astype(low)
     back_came = links.exchange(grad_head)
-    grad_mine = links.summed(links.fold_z(links.fold_third(rows_fold))).astype(low)
 
     def weight_given(left_matrix, slopes):
         return times_rows(left_matrix, links.half(slopes, True)).astype(low)
@@ -1433,7 +1447,8 @@
         (((length, qkv_width), low),),
         megabytes=16,
     )
-    sent, sums_1 = kernel_call(
+    sent_rows = kept_count // 2 + tail_rows(2 * slice_width, cond_width)
+    (sent,) = kernel_call(
         functools.partial(start_back_kernel, ends[1]),
         here,
         (
@@ -1446,21 +1461,21 @@
             a_other,
             collect,
             masked,
+            sums_2,
+            sums_3,
+            ada_weight,
+            hidden_time,
+            before_time,
         ),
-        (
-            ((dp_count, kept_count // 2, 2 * slice_width), low),
-            ((8, model_width), wide),
-        ),
-        [pltpu.VMEM((kept_count // 2, 2 * slice_width), wide)],
+        (((dp_count, sent_rows, 2 * slice_width), low),),
+        [pltpu.VMEM((sent_rows, 2 * slice_width), wide)],
         megabytes=16,
     )
 
     start_dp = links.near(sent, "dp")
     a_given = [weight_given(normed_a, grad_triple), weight_given(attended, grad_branch_a)]
     a_came = links.hop(jnp.concatenate(a_given, 1), "c", 1)
-    vector = tell(sums_1, sums_2, sums_3, ada_weight, hidden_time, before_time)
-    vector = links.doubled(vector, "z")
-    start_dp, a_came, vector = tie(start_dp, a_came, vector)
+    start_dp, a_came = tie(start_dp, a_came)
     start_z = links.heard(jnp.stack(start_dp), "z")
     a_own = [weight_own(normed_a, grad_triple), weight_own(attended, grad_branch_a)]
     a_sum = (jnp.concatenate(a_own, 1) + a_came.astype(wide)).astype(low)
@@ -1469,19 +1484,17 @@
     start_mine = jnp.concatenate(start_z, 0)
     start_theirs = links.hop(start_mine, "c", 1)
     a_fold = links.fold_second(a_fold)
-    vector = links.heard(vector, "c")
-    start_theirs, a_fold, layer_wide, back_came, vector = tie(
-        start_theirs, a_fold, layer_wide, back_came, vector
-    )
-    vectors = links.doubled(links.piled(vector, "c"), "dp")
-    vectors = vectors.reshape((device_count,) + vectors.shape[3:])
+    start_theirs, a_fold, layer_wide, back_came = tie(
+        start_theirs, a_fold, layer_wide, back_came
+    )
     back_pieces = links.exchanged(back_came)
     a_block = links.fold_third(a_fold)
     all_fold = links.fold_z(jnp.concatenate([a_block, layer_wide], 2))
     grad_table, table_squares = add_up(
         spot, first, last, ids_all, start_mine, start_theirs, span, grid
     )
-    grad_table, all_fold, vectors, back_pieces = tie(grad_table, all_fold, vectors, back_pieces)
+    tails = jnp.concatenate([start_mine[:, kept_count // 2 :], start_theirs[:, kept_count // 2 :]], 0)
+    grad_table, all_fold = tie(grad_table, all_fold)
     all_sums = links.summed(all_fold)
     cuts = (0, a_block.shape[2], a_block.shape[2] + half_up, all_sums.shape[1])
     sum_a, sum_up, sum_down = [all_sums[:, cuts[n] : cuts[n + 1]] for n in range(3)]
@@ -1493,8 +1506,8 @@
     grad_out = jnp.concatenate([side[:, ends[1] :] for side in grad_a], 1)
     grad_head = jnp.concatenate(links.ordered(back_pieces, "dp"), 1)[:, :columns].astype(wide)
     grad_ada, grad_time, grad_gain_rows, mask_grad_own, small_square = finish(
-        jnp.stack([device_index, dp_index, mask_owner.astype(jnp.int32)]).astype(jnp.int32),
-        vectors,
+        jnp.stack([vocab_index, mask_owner]).astype(jnp.int32),
+        tails.astype(wide),
         spectrum_rows,
         w_ada.shape[1],
         cond_width,

time: 651 us -> 613 us (0.942)
  waiting for transfers between devices: 199 us -> 172 us
  local copies, waits for them, and re-layouts: 59.2 us -> 48.4 us
    all_gather x2 -> x1, waiting for transfers between devices: 22.8 us -> 0.01 us  [wide_across(): block = lax.all_gather(self.piled(pieces, 'z'), 'dp', axis=0, tiled=False)]
    another operation x24 -> x26, other arithmetic: 8.65 us -> 15 us  [piled(): return jnp.stack(self.ordered(pieces, axis), dim)]
    ppermute x86 -> x81, waiting for transfers between devices: 176 us -> 172 us  [hop(): return lax.ppermute(value, ('dp', 'vocab'), pairs)]
    ppermute x86 -> x81, starting transfers between devices: 104 us -> 107 us  [hop(): return lax.ppermute(value, ('dp', 'vocab'), pairs)]
    pallas_call x11 -> x10, Pallas kernels: 54.2 us -> 53.2 us  [kernel_call(): pl.pallas_call(kernel, out_shape=out, in_specs=[pl.BlockSpec(memory_space...]
    unnamed x259 -> x221, local copies, waits for them, and re-layouts: 28.2 us -> 27.7 us
  transfers between devices with their start and end apart: 89 -> 83, of which waited for: 43 -> 41; matrix products, arithmetic and copies ran while one was open for 15% -> 12% of each run, Pallas kernels for 18% -> 20%
where the time goes in v3:
time: 613 us; the launch traced here: 609 us
  waiting for transfers between devices  172 us (28%)
  Pallas kernels  170 us (28%)
  starting transfers between devices  107 us (17%)
  other arithmetic  74 us (12%)
  local copies, waits for them, and re-layouts  48.4 us (8%)
  between operations  23.7 us (4%)
  matrix products  14.1 us (2%)
    ppermute x81, waiting for transfers between devices, hop(): return lax.ppermute(value, ('dp', 'vocab'), pairs)  172 us
    ppermute x81, starting transfers between devices, hop(): return lax.ppermute(value, ('dp', 'vocab'), pairs)  107 us
    pallas_call x10, Pallas kernels, kernel_call(): pl.pallas_call(kernel, out_shape=out, in_specs=[pl.BlockSpec(memory_space...  53.2 us
    unnamed x221, local copies, waits for them, and re-layouts  27.7 us
    pallas_call x1, Pallas kernels, add_up(): pl.pallas_call(functools.partial(add_up_kernel, grid), out_shape=(jax.Sha...  25.5 us
    pallas_call x1, Pallas kernels, head_slopes(): head_call(slopes_kernel, half, (jax.ShapeDtypeStruct((2 * count, columns)...  19.7 us
    pallas_call x1, Pallas kernels, head_logits(): head_call(logits_kernel, half, (jax.ShapeDtypeStruct((2 * count, columns)...  18.2 us
    pallas_call x1, Pallas kernels, look_up(): pl.pallas_call(functools.partial(look_up_kernel, grid), out_shape=(out, o...  17.8 us
  transfers between devices with their start and end apart: 83, of which 41 were waited for; matrix products, arithmetic and copies ran while one was open for 12% of the time, Pallas kernels for 20%

profile of v3, /device:TPU:0, one launch (start us, length us, event | category | flops | bytes accessed | tf_op | source)
XLA Modules:
  0.0 608.6 jit_solution(2479474823992627142)
XLA Ops:
  30.9 7.7 %shard_map.529.table_ref = f32[6288,192]{1,0:T(8,128)} custom-call(f32[192,6288]{1,0:T(8,128)} %bitcast.588), custom_call_target="tpu_custom_call" | custom-call | bytes 25165824 | tf_op jit(solution)/shard_map/pallas_call | solution.py:244
  63.2 17.8 %shard_map.530 = (bf16[16,112,384]{2,1,0:T(8,128)(2,1)}, bf16[16,112,384]{2,1,0:T(8,128)(2,1)}) custom-call(s32[4]{0:T(128)} %pad_add_fusion.spot_ref, s32[32]{0:T(128)} %copy-done.100, s32[32]{0:T(128)} %max.68.last_ref, s32[32,224]{1,0:T(8,128)} %fusion.30.ids_ref, f32[6288,192]{1,0:T(8,128)} %shard_map.529.table_ref), custom_call_target="tpu_custom_call" | custom-call | bytes 37748736 | tf_op jit(solution)/shard_map/pallas_call | solution.py:343
  95.8 5.3 collective-permute-start.15
  103.6 6.4 %collective-permute-done.18 = bf16[4,48,1536]{2,1,0:T(8,128)(2,1)} collective-permute-done((bf16[4,48,1536]{2,1,0:T(8,128)(2,1)S(1)}, bf16[4,48,1536]{2,1,0:T(8,128)(2,1)}, u32[]{:S(2)}, u32[]{:S(2)}) %collective-permute-start.18) | collective-permute-done | bytes 589856 | tf_op jit(solution)/shard_map/ppermute | solution.py:64
  115.8 11.8 %collective-permute-done.16 = bf16[4,112,384]{2,1,0:T(8,128)(2,1)S(1)} collective-permute-done((bf16[4,112,384]{2,1,0:T(8,128)(2,1)S(1)}, bf16[4,112,384]{2,1,0:T(8,128)(2,1)S(1)}, u32[]{:S(2)}, u32[]{:S(2)}) %collective-permute-start.16) | collective-permute-done | bytes 344096 | tf_op jit(solution)/shard_map/ppermute | solution.py:64
  157.1 9.3 %collective-permute-done.25 = bf16[2,4,48,1536]{3,2,1,0:T(8,128)(2,1)} collective-permute-done((bf16[2,4,48,1536]{3,2,1,0:T(8,128)(2,1)}, bf16[2,4,48,1536]{3,2,1,0:T(8,128)(2,1)}, u32[]{:S(2)}, u32[]{:S(2)}) %collective-permute-start.25) | collective-permute-done | bytes 1179680 | tf_op jit(solution)/shard_map/ppermute | solution.py:64
  175.6 4.6 shard_map.534
  182.5 6.0 shard_map.535
  189.8 5.2 shard_map.536
  197.7 7.2 %collective-permute-start.28 = (bf16[96,768]{1,0:T(8,128)(2,1)S(1)}, bf16[96,768]{1,0:T(8,128)(2,1)S(1)}, u32[]{:S(2)}, u32[]{:S(2)}) collective-permute-start(bf16[96,768]{1,0:T(8,128)(2,1)S(1)} %get-tuple-element.237), channel_id=1, source_target_pairs={{0,2},{1,3},{2,0},{3,1},{4,6},{5,7},{6,4},{7,5},{8,10},{9,11},{10,... | collective-permute-start | bytes 442376 | tf_op jit(solution)/shard_map/ppermute | solution.py:64
  207.3 19.5 %collective-permute-done.31 = bf16[2,192,1664]{2,1,0:T(8,128)(2,1)S(1)} collective-permute-done((bf16[2,192,1664]{2,1,0:T(8,128)(2,1)S(1)}, bf16[2,192,1664]{2,1,0:T(8,128)(2,1)S(1)}, u32[]{:S(2)}, u32[]{:S(2)}) %collective-permute-start.31) | collective-permute-done | bytes 1277984 | tf_op jit(solution)/shard_map/ppermute | solution.py:64
  228.3 6.6 %collective-permute-done.32 = bf16[4,96,384]{2,1,0:T(8,128)(2,1)S(1)} collective-permute-done((bf16[4,96,384]{2,1,0:T(8,128)(2,1)S(1)}, bf16[4,96,384]{2,1,0:T(8,128)(2,1)S(1)}, u32[]{:S(2)}, u32[]{:S(2)}) %collective-permute-start.32) | collective-permute-done | bytes 294944 | tf_op jit(solution)/shard_map/ppermute | solution.py:64
  237.6 10.6 %collective-permute-done.35 = bf16[2,4,96,384]{3,2,1,0:T(8,128)(2,1)S(1)} collective-permute-done((bf16[2,4,96,384]{3,2,1,0:T(8,128)(2,1)S(1)}, bf16[2,4,96,384]{3,2,1,0:T(8,128)(2,1)S(1)}, u32[]{:S(2)}, u32[]{:S(2)}) %collective-permute-start.35) | collective-permute-done | bytes 589856 | tf_op jit(solution)/shard_map/ppermute | solution.py:64
  256.1 18.2 %shard_map.537 = (f32[3072,1664]{1,0:T(8,128)}, f32[3,6,512]{2,1,0:T(8,128)S(1)}) custom-call(s32[3]{0:T(128)S(1)} %pad_add_fusion.2.scalar_ref, bf16[1536,768]{1,0:T(8,128)(2,1)S(1)} %pad_maximum_fusion.7.mine_ref, bf16[1536,768]{1,0:T(8,128)(2,1)} %copy-done.105, bf16[768,1664]{1,0:T(8,128)(2,1)} %pad_maximum_fusion.head_ref, ...), custom_call_target="tpu_custom_call" | custom-call | flops 7851737088 | bytes 20447232 | tf_op jit(solution)/shard_map/pallas_call | solution.py:797
  274.3 7.2 %collective-permute-start.37 = (f32[3,6,512]{2,1,0:T(8,128)S(1)}, f32[3,6,512]{2,1,0:T(8,128)S(1)}, u32[]{:S(2)}, u32[]{:S(2)}) collective-permute-start(f32[3,6,512]{2,1,0:T(8,128)S(1)} %get-tuple-element.244), channel_id=1, source_target_pairs={{0,2},{1,3},{2,0},{3,1},{4,6},{5,7},{6,4},{7,5},{8,10},{9,11},{10,... | collective-permute-start | bytes 110600 | tf_op jit(solution)/shard_map/ppermute | solution.py:64
  295.8 19.7 %shard_map.538 = (bf16[3072,1664]{1,0:T(8,128)(2,1)}, bf16[1536,768]{1,0:T(8,128)(2,1)S(1)}, bf16[1536,768]{1,0:T(8,128)(2,1)}) custom-call(s32[3]{0:T(128)S(1)} %pad_add_fusion.2.scalar_ref, f32[3072,1664]{1,0:T(8,128)} %get-tuple-element.243.value_ref, bf16[768,1664]{1,0:T(8,128)(2,1)} %pad_maximum_fusion.head_ref, ...), custom_call_target="tpu_custom_call" | custom-call | flops 7851737088 | bytes 20447232 | tf_op jit(solution)/shard_map/pallas_call | solution.py:841
  317.1 4.7 collective-permute-done.44
  328.5 16.0 %shard_map.539 = (bf16[4,192,1664]{2,1,0:T(8,128)(2,1)}, f32[1,1664]{1,0:T(1,128)S(1)}) custom-call(s32[3]{0:T(128)S(1)} %pad_add_fusion.2.scalar_ref, bf16[1536,768]{1,0:T(8,128)(2,1)S(1)} %copy-done.9, bf16[1536,768]{1,0:T(8,128)(2,1)} %copy-done.105, bf16[3072,1664]{1,0:T(8,128)(2,1)} %get-tuple-element.251.slope_ref), custom_call_target="tpu_custom_call" | custom-call | flops 7851737088 | bytes 20447232 | tf_op jit(solution)/shard_map/pallas_call | solution.py:885
  346.4 7.0 %collective-permute-done.47 = bf16[4,96,384]{2,1,0:T(8,128)(2,1)S(1)} collective-permute-done((bf16[4,96,384]{2,1,0:T(8,128)(2,1)S(1)}, bf16[4,96,384]{2,1,0:T(8,128)(2,1)S(1)}, u32[]{:S(2)}, u32[]{:S(2)}) %collective-permute-start.47) | collective-permute-done | bytes 294944 | tf_op jit(solution)/shard_map/ppermute | solution.py:64
  365.3 5.4 collective-permute-done.50
  374.6 8.4 %shard_map.540 = (f32[256,768]{1,0:T(8,128)S(1)}, bf16[256,768]{1,0:T(8,128)(2,1)S(1)}, bf16[256,3072]{1,0:T(8,128)(2,1)}, f32[8,768]{1,0:T(8,128)S(1)}) custom-call(s32[2]{0:T(128)S(1)} %pad_add_fusion.1.core_ref, bf16[96,768]{1,0:T(8,128)(2,1)S(1)} %fusion.18.picked_ref, bf16[96,256]{1,0:T(8,128)(2,1)S(1)} %copy-done.35, f32[256,768]{1,0:T(8,128)S(1)} %copy-done.21, ...), custom_call_target="tpu_custom_call" | custom-call | bytes 16777216 | tf_op jit(solution)/shard_map/pallas_call | solution.py:909
  392.4 7.8 %shard_map.541 = (f32[256,768]{1,0:T(8,128)S(1)}, bf16[256,768]{1,0:T(8,128)(2,1)S(1)}, bf16[256,768]{1,0:T(8,128)(2,1)S(1)}, f32[8,768]{1,0:T(8,128)S(1)}) custom-call(s32[2]{0:T(128)S(1)} %pad_add_fusion.1.core_ref, bf16[256,3072]{1,0:T(8,128)(2,1)} %get-tuple-element.265.up_back_ref, f32[256,768]{1,0:T(8,128)S(1)} %copy-done.6, ...), custom_call_target="tpu_custom_call" | custom-call | bytes 16777216 | tf_op jit(solution)/shard_map/pallas_call | solution.py:909
  416.1 6.3 %shard_map.542.triple_back_ref = bf16[256,2304]{1,0:T(8,128)(2,1)S(1)} custom-call(s32[2]{0:T(128)S(1)} %pad_add_fusion.1.core_ref, bf16[256,2304]{1,0:T(8,128)(2,1)S(1)} %copy-done.4, bf16[256,768]{1,0:T(8,128)(2,1)S(1)} %copy-done.30, s32[1,256]{1,0:T(1,128)S(1)} %copy-done.44), custom_call_target="tpu_custom_call" | custom-call | bytes 16777216 | tf_op jit(solution)/shard_map/pallas_call | solution.py:909
  426.6 6.5 %shard_map.543 = bf16[4,120,384]{2,1,0:T(8,128)(2,1)S(1)} custom-call(s32[2]{0:T(128)S(1)} %pad_add_fusion.1.core_ref, bf16[256,2304]{1,0:T(8,128)(2,1)S(1)} %shard_map.542.triple_back_ref, f32[256,768]{1,0:T(8,128)S(1)} %copy-done.2, f32[256,768]{1,0:T(8,128)S(1)} %copy-done.23, f32[8,768]{1,0:T(8,128)S(1)} %bitcast.571, f32[3,768]{1,0:T(4,128)S(1)} %reshape.367.gains, ...), custom_call_target="tpu_custom_call" | custom-call | bytes 16777216 | tf_op jit(solution)/shard_map/pallas_call | solution.py:909
  454.2 11.6 %collective-permute-done.59 = bf16[4,120,384]{2,1,0:T(8,128)(2,1)S(1)} collective-permute-done((bf16[4,120,384]{2,1,0:T(8,128)(2,1)S(1)}, bf16[4,120,384]{2,1,0:T(8,128)(2,1)S(1)}, u32[]{:S(2)}, u32[]{:S(2)}) %collective-permute-start.59) | collective-permute-done | bytes 368672 | tf_op jit(solution)/shard_map/ppermute | solution.py:64
  465.7 14.2 %collective-permute-done.60 = bf16[4,120,384]{2,1,0:T(8,128)(2,1)S(1)} collective-permute-done((bf16[4,120,384]{2,1,0:T(8,128)(2,1)S(1)}, bf16[4,120,384]{2,1,0:T(8,128)(2,1)S(1)}, u32[]{:S(2)}, u32[]{:S(2)}) %collective-permute-start.60) | collective-permute-done | bytes 368672 | tf_op jit(solution)/shard_map/ppermute | solution.py:64
  483.1 6.9 %collective-permute-done.66 = bf16[4,48,768]{2,1,0:T(8,128)(2,1)S(1)} collective-permute-done((bf16[4,48,768]{2,1,0:T(8,128)(2,1)S(1)}, bf16[4,48,768]{2,1,0:T(8,128)(2,1)S(1)}, u32[]{:S(2)}, u32[]{:S(2)}) %collective-permute-start.66) | collective-permute-done | bytes 294944 | tf_op jit(solution)/shard_map/ppermute | solution.py:64
  494.3 6.0 collective-permute-start.67
  505.3 25.5 %shard_map.544 = (f32[192,6288]{1,0:T(8,128)}, f32[1,128]{1,0:T(1,128)}) custom-call(s32[4]{0:T(128)} %pad_add_fusion.spot_ref, s32[32]{0:T(128)} %copy-done.100, s32[32]{0:T(128)} %max.68.last_ref, s32[32,224]{1,0:T(8,128)} %fusion.30.ids_ref, bf16[16,120,384]{2,1,0:T(8,128)(2,1)} %copy-done.57, bf16[16,120,384]{2,1,0:T(8,128)(2,1)} %collective-permute-done.64.theirs_ref), custom_call_target="tpu_custom_call" | custom-call | bytes 52428800 | tf_op jit(solution)/shard_map/pallas_call | solution.py:431
  554.2 9.7 %collective-permute-done.74 = f32[8,128]{1,0:T(8,128)S(1)} collective-permute-done((f32[8,128]{1,0:T(8,128)S(1)}, f32[8,128]{1,0:T(8,128)S(1)}, u32[]{:S(2)}, u32[]{:S(2)}) %collective-permute-start.74) | collective-permute-done | bytes 4128 | tf_op jit(solution)/shard_map/ppermute | solution.py:64
  568.7 12.3 %fusion.1 = (f32[6288,192]{0,1:T(8,128)}, f32[192,6288]{1,0:T(8,128)}, f32[6288,192]{0,1:T(8,128)}) fusion(f32[6288,192]{0,1:T(8,128)} %param.53, f32[6288,192]{0,1:T(8,128)} %param.44, f32[]{:T(128)S(6)} %min.28, f32[192,6288]{1,0:T(8,128)} %get-tuple-element.301, f32[192]{0:T(256)S(1)} %bitcast.574, pred[6288]{0:T(1024)(128)(4,1)S(1)} %iota_compare_fusion, ...), kind=kLoop, calls=%fused_computation.5 | loop fusion | flops 13280256 | bytes 33811348 | tf_op jit(solution)/shard_map/transpose | solution.py:1546
  589.3 9.8 %add_multiply_fusion = (f32[192,6288]{1,0:T(8,128)}, f32[192,6288]{1,0:T(8,128)}, f32[192,6288]{1,0:T(8,128)}) fusion(f32[192,6288]{1,0:T(8,128)} %param.54, f32[192,6288]{1,0:T(8,128)} %in_ref.1, f32[]{:T(128)S(6)} %min.28, bf16[192,1664]{1,0:T(8,128)(2,1)S(1)} %get-tuple-element.359, bf16[192,1664]{1,0:T(8,128)(2,1)S(1)} %get-tuple-element.358, ...), kind=kLoop, calls=%fused_computation.7 | loop fusion | flops 20524032 | bytes 31531012 | tf_op jit(solution)/shard_map/add | solution.py:1190
  (570 shorter events, 263.5 us)
Async XLA Ops:
  7.2 128.1 %all-gather.3.cloned.1.call-start = ((), (), s32[]{:S(2)}) async-start(), calls=%async_computation.1 | async-start | bytes 3932160 | tf_op jit(solution)/shard_map/all_gather | solution.py:134
  13.9 24.7 %collective-permute-start.1 = (f32[16,256]{1,0:T(8,128)}, f32[16,256]{1,0:T(8,128)S(1)}, u32[]{:S(2)}, u32[]{:S(2)}) collective-permute-start(f32[16,256]{1,0:T(8,128)} %get-tuple-element.179), channel_id=1, source_target_pairs={{0,4},{1,5},{2,6},{3,7},{4,0},{5,1},{6,2},{7,3},{8,12},{9,13},{10,... | collective-permute-start | bytes 49160 | tf_op jit(solution)/shard_map/ppermute | solution.py:64
  48.6 35.7 %collective-permute-start.13 = (bf16[2,192,1664]{2,1,0:T(8,128)(2,1)S(1)}, bf16[2,192,1664]{2,1,0:T(8,128)(2,1)}, u32[]{:S(2)}, u32[]{:S(2)}) collective-permute-start(bf16[2,192,1664]{2,1,0:T(8,128)(2,1)S(1)} %get-tuple-element.366), channel_id=1, source_target_pairs={{0,8},{1,9},{2,10},{3,11},{4,12},{5,13},{6,14},{7,15},{8,0},{9,1},... | collective-permute-start | bytes 3833864 | tf_op jit(solution)/shard_map/ppermute | solution.py:64
  52.4 439.2 %reduce-scatter.4.cloned.1.call-start = ((), (), s32[]{:S(2)}) async-start(), calls=%async_computation.2 | async-start | bytes 5898240
  53.2 27.8 %collective-permute-start.10 = (bf16[48,3072]{1,0:T(8,128)(2,1)S(1)}, bf16[48,3072]{1,0:T(8,128)(2,1)S(1)}, u32[]{:S(2)}, u32[]{:S(2)}) collective-permute-start(bf16[48,3072]{1,0:T(8,128)(2,1)S(1)} %slice.400), channel_id=1, source_target_pairs={{0,2},{1,3},{2,0},{3,1},{4,6},{5,7},{6,4},{7,5},{8,10},{9,11},{10,... | collective-permute-start | bytes 884744 | tf_op jit(solution)/shard_map/ppermute | solution.py:64
  57.6 23.4 %collective-permute-start.11 = (bf16[48,3072]{1,0:T(8,128)(2,1)S(1)}, bf16[48,3072]{1,0:T(8,128)(2,1)S(1)}, u32[]{:S(2)}, u32[]{:S(2)}) collective-permute-start(bf16[48,3072]{1,0:T(8,128)(2,1)S(1)} %slice.400), channel_id=1, source_target_pairs={{0,4},{1,5},{2,6},{3,7},{4,0},{5,1},{6,2},{7,3},{8,12},{9,13},{10,... | collective-permute-start | bytes 884744 | tf_op jit(solution)/shard_map/ppermute | solution.py:64
  57.6 23.4 %collective-permute-start.12 = (bf16[48,3072]{1,0:T(8,128)(2,1)S(1)}, bf16[48,3072]{1,0:T(8,128)(2,1)}, u32[]{:S(2)}, u32[]{:S(2)}) collective-permute-start(bf16[48,3072]{1,0:T(8,128)(2,1)S(1)} %slice.400), channel_id=1, source_target_pairs={{0,6},{1,7},{2,4},{3,5},{4,2},{5,3},{6,0},{7,1},{8,14},{9,15},{10,... | collective-permute-start | bytes 884744 | tf_op jit(solution)/shard_map/ppermute | solution.py:64
  85.7 24.3 %collective-permute-start.18 = (bf16[4,48,1536]{2,1,0:T(8,128)(2,1)S(1)}, bf16[4,48,1536]{2,1,0:T(8,128)(2,1)}, u32[]{:S(2)}, u32[]{:S(2)}) collective-permute-start(bf16[4,48,1536]{2,1,0:T(8,128)(2,1)S(1)} %get-tuple-element.216), channel_id=1, source_target_pairs={{0,8},{1,9},{2,10},{3,11},{4,12},{5,13},{6,14},{7,15},{8,0},{9,1},... | collective-permute-start | bytes 1769480 | tf_op jit(solution)/shard_map/ppermute | solution.py:64
  87.3 25.3 %collective-permute-start.19 = (bf16[4,48,1536]{2,1,0:T(8,128)(2,1)S(1)}, bf16[4,48,1536]{2,1,0:T(8,128)(2,1)}, u32[]{:S(2)}, u32[]{:S(2)}) collective-permute-start(bf16[4,48,1536]{2,1,0:T(8,128)(2,1)S(1)} %get-tuple-element.218), channel_id=1, source_target_pairs={{0,16},{1,17},{2,18},{3,19},{4,20},{5,21},{6,22},{7,23},{8,24},{9,... | collective-permute-start | bytes 1769480 | tf_op jit(solution)/shard_map/ppermute | solution.py:64
  95.8 20.1 %collective-permute-start.15 = (bf16[4,112,384]{2,1,0:T(8,128)(2,1)S(1)}, bf16[4,112,384]{2,1,0:T(8,128)(2,1)S(1)}, u32[]{:S(2)}, u32[]{:S(2)}) collective-permute-start(bf16[4,112,384]{2,1,0:T(8,128)(2,1)S(1)} %get-tuple-element.390), channel_id=1, source_target_pairs={{0,2},{1,3},{2,0},{3,1},{4,6},{5,7},{6,4},{7,5},{8,10},{9,11},{10,... | collective-permute-start | bytes 1032200 | tf_op jit(solution)/shard_map/ppermute | solution.py:64
  101.1 26.6 %collective-permute-start.16 = (bf16[4,112,384]{2,1,0:T(8,128)(2,1)S(1)}, bf16[4,112,384]{2,1,0:T(8,128)(2,1)S(1)}, u32[]{:S(2)}, u32[]{:S(2)}) collective-permute-start(bf16[4,112,384]{2,1,0:T(8,128)(2,1)S(1)} %get-tuple-element.389), channel_id=1, source_target_pairs={{0,4},{1,5},{2,6},{3,7},{4,0},{5,1},{6,2},{7,3},{8,12},{9,13},{10,... | collective-permute-start | bytes 1032200 | tf_op jit(solution)/shard_map/ppermute | solution.py:64
  101.1 26.6 %collective-permute-start.17 = (bf16[4,112,384]{2,1,0:T(8,128)(2,1)S(1)}, bf16[4,112,384]{2,1,0:T(8,128)(2,1)S(1)}, u32[]{:S(2)}, u32[]{:S(2)}) collective-permute-start(bf16[4,112,384]{2,1,0:T(8,128)(2,1)S(1)} %get-tuple-element.388), channel_id=1, source_target_pairs={{0,6},{1,7},{2,4},{3,5},{4,2},{5,3},{6,0},{7,1},{8,14},{9,15},{10,... | collective-permute-start | bytes 1032200 | tf_op jit(solution)/shard_map/ppermute | solution.py:64
  137.7 28.7 %collective-permute-start.25 = (bf16[2,4,48,1536]{3,2,1,0:T(8,128)(2,1)}, bf16[2,4,48,1536]{3,2,1,0:T(8,128)(2,1)}, u32[]{:S(2)}, u32[]{:S(2)}) collective-permute-start(bf16[2,4,48,1536]{3,2,1,0:T(8,128)(2,1)} %pad_maximum_fusion.14), channel_id=1, source_target_pairs={{0,8},{1,9},{2,10},{3,11},{4,12},{5,13},{6,14},{7,15},{8,0},{9,1},... | collective-permute-start | bytes 3538952 | tf_op jit(solution)/shard_map/ppermute | solution.py:64
  141.5 28.4 %collective-permute-start.24 = (bf16[2,4,48,1536]{3,2,1,0:T(8,128)(2,1)}, bf16[2,4,48,1536]{3,2,1,0:T(8,128)(2,1)}, u32[]{:S(2)}, u32[]{:S(2)}) collective-permute-start(bf16[2,4,48,1536]{3,2,1,0:T(8,128)(2,1)} %pad_maximum_fusion.13), channel_id=1, source_target_pairs={{0,16},{1,17},{2,18},{3,19},{4,20},{5,21},{6,22},{7,23},{8,24},{9,... | collective-permute-start | bytes 3538952 | tf_op jit(solution)/shard_map/ppermute | solution.py:64
  197.1 29.7 %collective-permute-start.31 = (bf16[2,192,1664]{2,1,0:T(8,128)(2,1)S(1)}, bf16[2,192,1664]{2,1,0:T(8,128)(2,1)S(1)}, u32[]{:S(2)}, u32[]{:S(2)}) collective-permute-start(bf16[2,192,1664]{2,1,0:T(8,128)(2,1)S(1)} %pad_maximum_fusion.10), channel_id=1, source_target_pairs={{0,16},{1,17},{2,18},{3,19},{4,20},{5,21},{6,22},{7,23},{8,24},{9,... | collective-permute-start | bytes 3833864 | tf_op jit(solution)/shard_map/ppermute | solution.py:64
  197.7 29.2 %collective-permute-start.28 = (bf16[96,768]{1,0:T(8,128)(2,1)S(1)}, bf16[96,768]{1,0:T(8,128)(2,1)S(1)}, u32[]{:S(2)}, u32[]{:S(2)}) collective-permute-start(bf16[96,768]{1,0:T(8,128)(2,1)S(1)} %get-tuple-element.237), channel_id=1, source_target_pairs={{0,2},{1,3},{2,0},{3,1},{4,6},{5,7},{6,4},{7,5},{8,10},{9,11},{10,... | collective-permute-start | bytes 442376 | tf_op jit(solution)/shard_map/ppermute | solution.py:64
  204.9 22.0 %collective-permute-start.29 = (bf16[96,768]{1,0:T(8,128)(2,1)S(1)}, bf16[96,768]{1,0:T(8,128)(2,1)S(1)}, u32[]{:S(2)}, u32[]{:S(2)}) collective-permute-start(bf16[96,768]{1,0:T(8,128)(2,1)S(1)} %get-tuple-element.237), channel_id=1, source_target_pairs={{0,4},{1,5},{2,6},{3,7},{4,0},{5,1},{6,2},{7,3},{8,12},{9,13},{10,... | collective-permute-start | bytes 442376 | tf_op jit(solution)/shard_map/ppermute | solution.py:64
  204.9 22.0 %collective-permute-start.30 = (bf16[96,768]{1,0:T(8,128)(2,1)S(1)}, bf16[96,768]{1,0:T(8,128)(2,1)S(1)}, u32[]{:S(2)}, u32[]{:S(2)}) collective-permute-start(bf16[96,768]{1,0:T(8,128)(2,1)S(1)} %get-tuple-element.237), channel_id=1, source_target_pairs={{0,6},{1,7},{2,4},{3,5},{4,2},{5,3},{6,0},{7,1},{8,14},{9,15},{10,... | collective-permute-start | bytes 442376 | tf_op jit(solution)/shard_map/ppermute | solution.py:64
  325.2 19.3 %collective-permute-start.46 = (bf16[2,4,96,384]{3,2,1,0:T(8,128)(2,1)S(1)}, bf16[2,4,96,384]{3,2,1,0:T(8,128)(2,1)S(1)}, u32[]{:S(2)}, u32[]{:S(2)}) collective-permute-start(bf16[2,4,96,384]{3,2,1,0:T(8,128)(2,1)S(1)} %get-tuple-element.402), channel_id=1, source_target_pairs={{0,8},{1,9},{2,10},{3,11},{4,12},{5,13},{6,14},{7,15},{8,0},{9,1},... | collective-permute-start | bytes 1769480 | tf_op jit(solution)/shard_map/ppermute | solution.py:64
  326.8 17.7 %collective-permute-start.45 = (bf16[2,4,96,384]{3,2,1,0:T(8,128)(2,1)S(1)}, bf16[2,4,96,384]{3,2,1,0:T(8,128)(2,1)S(1)}, u32[]{:S(2)}, u32[]{:S(2)}) collective-permute-start(bf16[2,4,96,384]{3,2,1,0:T(8,128)(2,1)S(1)} %get-tuple-element.404), channel_id=1, source_target_pairs={{0,16},{1,17},{2,18},{3,19},{4,20},{5,21},{6,22},{7,23},{8,24},{9,... | collective-permute-start | bytes 1769480 | tf_op jit(solution)/shard_map/ppermute | solution.py:64
  355.8 29.8 %collective-permute-start.52 = (bf16[2,192,1664]{2,1,0:T(8,128)(2,1)}, bf16[2,192,1664]{2,1,0:T(8,128)(2,1)}, u32[]{:S(2)}, u32[]{:S(2)}) collective-permute-start(bf16[2,192,1664]{2,1,0:T(8,128)(2,1)} %get-tuple-element.360), channel_id=1, source_target_pairs={{0,8},{1,9},{2,10},{3,11},{4,12},{5,13},{6,14},{7,15},{8,0},{9,1},... | collective-permute-start | bytes 3833864 | tf_op jit(solution)/shard_map/ppermute | solution.py:64
  424.8 19.8 %collective-permute-start.58 = (bf16[768,1536]{1,0:T(8,128)(2,1)}, bf16[768,1536]{1,0:T(8,128)(2,1)}, u32[]{:S(2)}, u32[]{:S(2)}) collective-permute-start(bf16[768,1536]{1,0:T(8,128)(2,1)} %pad_maximum_fusion.8), channel_id=1, source_target_pairs={{0,1},{1,0},{2,3},{3,2},{4,5},{5,4},{6,7},{7,6},{8,9},{9,8},{10,11... | collective-permute-start | bytes 7077896 | tf_op jit(solution)/shard_map/ppermute | solution.py:64
  447.1 32.9 %collective-permute-start.63 = (bf16[2,4,48,768]{3,2,1,0:T(8,128)(2,1)S(1)}, bf16[2,4,48,768]{3,2,1,0:T(8,128)(2,1)S(1)}, u32[]{:S(2)}, u32[]{:S(2)}) collective-permute-start(bf16[2,4,48,768]{3,2,1,0:T(8,128)(2,1)S(1)} %get-tuple-element.398), channel_id=1, source_target_pairs={{0,8},{1,9},{2,10},{3,11},{4,12},{5,13},{6,14},{7,15},{8,0},{9,1},... | collective-permute-start | bytes 1769480 | tf_op jit(solution)/shard_map/ppermute | solution.py:64
  448.8 31.2 %collective-permute-start.62 = (bf16[2,4,48,768]{3,2,1,0:T(8,128)(2,1)S(1)}, bf16[2,4,48,768]{3,2,1,0:T(8,128)(2,1)S(1)}, u32[]{:S(2)}, u32[]{:S(2)}) collective-permute-start(bf16[2,4,48,768]{3,2,1,0:T(8,128)(2,1)S(1)} %get-tuple-element.400), channel_id=1, source_target_pairs={{0,16},{1,17},{2,18},{3,19},{4,20},{5,21},{6,22},{7,23},{8,24},{9,... | collective-permute-start | bytes 1769480 | tf_op jit(solution)/shard_map/ppermute | solution.py:64
  451.8 28.2 %collective-permute-start.60 = (bf16[4,120,384]{2,1,0:T(8,128)(2,1)S(1)}, bf16[4,120,384]{2,1,0:T(8,128)(2,1)S(1)}, u32[]{:S(2)}, u32[]{:S(2)}) collective-permute-start(bf16[4,120,384]{2,1,0:T(8,128)(2,1)S(1)} %pad_maximum_fusion.24), channel_id=1, source_target_pairs={{0,4},{1,5},{2,6},{3,7},{4,0},{5,1},{6,2},{7,3},{8,12},{9,13},{10,... | collective-permute-start | bytes 1105928 | tf_op jit(solution)/shard_map/ppermute | solution.py:64
  451.8 28.2 %collective-permute-start.61 = (bf16[4,120,384]{2,1,0:T(8,128)(2,1)S(1)}, bf16[4,120,384]{2,1,0:T(8,128)(2,1)S(1)}, u32[]{:S(2)}, u32[]{:S(2)}) collective-permute-start(bf16[4,120,384]{2,1,0:T(8,128)(2,1)S(1)} %pad_maximum_fusion.24), channel_id=1, source_target_pairs={{0,6},{1,7},{2,4},{3,5},{4,2},{5,3},{6,0},{7,1},{8,14},{9,15},{10,... | collective-permute-start | bytes 1105928 | tf_op jit(solution)/shard_map/ppermute | solution.py:64
  494.3 44.7 %collective-permute-start.67 = (bf16[48,4608]{1,0:T(8,128)(2,1)}, bf16[48,4608]{1,0:T(8,128)(2,1)}, u32[]{:S(2)}, u32[]{:S(2)}) collective-permute-start(bf16[48,4608]{1,0:T(8,128)(2,1)} %get-tuple-element.386), channel_id=1, source_target_pairs={{0,2},{1,3},{2,0},{3,1},{4,6},{5,7},{6,4},{7,5},{8,10},{9,11},{10,... | collective-permute-start | bytes 1327112 | tf_op jit(solution)/shard_map/ppermute | solution.py:64
  500.3 38.7 %collective-permute-start.68 = (bf16[48,4608]{1,0:T(8,128)(2,1)}, bf16[48,4608]{1,0:T(8,128)(2,1)}, u32[]{:S(2)}, u32[]{:S(2)}) collective-permute-start(bf16[48,4608]{1,0:T(8,128)(2,1)} %get-tuple-element.385), channel_id=1, source_target_pairs={{0,4},{1,5},{2,6},{3,7},{4,0},{5,1},{6,2},{7,3},{8,12},{9,13},{10,... | collective-permute-start | bytes 1327112 | tf_op jit(solution)/shard_map/ppermute | solution.py:64
  500.7 38.3 %collective-permute-start.69 = (bf16[48,4608]{1,0:T(8,128)(2,1)}, bf16[48,4608]{1,0:T(8,128)(2,1)}, u32[]{:S(2)}, u32[]{:S(2)}) collective-permute-start(bf16[48,4608]{1,0:T(8,128)(2,1)} %get-tuple-element.384), channel_id=1, source_target_pairs={{0,6},{1,7},{2,4},{3,5},{4,2},{5,3},{6,0},{7,1},{8,14},{9,15},{10,... | collective-permute-start | bytes 1327112 | tf_op jit(solution)/shard_map/ppermute | solution.py:64
  535.4 52.0 %collective-permute-start.77 = (bf16[2,192,1664]{2,1,0:T(8,128)(2,1)}, bf16[2,192,1664]{2,1,0:T(8,128)(2,1)}, u32[]{:S(2)}, u32[]{:S(2)}) collective-permute-start(bf16[2,192,1664]{2,1,0:T(8,128)(2,1)} %pad_maximum_fusion.11), channel_id=1, source_target_pairs={{0,16},{1,17},{2,18},{3,19},{4,20},{5,21},{6,22},{7,23},{8,24},{9,... | collective-permute-start | bytes 3833864 | tf_op jit(solution)/shard_map/ppermute | solution.py:64
  547.3 34.5 %collective-permute-start.80 = (f32[96,384]{1,0:T(8,128)S(1)}, f32[96,384]{1,0:T(8,128)}, u32[]{:S(2)}, u32[]{:S(2)}) collective-permute-start(f32[96,384]{1,0:T(8,128)S(1)} %dynamic-slice_bitcast_fusion.18), channel_id=1, source_target_pairs={{0,1},{1,0},{2,3},{3,2},{4,5},{5,4},{6,7},{7,6},{8,9},{9,8},{10,11... | collective-permute-start | bytes 442376 | tf_op jit(solution)/shard_map/ppermute | solution.py:64
  554.2 30.3 %collective-permute-start.79 = (f32[24,1536]{1,0:T(8,128)S(1)}, f32[24,1536]{1,0:T(8,128)}, u32[]{:S(2)}, u32[]{:S(2)}) collective-permute-start(f32[24,1536]{1,0:T(8,128)S(1)} %dynamic-slice_bitcast_fusion.19), channel_id=1, source_target_pairs={{0,1},{1,0},{2,3},{3,2},{4,5},{5,4},{6,7},{7,6},{8,9},{9,8},{10,11... | collective-permute-start | bytes 442376 | tf_op jit(solution)/shard_map/ppermute | solution.py:64
  (157 other events, 1409.3 us)
Sparse Core Ops, SparseCore 0:
  52.5 63.1 all-gather.2
  412.6 64.9 reduce-scatter.3

commit v4 on v3

--- a/solution.py
+++ b/solution.py
@@ -688,7 +688,7 @@
     return info[:, n : n + 1]
 
 
-ROW_BLOCK = 512
+ROW_BLOCK = 768
 
 
 def split_kernel(columns, place_ref, in_ref, out_ref):
@@ -879,7 +879,7 @@
 
 def head_grads(links, scalars, mine, theirs, slopes):
     (count, width), columns = mine.shape, slopes.shape[1]
-    rows = 3 * ROW_BLOCK if count % (3 * ROW_BLOCK) == 0 else ROW_BLOCK
+    rows = 2 * ROW_BLOCK if count % (2 * ROW_BLOCK) == 0 else ROW_BLOCK
     by_step, by_mine, by_theirs, whole = head_specs(count // rows, rows)
     out = (links.dp_count, width // links.dp_count, columns)
     return head_call(
@@ -1256,13 +1256,12 @@
     a_z = links.heard(pair_a, "z")
     table = turned(embedding.T)
     small_z, head_slots, a_z, table = tie(small_z, head_slots, a_z, table)
-    a_mine = links.wide_across(a_z)
     small_dp, step = links.piled(small_z, "z")[None], 1
     while step < dp_count:
         small_dp, step = links.doubled(small_dp, "dp", step), 2 * step
     small_c = links.heard(small_dp, "c")
     head_came = links.exchange(head_slots)
-    small_c, pair_bc = tie(small_c, pair_bc)
+    pair_bc, _ = tie(pair_bc, a_z)
     bc_z = links.heard(pair_bc, "z")
 
     numbers = links.piled(small_c, "c", 2).reshape((device_count,) + small.shape)
@@ -1276,9 +1275,10 @@
     ).astype(jnp.int32)
     grid = (dp_count, links.size("z"), links.size("c"))
     looked = look_up(spot, first, last, ids_all, table, grid)
-    looked, bc_z, head_came, numbers = tie(looked, bc_z, head_came, numbers)
+    looked, bc_z, head_came, a_z = tie(looked, bc_z, head_came, a_z)
+    a_mine = links.wide_across(a_z)
     looked_c = looked[0], [links.hop(looked[1], "c", 1)]
-    looked = links.summed(looked_c).astype(low)
+    looked, numbers = tie(links.summed(looked_c).astype(low), numbers)
     looked = looked.reshape((grid[1], grid[0]) + looked.shape[1:])
     looked_z = links.near(looked, "z")
     half_up = w_up.shape[1] // 2
@@ -1316,12 +1316,13 @@
     spectrum_rows = by_steps(spectrum_rows.reshape(grid + (time_rows,)), spot, grid)
     spectrum_rows = spectrum_rows.transpose(2, 1, 0, 3).reshape(device_count, time_rows)
     early = (hidden_time, gains, mask_row_full, target_local, row_share, scalars, spectrum_rows)
-    looked_z, early, bc_first = tie(looked_z, early, bc_first)
-    bc_second = links.across_second(bc_first)
-    hidden_time, gains, mask_row_full, target_local, row_share, scalars, spectrum_rows = early
+    looked_z, bc_first = tie(looked_z, bc_first)
+    bc_blocks = links.piled(bc_first[0], "v"), links.piled(bc_first[1], "u")
     looked = links.summed((looked_z[0], looked_z[1:])).astype(low)
     looked_dp = links.near(looked, "dp")
-    looked_dp, a_mine = tie(looked_dp, a_mine)
+    looked_dp, a_mine, early, bc_blocks = tie(looked_dp, a_mine, early, bc_blocks)
+    hidden_time, gains, mask_row_full, target_local, row_share, scalars, spectrum_rows = early
+    bc_second = links.heard(bc_blocks[0], "u"), links.heard(bc_blocks[1], "v")
     a_other = links.hop(a_mine, "c", 1)
     hidden_start = enter(
         first_half, second_half, masked, mask_row_full, links.ordered(looked_dp, "dp")
@@ -1367,9 +1368,9 @@
     picked, head_came = tie(picked, head_came)
     picked_z = links.heard(picked, "z")
     head_pieces = links.exchanged(head_came)
-    picked_z, head_pieces = tie(picked_z, head_pieces)
+    rows_first = links.across_first(picked_z, cut_rows)
+    rows_first, head_pieces = tie(rows_first, head_pieces)
     head = jnp.concatenate(links.ordered(head_pieces, "dp"), 0)
-    rows_first = links.across_first(picked_z, cut_rows)
     rows_second = links.across_second(rows_first)
     rows_mine = jnp.concatenate(links.across_done(rows_second), 1)
     rows_theirs = links.hop(rows_mine, "c", 1)

time: 613 us -> 599 us (0.977)
  Pallas kernels: 170 us -> 159 us
    all_gather x1, waiting for transfers between devices: 0.01 us -> 6.97 us  [wide_across(): block = lax.all_gather(self.piled(pieces, 'z'), 'dp', axis=0, tiled=False)]
    ppermute x81, waiting for transfers between devices: 172 us -> 166 us  [hop(): return lax.ppermute(value, ('dp', 'vocab'), pairs)]
    unnamed x221 -> x229, local copies, waits for them, and re-layouts: 27.7 us -> 27.5 us
  transfers between devices with their start and end apart: 83 -> 83, of which waited for: 41 -> 41; matrix products, arithmetic and copies ran while one was open for 12% -> 13% of each run, Pallas kernels for 20% -> 19%
where the time goes in v4:
time: 599 us; the launch traced here: 592 us
  waiting for transfers between devices  173 us (29%)
  Pallas kernels  159 us (27%)
  starting transfers between devices  102 us (17%)
  other arithmetic  71.8 us (12%)
  local copies, waits for them, and re-layouts  49.1 us (8%)
  between operations  23.6 us (4%)
  matrix products  14.1 us (2%)
    ppermute x81, waiting for transfers between devices, hop(): return lax.ppermute(value, ('dp', 'vocab'), pairs)  166 us
    ppermute x81, starting transfers between devices, hop(): return lax.ppermute(value, ('dp', 'vocab'), pairs)  102 us
    pallas_call x10, Pallas kernels, kernel_call(): pl.pallas_call(kernel, out_shape=out, in_specs=[pl.BlockSpec(memory_space...  53.4 us
    unnamed x229, local copies, waits for them, and re-layouts  27.5 us
    pallas_call x1, Pallas kernels, add_up(): pl.pallas_call(functools.partial(add_up_kernel, grid), out_shape=(jax.Sha...  19.9 us
    pallas_call x1, Pallas kernels, head_slopes(): head_call(slopes_kernel, half, (jax.ShapeDtypeStruct((2 * count, columns)...  18.6 us
    pallas_call x1, Pallas kernels, head_logits(): head_call(logits_kernel, half, (jax.ShapeDtypeStruct((2 * count, columns)...  18 us
    pallas_call x1, Pallas kernels, head_grads(): head_call(functools.partial(head_grads_kernel, links), count // rows, (ja...  16.3 us
  transfers between devices with their start and end apart: 83, of which 41 were waited for; matrix products, arithmetic and copies ran while one was open for 13% of the time, Pallas kernels for 19%

profile of v4, /device:TPU:0, one launch (start us, length us, event | category | flops | bytes accessed | tf_op | source)
XLA Modules:
  0.0 592.2 jit_solution(11112489113112609854)
XLA Ops:
  26.3 7.7 %shard_map.529.table_ref = f32[6288,192]{1,0:T(8,128)} custom-call(f32[192,6288]{1,0:T(8,128)} %bitcast.588), custom_call_target="tpu_custom_call" | custom-call | bytes 25165824 | tf_op jit(solution)/shard_map/pallas_call | solution.py:244
  61.0 13.5 %shard_map.530 = (bf16[16,112,384]{2,1,0:T(8,128)(2,1)}, bf16[16,112,384]{2,1,0:T(8,128)(2,1)}) custom-call(s32[4]{0:T(128)} %pad_add_fusion.spot_ref, s32[32]{0:T(128)} %copy-done.104, s32[32]{0:T(128)} %max.68.last_ref, s32[32,224]{1,0:T(8,128)} %fusion.30.ids_ref, f32[6288,192]{1,0:T(8,128)} %shard_map.529.table_ref), custom_call_target="tpu_custom_call" | custom-call | bytes 37748736 | tf_op jit(solution)/shard_map/pallas_call | solution.py:343
  86.6 6.2 %collective-permute-start.15 = (bf16[4,112,384]{2,1,0:T(8,128)(2,1)}, bf16[4,112,384]{2,1,0:T(8,128)(2,1)S(1)}, u32[]{:S(2)}, u32[]{:S(2)}) collective-permute-start(bf16[4,112,384]{2,1,0:T(8,128)(2,1)} %get-tuple-element.400), channel_id=1, source_target_pairs={{0,2},{1,3},{2,0},{3,1},{4,6},{5,7},{6,4},{7,5},{8,10},{9,11},{10,... | collective-permute-start | bytes 1032200 | tf_op jit(solution)/shard_map/ppermute | solution.py:64
  101.4 5.9 collective-permute-done.15
  107.3 12.3 %collective-permute-done.16 = bf16[4,112,384]{2,1,0:T(8,128)(2,1)S(1)} collective-permute-done((bf16[4,112,384]{2,1,0:T(8,128)(2,1)}, bf16[4,112,384]{2,1,0:T(8,128)(2,1)S(1)}, u32[]{:S(2)}, u32[]{:S(2)}) %collective-permute-start.16) | collective-permute-done | bytes 344096 | tf_op jit(solution)/shard_map/ppermute | solution.py:64
  129.4 7.0 %all-gather.3.cloned.1.call-done = bf16[16,48,2048]{2,1,0:T(8,128)(2,1)} async-done(((bf16[4,48,2048]{2,1,0:T(8,128)(2,1)}), bf16[16,48,2048]{2,1,0:T(8,128)(2,1)}) %all-gather.3.cloned.1.call-update) | async-done | bytes 3145744 | tf_op jit(solution)/shard_map/all_gather | solution.py:134
  153.4 11.6 %collective-permute-done.24 = bf16[2,4,48,1536]{3,2,1,0:T(8,128)(2,1)} collective-permute-done((bf16[2,4,48,1536]{3,2,1,0:T(8,128)(2,1)}, bf16[2,4,48,1536]{3,2,1,0:T(8,128)(2,1)}, u32[]{:S(2)}, u32[]{:S(2)}) %collective-permute-start.24) | collective-permute-done | bytes 1179680 | tf_op jit(solution)/shard_map/ppermute | solution.py:64
  178.8 6.2 %shard_map.535 = (f32[256,3072]{1,0:T(8,128)}, bf16[256,3072]{1,0:T(8,128)(2,1)S(1)}) custom-call(s32[2]{0:T(128)S(1)} %pad_add_fusion.1.core_ref, bf16[256,768]{1,0:T(8,128)(2,1)S(1)} %get-tuple-element.230.normed_ref, bf16[768,1536]{1,0:T(8,128)(2,1)} %bitcast.583, bf16[768,1536]{1,0:T(8,128)(2,1)} %copy-done.52), custom_call_target="tpu_custom_call" | custom-call | bytes 8388608 | tf_op jit(solution)/shard_map/pallas_call | solution.py:909
  186.2 5.2 shard_map.536
  202.8 6.9 %collective-permute-done.29 = bf16[96,768]{1,0:T(8,128)(2,1)S(1)} collective-permute-done((bf16[96,768]{1,0:T(8,128)(2,1)S(1)}, bf16[96,768]{1,0:T(8,128)(2,1)S(1)}, u32[]{:S(2)}, u32[]{:S(2)}) %collective-permute-start.29) | collective-permute-done | bytes 147488 | tf_op jit(solution)/shard_map/ppermute | solution.py:64
  212.1 12.5 %collective-permute-done.33 = bf16[2,192,1664]{2,1,0:T(8,128)(2,1)S(1)} collective-permute-done((bf16[2,192,1664]{2,1,0:T(8,128)(2,1)S(1)}, bf16[2,192,1664]{2,1,0:T(8,128)(2,1)S(1)}, u32[]{:S(2)}, u32[]{:S(2)}) %collective-permute-start.33) | collective-permute-done | bytes 1277984 | tf_op jit(solution)/shard_map/ppermute | solution.py:64
  224.7 4.9 collective-permute-done.32
  232.0 11.8 %collective-permute-done.35 = bf16[2,4,96,384]{3,2,1,0:T(8,128)(2,1)S(1)} collective-permute-done((bf16[2,4,96,384]{3,2,1,0:T(8,128)(2,1)S(1)}, bf16[2,4,96,384]{3,2,1,0:T(8,128)(2,1)S(1)}, u32[]{:S(2)}, u32[]{:S(2)}) %collective-permute-start.35) | collective-permute-done | bytes 589856 | tf_op jit(solution)/shard_map/ppermute | solution.py:64
  250.8 18.0 %shard_map.537 = (f32[3072,1664]{1,0:T(8,128)}, f32[3,4,768]{2,1,0:T(4,128)S(1)}) custom-call(s32[3]{0:T(128)S(1)} %pad_add_fusion.2.scalar_ref, bf16[1536,768]{1,0:T(8,128)(2,1)S(1)} %pad_maximum_fusion.7.mine_ref, bf16[1536,768]{1,0:T(8,128)(2,1)} %copy-done.109, bf16[768,1664]{1,0:T(8,128)(2,1)} %pad_maximum_fusion.head_ref, ...), custom_call_target="tpu_custom_call" | custom-call | flops 7851737088 | bytes 20447232 | tf_op jit(solution)/shard_map/pallas_call | solution.py:797
  286.8 18.6 %shard_map.538 = (bf16[3072,1664]{1,0:T(8,128)(2,1)}, bf16[1536,768]{1,0:T(8,128)(2,1)S(1)}, bf16[1536,768]{1,0:T(8,128)(2,1)}) custom-call(s32[3]{0:T(128)S(1)} %pad_add_fusion.2.scalar_ref, f32[3072,1664]{1,0:T(8,128)} %get-tuple-element.253.value_ref, bf16[768,1664]{1,0:T(8,128)(2,1)} %pad_maximum_fusion.head_ref, ...), custom_call_target="tpu_custom_call" | custom-call | flops 7851737088 | bytes 20447232 | tf_op jit(solution)/shard_map/pallas_call | solution.py:841
  307.1 4.7 collective-permute-done.44
  317.5 16.3 %shard_map.539 = (bf16[4,192,1664]{2,1,0:T(8,128)(2,1)}, f32[1,1664]{1,0:T(1,128)S(1)}) custom-call(s32[3]{0:T(128)S(1)} %pad_add_fusion.2.scalar_ref, bf16[1536,768]{1,0:T(8,128)(2,1)S(1)} %copy-done.9, bf16[1536,768]{1,0:T(8,128)(2,1)} %copy-done.109, bf16[3072,1664]{1,0:T(8,128)(2,1)} %get-tuple-element.261.slope_ref), custom_call_target="tpu_custom_call" | custom-call | flops 7851737088 | bytes 20447232 | tf_op jit(solution)/shard_map/pallas_call | solution.py:885
  336.4 6.2 %collective-permute-done.47 = bf16[4,96,384]{2,1,0:T(8,128)(2,1)S(1)} collective-permute-done((bf16[4,96,384]{2,1,0:T(8,128)(2,1)S(1)}, bf16[4,96,384]{2,1,0:T(8,128)(2,1)S(1)}, u32[]{:S(2)}, u32[]{:S(2)}) %collective-permute-start.47) | collective-permute-done | bytes 294944 | tf_op jit(solution)/shard_map/ppermute | solution.py:64
  352.2 7.1 %collective-permute-done.50 = bf16[96,768]{1,0:T(8,128)(2,1)S(1)} collective-permute-done((bf16[96,768]{1,0:T(8,128)(2,1)S(1)}, bf16[96,768]{1,0:T(8,128)(2,1)S(1)}, u32[]{:S(2)}, u32[]{:S(2)}) %collective-permute-start.50) | collective-permute-done | bytes 147488 | tf_op jit(solution)/shard_map/ppermute | solution.py:64
  363.2 8.4 %shard_map.540 = (f32[256,768]{1,0:T(8,128)S(1)}, bf16[256,768]{1,0:T(8,128)(2,1)S(1)}, bf16[256,3072]{1,0:T(8,128)(2,1)}, f32[8,768]{1,0:T(8,128)S(1)}) custom-call(s32[2]{0:T(128)S(1)} %pad_add_fusion.1.core_ref, bf16[96,768]{1,0:T(8,128)(2,1)S(1)} %fusion.18.picked_ref, bf16[96,256]{1,0:T(8,128)(2,1)S(1)} %copy-done.35, f32[256,768]{1,0:T(8,128)S(1)} %copy-done.21, ...), custom_call_target="tpu_custom_call" | custom-call | bytes 16777216 | tf_op jit(solution)/shard_map/pallas_call | solution.py:909
  381.0 7.8 %shard_map.541 = (f32[256,768]{1,0:T(8,128)S(1)}, bf16[256,768]{1,0:T(8,128)(2,1)S(1)}, bf16[256,768]{1,0:T(8,128)(2,1)S(1)}, f32[8,768]{1,0:T(8,128)S(1)}) custom-call(s32[2]{0:T(128)S(1)} %pad_add_fusion.1.core_ref, bf16[256,3072]{1,0:T(8,128)(2,1)} %get-tuple-element.275.up_back_ref, f32[256,768]{1,0:T(8,128)S(1)} %copy-done.6, ...), custom_call_target="tpu_custom_call" | custom-call | bytes 16777216 | tf_op jit(solution)/shard_map/pallas_call | solution.py:909
  404.7 6.3 %shard_map.542.triple_back_ref = bf16[256,2304]{1,0:T(8,128)(2,1)S(1)} custom-call(s32[2]{0:T(128)S(1)} %pad_add_fusion.1.core_ref, bf16[256,2304]{1,0:T(8,128)(2,1)S(1)} %copy-done.4, bf16[256,768]{1,0:T(8,128)(2,1)S(1)} %copy-done.30, s32[1,256]{1,0:T(1,128)S(1)} %copy-done.44), custom_call_target="tpu_custom_call" | custom-call | bytes 16777216 | tf_op jit(solution)/shard_map/pallas_call | solution.py:909
  415.4 6.5 %shard_map.543 = bf16[4,120,384]{2,1,0:T(8,128)(2,1)S(1)} custom-call(s32[2]{0:T(128)S(1)} %pad_add_fusion.1.core_ref, bf16[256,2304]{1,0:T(8,128)(2,1)S(1)} %shard_map.542.triple_back_ref, f32[256,768]{1,0:T(8,128)S(1)} %copy-done.2, f32[256,768]{1,0:T(8,128)S(1)} %copy-done.23, f32[8,768]{1,0:T(8,128)S(1)} %bitcast.571, f32[3,768]{1,0:T(4,128)S(1)} %reshape.368.gains, ...), custom_call_target="tpu_custom_call" | custom-call | bytes 16777216 | tf_op jit(solution)/shard_map/pallas_call | solution.py:909
  443.1 11.3 %collective-permute-done.59 = bf16[4,120,384]{2,1,0:T(8,128)(2,1)S(1)} collective-permute-done((bf16[4,120,384]{2,1,0:T(8,128)(2,1)S(1)}, bf16[4,120,384]{2,1,0:T(8,128)(2,1)S(1)}, u32[]{:S(2)}, u32[]{:S(2)}) %collective-permute-start.59) | collective-permute-done | bytes 368672 | tf_op jit(solution)/shard_map/ppermute | solution.py:64
  454.4 14.5 %collective-permute-done.60 = bf16[4,120,384]{2,1,0:T(8,128)(2,1)S(1)} collective-permute-done((bf16[4,120,384]{2,1,0:T(8,128)(2,1)S(1)}, bf16[4,120,384]{2,1,0:T(8,128)(2,1)S(1)}, u32[]{:S(2)}, u32[]{:S(2)}) %collective-permute-start.60) | collective-permute-done | bytes 368672 | tf_op jit(solution)/shard_map/ppermute | solution.py:64
  471.9 7.0 %collective-permute-done.66 = bf16[4,48,768]{2,1,0:T(8,128)(2,1)S(1)} collective-permute-done((bf16[4,48,768]{2,1,0:T(8,128)(2,1)S(1)}, bf16[4,48,768]{2,1,0:T(8,128)(2,1)S(1)}, u32[]{:S(2)}, u32[]{:S(2)}) %collective-permute-start.66) | collective-permute-done | bytes 294944 | tf_op jit(solution)/shard_map/ppermute | solution.py:64
  482.1 6.0 %collective-permute-start.67 = (bf16[48,4608]{1,0:T(8,128)(2,1)}, bf16[48,4608]{1,0:T(8,128)(2,1)}, u32[]{:S(2)}, u32[]{:S(2)}) collective-permute-start(bf16[48,4608]{1,0:T(8,128)(2,1)} %get-tuple-element.396), channel_id=1, source_target_pairs={{0,2},{1,3},{2,0},{3,1},{4,6},{5,7},{6,4},{7,5},{8,10},{9,11},{10,... | collective-permute-start | bytes 1327112 | tf_op jit(solution)/shard_map/ppermute | solution.py:64
  493.2 19.9 %shard_map.544 = (f32[192,6288]{1,0:T(8,128)}, f32[1,128]{1,0:T(1,128)}) custom-call(s32[4]{0:T(128)} %pad_add_fusion.spot_ref, s32[32]{0:T(128)} %copy-done.104, s32[32]{0:T(128)} %max.68.last_ref, s32[32,224]{1,0:T(8,128)} %fusion.30.ids_ref, bf16[16,120,384]{2,1,0:T(8,128)(2,1)} %copy-done.57, bf16[16,120,384]{2,1,0:T(8,128)(2,1)} %collective-permute-done.64.theirs_ref), custom_call_target="tpu_custom_call" | custom-call | bytes 52428800 | tf_op jit(solution)/shard_map/pallas_call | solution.py:431
  525.0 7.5 %collective-permute-start.70 = (f32[8,128]{1,0:T(8,128)S(1)}, f32[8,128]{1,0:T(8,128)S(1)}, u32[]{:S(2)}, u32[]{:S(2)}) collective-permute-start(f32[8,128]{1,0:T(8,128)S(1)} %broadcast_in_dim.90), channel_id=1, source_target_pairs={{0,2},{1,3},{2,0},{3,1},{4,6},{5,7},{6,4},{7,5},{8,10},{9,11},{10,... | collective-permute-start | bytes 12296 | tf_op jit(solution)/shard_map/ppermute | solution.py:64
  541.9 5.9 collective-permute-done.74
  552.5 12.3 %fusion.1 = (f32[6288,192]{0,1:T(8,128)}, f32[192,6288]{1,0:T(8,128)}, f32[6288,192]{0,1:T(8,128)}) fusion(f32[6288,192]{0,1:T(8,128)} %param.53, f32[6288,192]{0,1:T(8,128)} %param.44, f32[]{:T(128)S(6)} %min.28, f32[192,6288]{1,0:T(8,128)} %get-tuple-element.311, f32[192]{0:T(256)S(1)} %bitcast.574, pred[6288]{0:T(1024)(128)(4,1)S(1)} %iota_compare_fusion, ...), kind=kLoop, calls=%fused_computation.5 | loop fusion | flops 13280256 | bytes 33811348 | tf_op jit(solution)/shard_map/transpose | solution.py:1547
  573.1 9.8 %add_multiply_fusion = (f32[192,6288]{1,0:T(8,128)}, f32[192,6288]{1,0:T(8,128)}, f32[192,6288]{1,0:T(8,128)}) fusion(f32[192,6288]{1,0:T(8,128)} %param.54, f32[192,6288]{1,0:T(8,128)} %in_ref.1, f32[]{:T(128)S(6)} %min.28, bf16[192,1664]{1,0:T(8,128)(2,1)S(1)} %get-tuple-element.369, bf16[192,1664]{1,0:T(8,128)(2,1)S(1)} %get-tuple-element.368, ...), kind=kLoop, calls=%fused_computation.7 | loop fusion | flops 20524032 | bytes 31531012 | tf_op jit(solution)/shard_map/add | solution.py:1190
  (578 shorter events, 263.1 us)
Async XLA Ops:
  7.2 129.1 %all-gather.3.cloned.1.call-start = ((), (), s32[]{:S(2)}) async-start(), calls=%async_computation.1 | async-start | bytes 3932160 | tf_op jit(solution)/shard_map/all_gather | solution.py:134
  13.9 24.6 %collective-permute-start.1 = (f32[16,256]{1,0:T(8,128)}, f32[16,256]{1,0:T(8,128)S(1)}, u32[]{:S(2)}, u32[]{:S(2)}) collective-permute-start(f32[16,256]{1,0:T(8,128)} %get-tuple-element.184), channel_id=1, source_target_pairs={{0,4},{1,5},{2,6},{3,7},{4,0},{5,1},{6,2},{7,3},{8,12},{9,13},{10,... | collective-permute-start | bytes 49160 | tf_op jit(solution)/shard_map/ppermute | solution.py:64
  22.2 17.5 %collective-permute-start.5 = (bf16[48,2048]{1,0:T(8,128)(2,1)S(1)}, bf16[48,2048]{1,0:T(8,128)(2,1)S(1)}, u32[]{:S(2)}, u32[]{:S(2)}) collective-permute-start(bf16[48,2048]{1,0:T(8,128)(2,1)S(1)} %slice.399), channel_id=1, source_target_pairs={{0,4},{1,5},{2,6},{3,7},{4,0},{5,1},{6,2},{7,3},{8,12},{9,13},{10,... | collective-permute-start | bytes 589832 | tf_op jit(solution)/shard_map/ppermute | solution.py:64
  22.2 17.5 %collective-permute-start.6 = (bf16[48,2048]{1,0:T(8,128)(2,1)S(1)}, bf16[48,2048]{1,0:T(8,128)(2,1)S(1)}, u32[]{:S(2)}, u32[]{:S(2)}) collective-permute-start(bf16[48,2048]{1,0:T(8,128)(2,1)S(1)} %slice.399), channel_id=1, source_target_pairs={{0,6},{1,7},{2,4},{3,5},{4,2},{5,3},{6,0},{7,1},{8,14},{9,15},{10,... | collective-permute-start | bytes 589832 | tf_op jit(solution)/shard_map/ppermute | solution.py:64
  48.6 30.4 %collective-permute-start.13 = (bf16[2,192,1664]{2,1,0:T(8,128)(2,1)S(1)}, bf16[2,192,1664]{2,1,0:T(8,128)(2,1)}, u32[]{:S(2)}, u32[]{:S(2)}) collective-permute-start(bf16[2,192,1664]{2,1,0:T(8,128)(2,1)S(1)} %get-tuple-element.376), channel_id=1, source_target_pairs={{0,8},{1,9},{2,10},{3,11},{4,12},{5,13},{6,14},{7,15},{8,0},{9,1},... | collective-permute-start | bytes 3833864 | tf_op jit(solution)/shard_map/ppermute | solution.py:64
  50.9 23.6 %collective-permute-start.10 = (bf16[48,3072]{1,0:T(8,128)(2,1)S(1)}, bf16[48,3072]{1,0:T(8,128)(2,1)S(1)}, u32[]{:S(2)}, u32[]{:S(2)}) collective-permute-start(bf16[48,3072]{1,0:T(8,128)(2,1)S(1)} %slice.401), channel_id=1, source_target_pairs={{0,2},{1,3},{2,0},{3,1},{4,6},{5,7},{6,4},{7,5},{8,10},{9,11},{10,... | collective-permute-start | bytes 884744 | tf_op jit(solution)/shard_map/ppermute | solution.py:64
  55.4 23.5 %collective-permute-start.11 = (bf16[48,3072]{1,0:T(8,128)(2,1)S(1)}, bf16[48,3072]{1,0:T(8,128)(2,1)}, u32[]{:S(2)}, u32[]{:S(2)}) collective-permute-start(bf16[48,3072]{1,0:T(8,128)(2,1)S(1)} %slice.401), channel_id=1, source_target_pairs={{0,4},{1,5},{2,6},{3,7},{4,0},{5,1},{6,2},{7,3},{8,12},{9,13},{10,... | collective-permute-start | bytes 884744 | tf_op jit(solution)/shard_map/ppermute | solution.py:64
  55.4 23.5 %collective-permute-start.12 = (bf16[48,3072]{1,0:T(8,128)(2,1)S(1)}, bf16[48,3072]{1,0:T(8,128)(2,1)}, u32[]{:S(2)}, u32[]{:S(2)}) collective-permute-start(bf16[48,3072]{1,0:T(8,128)(2,1)S(1)} %slice.401), channel_id=1, source_target_pairs={{0,6},{1,7},{2,4},{3,5},{4,2},{5,3},{6,0},{7,1},{8,14},{9,15},{10,... | collective-permute-start | bytes 884744 | tf_op jit(solution)/shard_map/ppermute | solution.py:64
  80.5 20.9 %collective-permute-start.18 = (bf16[4,48,1536]{2,1,0:T(8,128)(2,1)S(1)}, bf16[4,48,1536]{2,1,0:T(8,128)(2,1)}, u32[]{:S(2)}, u32[]{:S(2)}) collective-permute-start(bf16[4,48,1536]{2,1,0:T(8,128)(2,1)S(1)} %get-tuple-element.214), channel_id=1, source_target_pairs={{0,8},{1,9},{2,10},{3,11},{4,12},{5,13},{6,14},{7,15},{8,0},{9,1},... | collective-permute-start | bytes 1769480 | tf_op jit(solution)/shard_map/ppermute | solution.py:64
  81.1 20.3 %collective-permute-start.19 = (bf16[4,48,1536]{2,1,0:T(8,128)(2,1)S(1)}, bf16[4,48,1536]{2,1,0:T(8,128)(2,1)}, u32[]{:S(2)}, u32[]{:S(2)}) collective-permute-start(bf16[4,48,1536]{2,1,0:T(8,128)(2,1)S(1)} %get-tuple-element.216), channel_id=1, source_target_pairs={{0,16},{1,17},{2,18},{3,19},{4,20},{5,21},{6,22},{7,23},{8,24},{9,... | collective-permute-start | bytes 1769480 | tf_op jit(solution)/shard_map/ppermute | solution.py:64
  83.6 395.9 %reduce-scatter.4.cloned.1.call-start = ((), (), s32[]{:S(2)}) async-start(), calls=%async_computation.2 | async-start | bytes 5898240
  86.6 20.6 %collective-permute-start.15 = (bf16[4,112,384]{2,1,0:T(8,128)(2,1)}, bf16[4,112,384]{2,1,0:T(8,128)(2,1)S(1)}, u32[]{:S(2)}, u32[]{:S(2)}) collective-permute-start(bf16[4,112,384]{2,1,0:T(8,128)(2,1)} %get-tuple-element.400), channel_id=1, source_target_pairs={{0,2},{1,3},{2,0},{3,1},{4,6},{5,7},{6,4},{7,5},{8,10},{9,11},{10,... | collective-permute-start | bytes 1032200 | tf_op jit(solution)/shard_map/ppermute | solution.py:64
  92.8 26.8 %collective-permute-start.16 = (bf16[4,112,384]{2,1,0:T(8,128)(2,1)}, bf16[4,112,384]{2,1,0:T(8,128)(2,1)S(1)}, u32[]{:S(2)}, u32[]{:S(2)}) collective-permute-start(bf16[4,112,384]{2,1,0:T(8,128)(2,1)} %get-tuple-element.399), channel_id=1, source_target_pairs={{0,4},{1,5},{2,6},{3,7},{4,0},{5,1},{6,2},{7,3},{8,12},{9,13},{10,... | collective-permute-start | bytes 1032200 | tf_op jit(solution)/shard_map/ppermute | solution.py:64
  92.8 26.8 %collective-permute-start.17 = (bf16[4,112,384]{2,1,0:T(8,128)(2,1)}, bf16[4,112,384]{2,1,0:T(8,128)(2,1)S(1)}, u32[]{:S(2)}, u32[]{:S(2)}) collective-permute-start(bf16[4,112,384]{2,1,0:T(8,128)(2,1)} %get-tuple-element.398), channel_id=1, source_target_pairs={{0,6},{1,7},{2,4},{3,5},{4,2},{5,3},{6,0},{7,1},{8,14},{9,15},{10,... | collective-permute-start | bytes 1032200 | tf_op jit(solution)/shard_map/ppermute | solution.py:64
  136.3 28.7 %collective-permute-start.24 = (bf16[2,4,48,1536]{3,2,1,0:T(8,128)(2,1)}, bf16[2,4,48,1536]{3,2,1,0:T(8,128)(2,1)}, u32[]{:S(2)}, u32[]{:S(2)}) collective-permute-start(bf16[2,4,48,1536]{3,2,1,0:T(8,128)(2,1)} %pad_maximum_fusion.13), channel_id=1, source_target_pairs={{0,16},{1,17},{2,18},{3,19},{4,20},{5,21},{6,22},{7,23},{8,24},{9,... | collective-permute-start | bytes 3538952 | tf_op jit(solution)/shard_map/ppermute | solution.py:64
  137.8 28.4 %collective-permute-start.25 = (bf16[2,4,48,1536]{3,2,1,0:T(8,128)(2,1)}, bf16[2,4,48,1536]{3,2,1,0:T(8,128)(2,1)}, u32[]{:S(2)}, u32[]{:S(2)}) collective-permute-start(bf16[2,4,48,1536]{3,2,1,0:T(8,128)(2,1)} %pad_maximum_fusion.14), channel_id=1, source_target_pairs={{0,8},{1,9},{2,10},{3,11},{4,12},{5,13},{6,14},{7,15},{8,0},{9,1},... | collective-permute-start | bytes 3538952 | tf_op jit(solution)/shard_map/ppermute | solution.py:64
  193.6 31.0 %collective-permute-start.33 = (bf16[2,192,1664]{2,1,0:T(8,128)(2,1)S(1)}, bf16[2,192,1664]{2,1,0:T(8,128)(2,1)S(1)}, u32[]{:S(2)}, u32[]{:S(2)}) collective-permute-start(bf16[2,192,1664]{2,1,0:T(8,128)(2,1)S(1)} %pad_maximum_fusion.10), channel_id=1, source_target_pairs={{0,16},{1,17},{2,18},{3,19},{4,20},{5,21},{6,22},{7,23},{8,24},{9,... | collective-permute-start | bytes 3833864 | tf_op jit(solution)/shard_map/ppermute | solution.py:64
  211.5 18.1 %collective-permute-start.32 = (bf16[4,96,384]{2,1,0:T(8,128)(2,1)S(1)}, bf16[4,96,384]{2,1,0:T(8,128)(2,1)S(1)}, u32[]{:S(2)}, u32[]{:S(2)}) collective-permute-start(bf16[4,96,384]{2,1,0:T(8,128)(2,1)S(1)} %get-tuple-element.247), channel_id=1, source_target_pairs={{0,16},{1,17},{2,18},{3,19},{4,20},{5,21},{6,22},{7,23},{8,24},{9,... | collective-permute-start | bytes 884744 | tf_op jit(solution)/shard_map/ppermute | solution.py:64
  315.2 18.6 %collective-permute-start.46 = (bf16[2,4,96,384]{3,2,1,0:T(8,128)(2,1)S(1)}, bf16[2,4,96,384]{3,2,1,0:T(8,128)(2,1)S(1)}, u32[]{:S(2)}, u32[]{:S(2)}) collective-permute-start(bf16[2,4,96,384]{3,2,1,0:T(8,128)(2,1)S(1)} %get-tuple-element.412), channel_id=1, source_target_pairs={{0,8},{1,9},{2,10},{3,11},{4,12},{5,13},{6,14},{7,15},{8,0},{9,1},... | collective-permute-start | bytes 1769480 | tf_op jit(solution)/shard_map/ppermute | solution.py:64
  345.8 28.7 %collective-permute-start.52 = (bf16[2,192,1664]{2,1,0:T(8,128)(2,1)}, bf16[2,192,1664]{2,1,0:T(8,128)(2,1)}, u32[]{:S(2)}, u32[]{:S(2)}) collective-permute-start(bf16[2,192,1664]{2,1,0:T(8,128)(2,1)} %get-tuple-element.370), channel_id=1, source_target_pairs={{0,8},{1,9},{2,10},{3,11},{4,12},{5,13},{6,14},{7,15},{8,0},{9,1},... | collective-permute-start | bytes 3833864 | tf_op jit(solution)/shard_map/ppermute | solution.py:64
  413.4 20.5 %collective-permute-start.58 = (bf16[768,1536]{1,0:T(8,128)(2,1)}, bf16[768,1536]{1,0:T(8,128)(2,1)}, u32[]{:S(2)}, u32[]{:S(2)}) collective-permute-start(bf16[768,1536]{1,0:T(8,128)(2,1)} %pad_maximum_fusion.8), channel_id=1, source_target_pairs={{0,1},{1,0},{2,3},{3,2},{4,5},{5,4},{6,7},{7,6},{8,9},{9,8},{10,11... | collective-permute-start | bytes 7077896 | tf_op jit(solution)/shard_map/ppermute | solution.py:64
  436.3 32.6 %collective-permute-start.63 = (bf16[2,4,48,768]{3,2,1,0:T(8,128)(2,1)S(1)}, bf16[2,4,48,768]{3,2,1,0:T(8,128)(2,1)S(1)}, u32[]{:S(2)}, u32[]{:S(2)}) collective-permute-start(bf16[2,4,48,768]{3,2,1,0:T(8,128)(2,1)S(1)} %get-tuple-element.408), channel_id=1, source_target_pairs={{0,8},{1,9},{2,10},{3,11},{4,12},{5,13},{6,14},{7,15},{8,0},{9,1},... | collective-permute-start | bytes 1769480 | tf_op jit(solution)/shard_map/ppermute | solution.py:64
  437.3 31.7 %collective-permute-start.62 = (bf16[2,4,48,768]{3,2,1,0:T(8,128)(2,1)S(1)}, bf16[2,4,48,768]{3,2,1,0:T(8,128)(2,1)S(1)}, u32[]{:S(2)}, u32[]{:S(2)}) collective-permute-start(bf16[2,4,48,768]{3,2,1,0:T(8,128)(2,1)S(1)} %get-tuple-element.410), channel_id=1, source_target_pairs={{0,16},{1,17},{2,18},{3,19},{4,20},{5,21},{6,22},{7,23},{8,24},{9,... | collective-permute-start | bytes 1769480 | tf_op jit(solution)/shard_map/ppermute | solution.py:64
  440.7 28.2 %collective-permute-start.60 = (bf16[4,120,384]{2,1,0:T(8,128)(2,1)S(1)}, bf16[4,120,384]{2,1,0:T(8,128)(2,1)S(1)}, u32[]{:S(2)}, u32[]{:S(2)}) collective-permute-start(bf16[4,120,384]{2,1,0:T(8,128)(2,1)S(1)} %pad_maximum_fusion.24), channel_id=1, source_target_pairs={{0,4},{1,5},{2,6},{3,7},{4,0},{5,1},{6,2},{7,3},{8,12},{9,13},{10,... | collective-permute-start | bytes 1105928 | tf_op jit(solution)/shard_map/ppermute | solution.py:64
  440.7 28.2 %collective-permute-start.61 = (bf16[4,120,384]{2,1,0:T(8,128)(2,1)S(1)}, bf16[4,120,384]{2,1,0:T(8,128)(2,1)S(1)}, u32[]{:S(2)}, u32[]{:S(2)}) collective-permute-start(bf16[4,120,384]{2,1,0:T(8,128)(2,1)S(1)} %pad_maximum_fusion.24), channel_id=1, source_target_pairs={{0,6},{1,7},{2,4},{3,5},{4,2},{5,3},{6,0},{7,1},{8,14},{9,15},{10,... | collective-permute-start | bytes 1105928 | tf_op jit(solution)/shard_map/ppermute | solution.py:64
  482.1 39.9 %collective-permute-start.67 = (bf16[48,4608]{1,0:T(8,128)(2,1)}, bf16[48,4608]{1,0:T(8,128)(2,1)}, u32[]{:S(2)}, u32[]{:S(2)}) collective-permute-start(bf16[48,4608]{1,0:T(8,128)(2,1)} %get-tuple-element.396), channel_id=1, source_target_pairs={{0,2},{1,3},{2,0},{3,1},{4,6},{5,7},{6,4},{7,5},{8,10},{9,11},{10,... | collective-permute-start | bytes 1327112 | tf_op jit(solution)/shard_map/ppermute | solution.py:64
  488.1 34.0 %collective-permute-start.68 = (bf16[48,4608]{1,0:T(8,128)(2,1)}, bf16[48,4608]{1,0:T(8,128)(2,1)}, u32[]{:S(2)}, u32[]{:S(2)}) collective-permute-start(bf16[48,4608]{1,0:T(8,128)(2,1)} %get-tuple-element.395), channel_id=1, source_target_pairs={{0,4},{1,5},{2,6},{3,7},{4,0},{5,1},{6,2},{7,3},{8,12},{9,13},{10,... | collective-permute-start | bytes 1327112 | tf_op jit(solution)/shard_map/ppermute | solution.py:64
  488.3 33.8 %collective-permute-start.69 = (bf16[48,4608]{1,0:T(8,128)(2,1)}, bf16[48,4608]{1,0:T(8,128)(2,1)}, u32[]{:S(2)}, u32[]{:S(2)}) collective-permute-start(bf16[48,4608]{1,0:T(8,128)(2,1)} %get-tuple-element.394), channel_id=1, source_target_pairs={{0,6},{1,7},{2,4},{3,5},{4,2},{5,3},{6,0},{7,1},{8,14},{9,15},{10,... | collective-permute-start | bytes 1327112 | tf_op jit(solution)/shard_map/ppermute | solution.py:64
  517.6 53.7 %collective-permute-start.77 = (bf16[2,192,1664]{2,1,0:T(8,128)(2,1)}, bf16[2,192,1664]{2,1,0:T(8,128)(2,1)}, u32[]{:S(2)}, u32[]{:S(2)}) collective-permute-start(bf16[2,192,1664]{2,1,0:T(8,128)(2,1)} %pad_maximum_fusion.11), channel_id=1, source_target_pairs={{0,16},{1,17},{2,18},{3,19},{4,20},{5,21},{6,22},{7,23},{8,24},{9,... | collective-permute-start | bytes 3833864 | tf_op jit(solution)/shard_map/ppermute | solution.py:64
  535.1 30.5 %collective-permute-start.80 = (f32[96,384]{1,0:T(8,128)S(1)}, f32[96,384]{1,0:T(8,128)}, u32[]{:S(2)}, u32[]{:S(2)}) collective-permute-start(f32[96,384]{1,0:T(8,128)S(1)} %dynamic-slice_bitcast_fusion.18), channel_id=1, source_target_pairs={{0,1},{1,0},{2,3},{3,2},{4,5},{5,4},{6,7},{7,6},{8,9},{9,8},{10,11... | collective-permute-start | bytes 442376 | tf_op jit(solution)/shard_map/ppermute | solution.py:64
  541.8 26.5 %collective-permute-start.79 = (f32[24,1536]{1,0:T(8,128)S(1)}, f32[24,1536]{1,0:T(8,128)}, u32[]{:S(2)}, u32[]{:S(2)}) collective-permute-start(f32[24,1536]{1,0:T(8,128)S(1)} %dynamic-slice_bitcast_fusion.19), channel_id=1, source_target_pairs={{0,1},{1,0},{2,3},{3,2},{4,5},{5,4},{6,7},{7,6},{8,9},{9,8},{10,11... | collective-permute-start | bytes 442376 | tf_op jit(solution)/shard_map/ppermute | solution.py:64
  547.8 17.7 %collective-permute-start.78 = (f32[24,1536]{1,0:T(8,128)S(1)}, f32[24,1536]{1,0:T(8,128)S(1)}, u32[]{:S(2)}, u32[]{:S(2)}) collective-permute-start(f32[24,1536]{1,0:T(8,128)S(1)} %dynamic-slice_bitcast_fusion.20), channel_id=1, source_target_pairs={{0,1},{1,0},{2,3},{3,2},{4,5},{5,4},{6,7},{7,6},{8,9},{9,8},{10,11... | collective-permute-start | bytes 442376 | tf_op jit(solution)/shard_map/ppermute | solution.py:64
  (161 other events, 1409.1 us)
Sparse Core Ops, SparseCore 0:
  83.7 52.5 all-gather.2
  401.1 64.4 reduce-scatter.3
